TPU v7x, 32 devices: a whole 2x2x4 slice. The times are simulated.
32 devices in a mesh: dp: 8 (over z, x), mp: 4 (over y, core).
Axes of the slice: x: 2, y: 2, z: 4, core: 2. Of those that a mesh axis runs over, the one named last changes fastest.
Arguments:
- inputs: bfloat16 [8192, 768], P(('dp', 'mp')), may hold values from -6 to 6
- query_key_value: bfloat16 [768, 3, 768], P('dp', None, 'mp'), may hold values from -0.21875 to 0.21875
- output_weight: bfloat16 [768, 768], P('mp', 'dp'), may hold values from -3.5 to 3.5
- expert_input: bfloat16 [8, 2, 768, 2048], P(None, None, 'dp', 'mp'), may hold values from -0.21875 to 0.21875
- expert_output: bfloat16 [8, 2048, 768], P(None, 'mp', 'dp'), may hold values from -0.25 to 0.25
- first_gain: bfloat16 [768], replicated, may hold values from 0.5 to 1.5
- second_gain: bfloat16 [768], replicated, may hold values from 0.5 to 1.5
- router_weight: bfloat16 [768, 12], replicated, may hold values from -0.21875 to 0.21875
- logit_carry: float32 [12, 12], replicated, may hold values from -1.75 to 1.75
- constant_mix: bfloat16 [768, 4], replicated, may hold values from -0.21875 to 0.21875
- constant_values: bfloat16 [2, 768], replicated, may hold values from -6 to 6
- previous_logits: float32 [8192, 12], P('dp'), may hold values from -6 to 6
- routes: int32 [8192, 2], P('dp'), may hold values from 0 to 11, all different within a row; in each aligned block of 1024 rows (0 to 1023, 1024 to 2047, ...) at most 256 rows name the same one
- cotangent: bfloat16 [8192, 768], P(('dp', 'mp')), may hold values from -6 to 6
Outputs:
- output: bfloat16 [8192, 768], P(('dp', 'mp'))
- input_grad: float32 [8192, 768], P(('dp', 'mp'))
- logits_grad: float32 [8192, 12], P(('dp', 'mp'))
- query_key_value_grad: float32 [768, 3, 768], P('dp', None, 'mp')
- output_weight_grad: float32 [768, 768], P('mp', 'dp')
- expert_input_grad: float32 [8, 2, 768, 2048], P(None, None, 'dp', 'mp')
- expert_output_grad: float32 [8, 2048, 768], P(None, 'mp', 'dp')
- first_gain_grad: float32 [768], replicated
- second_gain_grad: float32 [768], replicated
- router_grad: float32 [768, 12], replicated
- logit_carry_grad: float32 [12, 12], replicated
- constant_mix_grad: float32 [768, 4], replicated
- constant_values_grad: float32 [2, 768], replicated
Inputs may be any that keep to these rules, and one draw needn't show every extreme that they name: `routes`: each row names two different experts. Among the tokens of one index of dp no expert is named by more than 256 rows, a bound that some block reaches.
All inputs are finite; a program needn't handle non-finite values.
Results may differ from a plain program's by a relative error of at most 0.015.
Values may be sent and summed in bfloat16 or wider, within the bound.
A program may use at most 256 MiB of HBM per device.

v0:
```python
import jax
import jax.numpy as jnp
from jax import lax
from jax.sharding import PartitionSpec as P

HD = 64
NFFN = 8
NEXP = 12
SEQ = 1024
CAP = 256


epsilon = 1e-06
rope_base = 10000.0
highest = lax.Precision.HIGHEST


def rope_tables(length, period, half):
    positions = (jnp.arange(length, dtype=jnp.int32) % period).astype(jnp.float32)
    frequency = rope_base ** (-jnp.arange(half, dtype=jnp.float32) / half)
    angles = positions[:, None] * frequency[None, :]
    return (jnp.cos(angles), jnp.sin(angles))


def rotate(values, cosine, sine_table):
    half = values.shape[-1] // 2
    front_half = values[..., :half]
    back_half = values[..., half:]
    cosine = cosine[:, None, :]
    sine_table = sine_table[:, None, :]
    return jnp.concatenate(
        [
            front_half * cosine - back_half * sine_table,
            back_half * cosine + front_half * sine_table,
        ],
        axis=-1,
    )


def rotate_back(grads, cosine, sine_table):
    half = grads.shape[-1] // 2
    front_half = grads[..., :half]
    back_half = grads[..., half:]
    cosine = cosine[:, None, :]
    sine_table = sine_table[:, None, :]
    return jnp.concatenate(
        [
            front_half * cosine + back_half * sine_table,
            back_half * cosine - front_half * sine_table,
        ],
        axis=-1,
    )


def dispatch_tables(route_rows, experts, capacity):
    row_count = route_rows.shape[0]
    flat_routes = route_rows.reshape(-1)
    onehot = (flat_routes[:, None] == jnp.arange(experts, dtype=jnp.int32)[None, :]).astype(
        jnp.int32
    )
    before = jnp.cumsum(onehot, axis=0) - onehot
    position = jnp.sum(before * onehot, axis=1)
    target = jnp.where(flat_routes < experts, flat_routes * capacity + position, experts * capacity)
    assigned = (
        jnp.full((experts * capacity + 1,), 2 * row_count, jnp.int32)
        .at[target]
        .set(jnp.arange(2 * row_count, dtype=jnp.int32))[:-1]
    )
    tokens_of = jnp.minimum(assigned // 2, row_count - 1)
    return (assigned, tokens_of)


def norm_back(values, norm_scale, gain, grads):
    scaled = values * norm_scale
    gain_grad = jnp.sum(grads * scaled, axis=0)
    weighted_grad = grads * gain
    values_grad = norm_scale * (
        weighted_grad - scaled * jnp.mean(weighted_grad * scaled, axis=-1, keepdims=True)
    )
    return (gain_grad, values_grad)


def local_values(chosen_expert, normed_rows, constant_rows):
    expert_value = jnp.where(chosen_expert == NFFN + 1, normed_rows, 0.0)
    return (
        expert_value
        + jnp.where(chosen_expert == NFFN + 2, constant_rows[0], 0.0)
        + jnp.where(chosen_expert == NFFN + 3, constant_rows[1], 0.0)
    )


def per_device(
    inputs,
    query_key_value,
    output_weight,
    expert_input,
    expert_output,
    first_gain,
    second_gain,
    router_weight,
    logit_carry,
    constant_mix,
    constant_values,
    previous_logits,
    routes,
    cotangent,
):
    shard_rows = inputs.shape[0]
    model_width = inputs.shape[1]
    group_rows = shard_rows * lax.axis_size("mp")
    offset = lax.axis_index("mp") * shard_rows
    heads_here = query_key_value.shape[2] // HD
    score_scale = HD ** (-0.5)
    block_rows = min(512, SEQ)
    blocks_per_seq = SEQ // block_rows
    block_count = group_rows // block_rows
    sequences = group_rows // SEQ
    gain_one = first_gain.astype(jnp.float32)
    gain_two = second_gain.astype(jnp.float32)
    tokens = inputs.astype(jnp.float32)
    scale_one = lax.rsqrt(jnp.mean(tokens * tokens, axis=-1, keepdims=True) + epsilon)
    normed_one = (tokens * scale_one * gain_one).astype(jnp.bfloat16)
    rows_one = lax.all_gather(normed_one, "mp", axis=0, tiled=True)
    attention_in, attention_out = (
        lax.all_gather(query_key_value, "dp", axis=0, tiled=True),
        lax.all_gather(output_weight, "dp", axis=1, tiled=True),
    )
    joint_proj = jnp.einsum(
        "td,dkf->tkf", rows_one, attention_in, preferred_element_type=jnp.float32
    )
    cosine, sine_table = rope_tables(group_rows, SEQ, HD // 2)
    queries = rotate(
        joint_proj[:, 0].reshape(group_rows, heads_here, HD), cosine, sine_table
    ).astype(jnp.bfloat16)
    keys_turned = rotate(
        joint_proj[:, 1].reshape(group_rows, heads_here, HD), cosine, sine_table
    ).astype(jnp.bfloat16)
    values_heads = joint_proj[:, 2].reshape(group_rows, heads_here, HD).astype(jnp.bfloat16)
    query_blocks = queries.reshape(block_count, block_rows, heads_here, HD)
    key_seqs = keys_turned.reshape(sequences, SEQ, heads_here, HD)
    value_seqs = values_heads.reshape(sequences, SEQ, heads_here, HD)
    key_positions = jnp.arange(SEQ, dtype=jnp.int32)

    def block_scores(block_index):
        seq_index = block_index // blocks_per_seq
        query_rows = query_blocks[block_index]
        key_rows = key_seqs[seq_index]
        raw_scores = (
            jnp.einsum("qhd,khd->hqk", query_rows, key_rows, preferred_element_type=jnp.float32)
            * score_scale
        )
        query_positions = block_index % blocks_per_seq * block_rows + jnp.arange(
            block_rows, dtype=jnp.int32
        )
        causal = query_positions[:, None] >= key_positions[None, :]
        return (
            jnp.where(causal[None], raw_scores, -jnp.inf),
            query_rows,
            key_rows,
            value_seqs[seq_index],
        )

    def attend_block(block_index):
        scores, query_rows, key_rows, value_rows = block_scores(block_index)
        row_peak = jnp.max(scores, axis=-1, keepdims=True)
        exponent = jnp.exp(scores - row_peak)
        row_total = jnp.sum(exponent, axis=-1, keepdims=True)
        attention_weights = (exponent / row_total).astype(jnp.bfloat16)
        mixed_rows = jnp.einsum(
            "hqk,khd->qhd", attention_weights, value_rows, preferred_element_type=jnp.float32
        )
        return (mixed_rows, (row_peak + jnp.log(row_total))[..., 0])

    mixed_blocks, log_totals = lax.map(attend_block, jnp.arange(block_count, dtype=jnp.int32))
    mixed = mixed_blocks.reshape(group_rows, heads_here * HD).astype(jnp.bfloat16)
    attention_part = jnp.dot(mixed, attention_out, preferred_element_type=jnp.float32)
    attended = lax.psum_scatter(attention_part, "mp", scatter_dimension=0, tiled=True)
    hidden = tokens + attended
    scale_two = lax.rsqrt(jnp.mean(hidden * hidden, axis=-1, keepdims=True) + epsilon)
    normed_two = (hidden * scale_two * gain_two).astype(jnp.bfloat16)
    rows_two = lax.all_gather(normed_two, "mp", axis=0, tiled=True)
    logits = jnp.dot(rows_two, router_weight, preferred_element_type=jnp.float32) + jnp.dot(
        previous_logits, logit_carry, precision=highest
    )
    chosen = jnp.take_along_axis(logits, routes, axis=1)
    gates = jax.nn.softmax(chosen, axis=-1)
    assigned, tokens_of = dispatch_tables(routes, NFFN, CAP)
    gate_table = jnp.concatenate([gates.reshape(-1), jnp.zeros((1,), jnp.float32)])[
        assigned
    ].reshape(NFFN, CAP)
    expert_in_rows, expert_out_rows = (
        lax.all_gather(expert_input, "dp", axis=2, tiled=True),
        lax.all_gather(expert_output, "dp", axis=2, tiled=True),
    )
    rows_in = rows_two[tokens_of].reshape(NFFN, CAP, model_width)
    gate_up = jnp.einsum(
        "ecd,ekdf->ekcf", rows_in, expert_in_rows, preferred_element_type=jnp.float32
    )
    gate_pre = gate_up[:, 0]
    up_pre = gate_up[:, 1]
    hidden_units = (jax.nn.silu(gate_pre) * up_pre).astype(jnp.bfloat16)
    expert_rows = jnp.einsum(
        "ecf,efd->ecd", hidden_units, expert_out_rows, preferred_element_type=jnp.float32
    )
    weighted = (expert_rows * gate_table[:, :, None]).reshape(NFFN * CAP, model_width)
    routed = jnp.zeros((group_rows, model_width), jnp.float32).at[tokens_of].add(weighted)
    routed_own = lax.psum_scatter(
        routed.astype(jnp.bfloat16), "mp", scatter_dimension=0, tiled=True
    ).astype(jnp.float32)
    routes_own = lax.dynamic_slice_in_dim(routes, offset, shard_rows, 0)
    gates_own = lax.dynamic_slice_in_dim(gates, offset, shard_rows, 0)
    previous_own = lax.dynamic_slice_in_dim(previous_logits, offset, shard_rows, 0)
    normed_float = normed_two.astype(jnp.float32)
    mixing = constant_mix.astype(jnp.float32)
    constants = constant_values.astype(jnp.float32)
    mix_logits = jnp.dot(normed_two, constant_mix, preferred_element_type=jnp.float32).reshape(
        shard_rows, 2, 2
    )
    alphas = jax.nn.softmax(mix_logits, axis=-1)
    constant_rows = [
        alphas[:, 0, 0:1] * normed_float + alphas[:, 0, 1:2] * constants[0][None, :],
        alphas[:, 1, 0:1] * normed_float + alphas[:, 1, 1:2] * constants[1][None, :],
    ]
    first_value = local_values(routes_own[:, 0:1], normed_float, constant_rows)
    second_value = local_values(routes_own[:, 1:2], normed_float, constant_rows)
    local_rows = gates_own[:, 0:1] * first_value + gates_own[:, 1:2] * second_value
    output = (hidden + (routed_own + local_rows)).astype(jnp.bfloat16)
    grad_out = cotangent.astype(jnp.float32)
    grad_rows_all = lax.all_gather(cotangent, "mp", axis=0, tiled=True)
    slot_grads = grad_rows_all[tokens_of].reshape(NFFN, CAP, model_width).astype(jnp.float32)
    expert_grad = (slot_grads * gate_table[:, :, None]).astype(jnp.bfloat16)
    gate_slot = jnp.sum(slot_grads * expert_rows, axis=-1)
    output_side_grad = jnp.einsum(
        "ecf,ecd->efd", hidden_units, expert_grad, preferred_element_type=jnp.float32
    )
    units_grad = jnp.einsum(
        "ecd,efd->ecf", expert_grad, expert_out_rows, preferred_element_type=jnp.float32
    )
    sigmoid_gate = jax.nn.sigmoid(gate_pre)
    gate_pre_grad = units_grad * up_pre * sigmoid_gate * (1.0 + gate_pre * (1.0 - sigmoid_gate))
    up_pre_grad = units_grad * gate_pre * sigmoid_gate
    pre_grads = jnp.stack([gate_pre_grad, up_pre_grad], axis=1).astype(jnp.bfloat16)
    input_side_grad = jnp.einsum(
        "ecd,ekcf->ekdf", rows_in, pre_grads, preferred_element_type=jnp.float32
    )
    rows_grad = jnp.einsum(
        "ekcf,ekdf->ecd", pre_grads, expert_in_rows, preferred_element_type=jnp.float32
    )
    normed_part = (
        jnp.zeros((group_rows, model_width), jnp.float32)
        .at[tokens_of]
        .add(rows_grad.reshape(NFFN * CAP, model_width))
    )
    gate_part = (
        jnp.zeros((2 * group_rows + 1,), jnp.float32)
        .at[assigned]
        .add(gate_slot.reshape(-1))[:-1]
        .reshape(group_rows, 2)
    )
    normed_grad_moe, gate_grad_ffn = (
        lax.psum_scatter(normed_part, "mp", scatter_dimension=0, tiled=True),
        lax.psum_scatter(gate_part, "mp", scatter_dimension=0, tiled=True),
    )
    local_gate_grad = jnp.stack(
        [jnp.sum(grad_out * first_value, axis=-1), jnp.sum(grad_out * second_value, axis=-1)],
        axis=1,
    )
    gate_grad = gate_grad_ffn + local_gate_grad
    copy_weight = gates_own[:, 0:1] * (routes_own[:, 0:1] == NFFN + 1) + gates_own[:, 1:2] * (
        routes_own[:, 1:2] == NFFN + 1
    )
    normed_grad = normed_grad_moe + copy_weight * grad_out
    mix_grads = []
    values_grads = []
    for constant_index in range(2):
        expert_number = NFFN + 2 + constant_index
        route_weight = gates_own[:, 0:1] * (routes_own[:, 0:1] == expert_number) + gates_own[
            :, 1:2
        ] * (routes_own[:, 1:2] == expert_number)
        const_grad = route_weight * grad_out
        normed_grad = normed_grad + alphas[:, constant_index, 0:1] * const_grad
        alpha_grad = jnp.stack(
            [
                jnp.sum(const_grad * normed_float, axis=-1),
                jnp.sum(const_grad * constants[constant_index][None, :], axis=-1),
            ],
            axis=1,
        )
        values_grads.append(jnp.sum(alphas[:, constant_index, 1:2] * const_grad, axis=0))
        alpha_pair = alphas[:, constant_index]
        mix_grads.append(
            alpha_pair * (alpha_grad - jnp.sum(alpha_pair * alpha_grad, axis=-1, keepdims=True))
        )
    mix_grad = jnp.concatenate(mix_grads, axis=1)
    constant_mix_grad = jnp.einsum("td,tc->dc", normed_float, mix_grad, precision=highest)
    normed_grad = normed_grad + jnp.einsum("tc,dc->td", mix_grad, mixing, precision=highest)
    constant_values_grad = jnp.stack(values_grads, axis=0)
    chosen_grad = gates_own * (gate_grad - jnp.sum(gates_own * gate_grad, axis=-1, keepdims=True))
    expert_ids = jnp.arange(NEXP, dtype=jnp.int32)[None, :]
    logit_grad = chosen_grad[:, 0:1] * (routes_own[:, 0:1] == expert_ids) + chosen_grad[:, 1:2] * (
        routes_own[:, 1:2] == expert_ids
    )
    router_grad = jnp.einsum("td,te->de", normed_float, logit_grad, precision=highest)
    logit_carry_grad = jnp.einsum("tf,te->fe", previous_own, logit_grad, precision=highest)
    logits_grad = jnp.einsum("te,fe->tf", logit_grad, logit_carry, precision=highest)
    normed_grad = normed_grad + jnp.einsum(
        "te,de->td", logit_grad, router_weight.astype(jnp.float32), precision=highest
    )
    second_gain_grad, hidden_norm_grad = norm_back(hidden, scale_two, gain_two, normed_grad)
    hidden_grad = grad_out + hidden_norm_grad
    attended_grad = lax.all_gather(hidden_grad.astype(jnp.bfloat16), "mp", axis=0, tiled=True)
    output_weight_grad = jnp.einsum(
        "tf,td->fd", mixed, attended_grad, preferred_element_type=jnp.float32
    )
    mixed_grad = jnp.einsum(
        "td,fd->tf", attended_grad, attention_out, preferred_element_type=jnp.float32
    ).astype(jnp.bfloat16)
    mixed_grad_blocks = mixed_grad.reshape(block_count, block_rows, heads_here, HD)

    def attend_back(block_index):
        scores, query_rows, key_rows, value_rows = block_scores(block_index)
        out_grad_rows = mixed_grad_blocks[block_index]
        attention_weights = jnp.exp(scores - log_totals[block_index][:, :, None])
        weights_grad = jnp.einsum(
            "qhd,khd->hqk", out_grad_rows, value_rows, preferred_element_type=jnp.float32
        )
        inner_sum = jnp.sum(attention_weights * weights_grad, axis=-1, keepdims=True)
        score_grad = (attention_weights * (weights_grad - inner_sum)).astype(jnp.bfloat16)
        query_grad = (
            jnp.einsum("hqk,khd->qhd", score_grad, key_rows, preferred_element_type=jnp.float32)
            * score_scale
        )
        key_grad = (
            jnp.einsum("hqk,qhd->khd", score_grad, query_rows, preferred_element_type=jnp.float32)
            * score_scale
        )
        value_grad = jnp.einsum(
            "hqk,qhd->khd",
            attention_weights.astype(jnp.bfloat16),
            out_grad_rows,
            preferred_element_type=jnp.float32,
        )
        return (query_grad, key_grad, value_grad)

    query_grads, key_grads, value_grads = lax.map(
        attend_back, jnp.arange(block_count, dtype=jnp.int32)
    )
    query_grads = query_grads.reshape(group_rows, heads_here, HD)
    key_grads = (
        key_grads.reshape(sequences, blocks_per_seq, SEQ, heads_here, HD)
        .sum(axis=1)
        .reshape(group_rows, heads_here, HD)
    )
    value_grads = (
        value_grads.reshape(sequences, blocks_per_seq, SEQ, heads_here, HD)
        .sum(axis=1)
        .reshape(group_rows, heads_here, HD)
    )
    query_raw_grad = rotate_back(query_grads, cosine, sine_table).reshape(
        group_rows, heads_here * HD
    )
    key_raw_grad = rotate_back(key_grads, cosine, sine_table).reshape(group_rows, heads_here * HD)
    joint_grad = jnp.stack(
        [query_raw_grad, key_raw_grad, value_grads.reshape(group_rows, heads_here * HD)], axis=1
    ).astype(jnp.bfloat16)
    attention_in_grad = jnp.einsum(
        "td,tkf->dkf", rows_one, joint_grad, preferred_element_type=jnp.float32
    )
    normed_one_part = jnp.einsum(
        "tkf,dkf->td", joint_grad, attention_in, preferred_element_type=jnp.float32
    )
    normed_one_grad = lax.psum_scatter(
        normed_one_part.astype(jnp.bfloat16), "mp", scatter_dimension=0, tiled=True
    ).astype(jnp.float32)
    first_gain_grad, input_norm_grad = norm_back(tokens, scale_one, gain_one, normed_one_grad)
    input_grad = hidden_grad + input_norm_grad
    attention_in_own, attention_out_own = (
        lax.psum_scatter(attention_in_grad, "dp", scatter_dimension=0, tiled=True),
        lax.psum_scatter(output_weight_grad, "dp", scatter_dimension=1, tiled=True),
    )
    expert_in_grad = lax.psum_scatter(input_side_grad, "dp", scatter_dimension=2, tiled=True)
    expert_out_grad = lax.psum_scatter(output_side_grad, "dp", scatter_dimension=2, tiled=True)
    small_sums = lax.psum(
        (
            first_gain_grad,
            second_gain_grad,
            router_grad,
            logit_carry_grad,
            constant_mix_grad,
            constant_values_grad,
        ),
        ("dp", "mp"),
    )
    return (
        output,
        input_grad,
        logits_grad,
        attention_in_own,
        attention_out_own,
        expert_in_grad,
        expert_out_grad,
        small_sums[0],
        small_sums[1],
        small_sums[2],
        small_sums[3],
        small_sums[4],
        small_sums[5],
    )


def solution(mesh):
    in_specs = (
        P(("dp", "mp"), None),
        P("dp", None, "mp"),
        P("mp", "dp"),
        P(None, None, "dp", "mp"),
        P(None, "mp", "dp"),
        P(),
        P(),
        P(),
        P(),
        P(),
        P(),
        P("dp", None),
        P("dp", None),
        P(("dp", "mp"), None),
    )
    out_specs = (
        P(("dp", "mp"), None),
        P(("dp", "mp"), None),
        P(("dp", "mp"), None),
        P("dp", None, "mp"),
        P("mp", "dp"),
        P(None, None, "dp", "mp"),
        P(None, "mp", "dp"),
        P(),
        P(),
        P(),
        P(),
        P(),
        P(),
    )
    return jax.shard_map(
        per_device, mesh=mesh, in_specs=in_specs, out_specs=out_specs, check_vma=False
    )
```

profile of v0, /device:TPU:0, one launch (start us, length us, event | category | flops | bytes accessed | tf_op | source)
XLA Modules:
  0.0 1411.9 jit_solution(13169112331441578595)
XLA Ops:
  13.1 38.8 %all_gather.25 = bf16[768,3,192]{2,1,0:T(4,128)(2,1)S(1)} all-gather(bf16[96,3,192]{2,1,0:T(4,128)(2,1)S(1)} %copy.137), channel_id=1, replica_groups=mesh['dp'=8,'mp'=4] {'dp'}, dimensions={0}, use_global_device_ids=true | all-gather | bytes 995328 | tf_op jit(solution)/shard_map/all_gather | solution.py:125
  52.7 31.2 %all_gather.26 = bf16[192,768]{0,1:T(8,128)(2,1)S(1)} all-gather(bf16[192,96]{0,1:T(8,128)(2,1)S(1)} %copy.142), channel_id=1, replica_groups=mesh['dp'=8,'mp'=4] {'dp'}, dimensions={1}, use_global_device_ids=true | all-gather | bytes 331776 | tf_op jit(solution)/shard_map/all_gather | solution.py:126
  88.2 19.1 %while.32 = (s32[]{:T(128)}, bf16[2,512,3,64]{1,3,2,0:T(8,128)(2,1)S(1)}, f32[2,3,512]{2,1,0:T(4,128)S(1)}, s32[2]{0:T(128)S(1)}, bf16[2,512,3,64]{1,3,2,0:T(8,1...) while((s32[]{:T(128)}, ...), condition=%wide.region_4.5_spmd.clone, body=%wide.region_1.4_spmd.clone.sunk | while | flops 422050816 | bytes 22411556 | solution.py:174
  111.8 36.4 %reduce-scatter.14.cloned.1.call-done = f32[256,768]{1,0:T(8,128)} async-done(((f32[1024,768]{1,0:T(8,128)}), f32[256,768]{1,0:T(8,128)}) %reduce-scatter.14.cloned.1.call-update) | async-done | bytes 786448 | tf_op jit(solution)/shard_map/reduce_scatter | solution.py:177
  158.0 8.6 scatter_custom_fusion
  169.5 11.7 gather_fusion.2
  181.2 10.1 all-gather.9.cloned.1.call-done
  193.2 16.8 %gather_fusion.3 = f32[2048]{0:T(1024)S(1)} fusion(f32[1024,12]{0,1:T(8,128)S(1)} %convolution_add_fusion.1, s32[2048]{0:T(1024)S(1)} %reshape.424), kind=kCustom, calls=%fused_computation.3 | custom fusion | bytes 32768 | tf_op jit(solution)/shard_map/jit(take_along_axis)/gather | solution.py:185
  211.3 11.8 gather_fusion.1
  223.1 9.4 gather_fusion
  232.5 137.5 %all-gather.11.cloned.1.call-done = bf16[8,2,768,512]{3,2,1,0:T(8,128)(2,1)} async-done(((bf16[8,2,96,512]{3,2,1,0:T(8,128)(2,1)}), bf16[8,2,768,512]{3,2,1,0:T(8,128)(2,1)}) %all-gather.11.cloned.1.call-update) | async-done | bytes 12582928 | tf_op jit(solution)/shard_map/all_gather | solution.py:192
  370.0 12.2 convolution_bitcast_fusion.1
  382.2 87.4 %all-gather.13.cloned.1.call-done = bf16[8,512,768]{1,2,0:T(8,128)(2,1)} async-done(((bf16[8,512,96]{1,2,0:T(8,128)(2,1)}), bf16[8,512,768]{1,2,0:T(8,128)(2,1)}) %all-gather.13.cloned.1.call-update) | async-done | bytes 6291472 | tf_op jit(solution)/shard_map/all_gather | solution.py:193
  469.6 9.3 fusion.60
  478.9 4.0 fusion.53
  482.8 14.8 %scatter_custom_fusion.3 = f32[2049]{0:T(1024)S(1)} fusion(s32[2048]{0:T(1024)} %get-tuple-element.535, f32[2048]{0:T(1024)S(1)} %bitcast.334, f32[]{:T(128)} %constant.213.clone.1), kind=kCustom, calls=%fused_computation.228 | custom fusion | flops 2048 | bytes 8708 | tf_op jit(solution)/shard_map/scatter-add | solution.py:257
  499.1 11.4 fusion.50
  510.6 16.8 %scatter_custom_fusion.2 = f32[1024,768]{1,0:T(8,128)} fusion(s32[2048]{0:T(1024)} %get-tuple-element.538, f32[2048,768]{1,0:T(8,128)} %bitcast.345, f32[]{:T(128)} %constant.213.clone.1), kind=kCustom, calls=%fused_computation.101 | custom fusion | flops 1572864 | bytes 3146240 | tf_op jit(solution)/shard_map/scatter-add | solution.py:252
  531.4 32.2 %reduce-scatter.18.cloned.1.call-done = f32[256,768]{1,0:T(8,128)} async-done(((f32[1024,768]{1,0:T(8,128)}), f32[256,768]{1,0:T(8,128)}) %reduce-scatter.18.cloned.1.call-update) | async-done | bytes 786448 | tf_op jit(solution)/shard_map/reduce_scatter | solution.py:261
  567.8 16.7 %scatter_custom_fusion.1 = f32[1024,768]{1,0:T(8,128)} fusion(s32[2048]{0:T(1024)} %get-tuple-element.538, f32[2048,768]{1,0:T(8,128)} %bitcast.277, f32[]{:T(128)} %constant.213.clone.1), kind=kCustom, calls=%fused_computation.103 | custom fusion | flops 1572864 | bytes 3146240 | tf_op jit(solution)/shard_map/scatter-add | solution.py:206
  598.2 52.0 %while.33 = (s32[]{:T(128)}, f32[2,512,3,64]{1,0,3,2:T(2,128)}, f32[2,1024,3,64]{1,3,2,0:T(8,128)}, f32[2,1024,3,64]{1,3,2,0:T(8,128)}, s32[2]{0:T(128)S(1)}, /*...) while((s32[]{:T(128)}, f32[2,512,3,64]{1,0,3,2:T(2,128)}, ...), condition=%wide.region_34.35_spmd.clone, body=%wide.region_32.34_spmd.clone.sunk | while | flops 1031044096 | bytes 67418504 | solution.py:345
  616.1 8.1 dynamic_update_slice.51
  642.1 8.1 dynamic_update_slice.51
  660.5 15.0 %convolution_bitcast_fusion = f32[8,2,768,512]{2,3,1,0:T(8,128)} fusion(bf16[8,256,768,1]{2,1,3,0:T(8,128)(2,1)} %bitcast.272, bf16[8,1,256,512]{3,2,0,1:T(8,128)(2,1)} %get-tuple-element.517, bf16[8,1,256,512]{3,2,0,1:T(8,128)(2,1)} %copy-done.23), kind=kOutput, calls=%fused_computation.67 | convolution fusion | flops 3223322624 | bytes 32505856 | tf_op jit(solution)/shard_map/ecd,ekcf->ekdf/dot_general | solution.py:243
  675.5 25.1 %copy.158 = f32[8,2,768,512]{3,0,1,2:T(8,128)} copy(f32[8,2,768,512]{2,3,1,0:T(8,128)} %convolution_bitcast_fusion) | data formatting | bytes 50331648 | tf_op jit(solution)/shard_map/ecd,ekcf->ekdf/transpose | solution.py:243
  701.6 4.5 fusion.61
  706.2 9.2 fusion.55
  723.6 46.3 %all-reduce = (f32[768]{0:T(1024)}, f32[768]{0:T(1024)}, f32[768,12]{0,1:T(8,128)}, f32[12,12]{1,0:T(8,128)}, f32[768,4]{0,1:T(4,128)}, /*index=5*/f32[2,768]{1,0:T(2,128)}) all-reduce(f32[768]{0:T(1024)S(1)} %get-tuple-element.441, f32[768]{0:T(1024)S(1)} %get-tuple-element.437, ...), channel_id=1, replica_groups=mesh['dp'=8,'mp'=4] {'dp','mp'}, use_global_device_ids=true, to_apply=%region_44.45 | all-reduce | flops 15504 | bytes 124032 | tf_op jit(solution)/shard_map/psum | solution.py:383
  772.2 350.6 %reduce-scatter.24.cloned.1.call-done = f32[8,2,96,512]{3,0,1,2:T(8,128)} async-done(((f32[8,2,768,512]{3,0,1,2:T(8,128)}), f32[8,2,96,512]{3,0,1,2:T(8,128)}) %reduce-scatter.24.cloned.1.call-update) | async-done | bytes 3145744 | tf_op jit(solution)/shard_map/reduce_scatter | solution.py:381
  1122.8 5.4 copy.160
  1128.2 66.6 %reduce-scatter.22.cloned.1.call-done = f32[96,3,192]{2,0,1:T(8,128)} async-done(((f32[768,3,192]{2,0,1:T(8,128)}), f32[96,3,192]{2,0,1:T(8,128)}) %reduce-scatter.22.cloned.1.call-update) | async-done | bytes 221200 | tf_op jit(solution)/shard_map/reduce_scatter | solution.py:378
  1194.8 210.4 %reduce-scatter.26.cloned.1.call-done = f32[8,512,96]{1,2,0:T(8,128)} async-done(((f32[8,512,768]{1,2,0:T(8,128)}), f32[8,512,96]{1,2,0:T(8,128)}) %reduce-scatter.26.cloned.1.call-update) | async-done | bytes 1572880 | tf_op jit(solution)/shard_map/reduce_scatter | solution.py:382
  (334 shorter events, 117.1 us)
Async XLA Ops:
  7.2 160.0 %copy-start = (f32[1024,12]{0,1:T(8,128)S(1)}, f32[1024,12]{0,1:T(8,128)}, u32[]{:S(2)}) copy-start(f32[1024,12]{0,1:T(8,128)} %param.29) | copy-start | bytes 147460
  7.2 77.3 %all-gather.7.cloned.1.call-start = ((), (), s32[]{:S(2)}) async-start(), calls=%async_computation.9 | async-start | bytes 1966080 | tf_op jit(solution)/shard_map/all_gather | solution.py:123
  11.0 137.2 %reduce-scatter.14.cloned.1.call-start = ((), (), s32[]{:S(2)}) async-start(), calls=%async_computation.10 | async-start | bytes 3932160 | tf_op jit(solution)/shard_map/reduce_scatter | solution.py:177
  52.7 34.4 %copy-start.30 = (bf16[768,3,192]{0,2,1:T(8,128)(2,1)}, bf16[768,3,192]{0,2,1:T(8,128)(2,1)S(1)}, u32[]{:S(2)}) copy-start(bf16[768,3,192]{0,2,1:T(8,128)(2,1)S(1)} %copy.138) | copy-start | bytes 2654212
  83.9 23.9 %copy-start.19 = (bf16[192,768]{0,1:T(8,128)(2,1)}, bf16[192,768]{0,1:T(8,128)(2,1)S(1)}, u32[]{:S(2)}) copy-start(bf16[192,768]{0,1:T(8,128)(2,1)S(1)} %all_gather.26) | copy-start | bytes 884740
  108.6 39.6 %copy-start.11 = (bf16[256,768]{1,0:T(8,128)(2,1)S(1)}, bf16[256,768]{1,0:T(8,128)(2,1)}, u32[]{:S(2)}) copy-start(bf16[256,768]{1,0:T(8,128)(2,1)} %param.18) | copy-start | bytes 1179652
  110.9 41.6 %copy-start.35 = (s32[1024,2]{0,1:T(2,128)S(1)}, s32[1024,2]{0,1:T(2,128)}, u32[]{:S(2)}) copy-start(s32[1024,2]{0,1:T(2,128)} %param.30) | copy-start | bytes 24580
  110.9 58.6 %all-gather.15.cloned.1.call-start = ((), (), s32[]{:S(2)}) async-start(), calls=%async_computation.15 | async-start | bytes 1966080 | tf_op jit(solution)/shard_map/all_gather | solution.py:229
  111.7 79.6 %all-gather.9.cloned.1.call-start = ((), (), s32[]{:S(2)}) async-start(), calls=%async_computation.11 | async-start | bytes 1966080 | tf_op jit(solution)/shard_map/all_gather | solution.py:181
  111.7 41.0 %copy-start.37 = (f32[768]{0:T(1024)}, f32[768]{0:T(1024)S(1)}, u32[]{:S(2)}) copy-start(f32[768]{0:T(1024)S(1)} %convert_element_type.167) | copy-start | bytes 9220
  151.3 218.7 %all-gather.11.cloned.1.call-start = ((), (), s32[]{:S(2)}) async-start(), calls=%async_computation.12 | async-start | bytes 14155776 | tf_op jit(solution)/shard_map/all_gather | solution.py:192
  151.9 317.7 %all-gather.13.cloned.1.call-start = ((), (), s32[]{:S(2)}) async-start(), calls=%async_computation.13 | async-start | bytes 7077888 | tf_op jit(solution)/shard_map/all_gather | solution.py:193
  152.5 377.2 %reduce-scatter.28.cloned.1.call-start = ((), (), s32[]{:S(2)}) async-start(), calls=%async_computation.22 | async-start | bytes 655360
  169.5 21.8 %copy-start.41 = (bf16[768,12]{0,1:T(8,128)(2,1)S(1)}, bf16[768,12]{0,1:T(8,128)(2,1)}, u32[]{:S(2)}) copy-start(bf16[768,12]{0,1:T(8,128)(2,1)} %param.25) | copy-start | bytes 55300
  193.2 18.1 %copy-start.49 = (s32[2048]{0:T(1024)S(1)}, s32[2048]{0:T(1024)}, u32[]{:S(2)}) copy-start(s32[2048]{0:T(1024)} %get-tuple-element.536) | copy-start | bytes 24580
  478.8 20.3 %copy-start.23 = (bf16[8,1,256,512]{3,2,0,1:T(8,128)(2,1)}, bf16[8,1,256,512]{3,2,0,1:T(8,128)(2,1)S(1)}, u32[]{:S(2)}) copy-start(bf16[8,1,256,512]{3,2,0,1:T(8,128)(2,1)S(1)} %get-tuple-element.516) | copy-start | bytes 6291460
  498.9 64.7 %reduce-scatter.18.cloned.1.call-start = ((), (), s32[]{:S(2)}) async-start(), calls=%async_computation.16 | async-start | bytes 3932160 | tf_op jit(solution)/shard_map/reduce_scatter | solution.py:261
  510.5 17.6 %copy-start.13 = (bf16[256,768]{1,0:T(8,128)(2,1)S(1)}, bf16[256,768]{1,0:T(8,128)(2,1)}, u32[]{:S(2)}) copy-start(bf16[256,768]{1,0:T(8,128)(2,1)} %param.31) | copy-start | bytes 1179652
  527.4 60.4 %all-gather.17.cloned.1.call-start = ((), (), s32[]{:S(2)}) async-start(), calls=%async_computation.17 | async-start | bytes 1966080 | tf_op jit(solution)/shard_map/all_gather | solution.py:311
  528.0 39.6 %copy-start.59 = (pred[256]{0:T(512)(128)(4,1)}, pred[256]{0:T(512)(128)(4,1)S(1)}, u32[]{:S(2)}) copy-start(pred[256]{0:T(512)(128)(4,1)S(1)} %get-tuple-element.460) | copy-start | bytes 772
  528.0 39.6 %copy-start.61 = (pred[256]{0:T(512)(128)(4,1)}, pred[256]{0:T(512)(128)(4,1)S(1)}, u32[]{:S(2)}) copy-start(pred[256]{0:T(512)(128)(4,1)S(1)} %get-tuple-element.554) | copy-start | bytes 772
  528.1 39.6 %copy-start.63 = (pred[256]{0:T(512)(128)(4,1)}, pred[256]{0:T(512)(128)(4,1)S(1)}, u32[]{:S(2)}) copy-start(pred[256]{0:T(512)(128)(4,1)S(1)} %get-tuple-element.555) | copy-start | bytes 772
  528.1 39.6 %copy-start.65 = (pred[256]{0:T(512)(128)(4,1)}, pred[256]{0:T(512)(128)(4,1)S(1)}, u32[]{:S(2)}) copy-start(pred[256]{0:T(512)(128)(4,1)S(1)} %get-tuple-element.556) | copy-start | bytes 772
  530.7 36.9 %copy-start.67 = (f32[256,1]{0,1:T(1,128)}, f32[256,1]{0,1:T(1,128)S(1)}, u32[]{:S(2)}) copy-start(f32[256,1]{0,1:T(1,128)S(1)} %get-tuple-element.549) | copy-start | bytes 3076
  530.8 36.9 %copy-start.69 = (f32[256,1]{0,1:T(1,128)}, f32[256,1]{0,1:T(1,128)S(1)}, u32[]{:S(2)}) copy-start(f32[256,1]{0,1:T(1,128)S(1)} %get-tuple-element.550) | copy-start | bytes 3076
  567.7 150.2 %reduce-scatter.16.cloned.1.call-start = ((), (), s32[]{:S(2)}) async-start(), calls=%async_computation.14 | async-start | bytes 1966080 | tf_op jit(solution)/shard_map/reduce_scatter | solution.py:207
  587.7 132.8 %reduce-scatter.30.cloned.1.call-start = ((), (), s32[]{:S(2)}) async-start(), calls=%async_computation.23 | async-start | bytes 884736
  597.9 124.3 %reduce-scatter.20.cloned.1.call-start = ((), (), s32[]{:S(2)}) async-start(), calls=%async_computation.18 | async-start | bytes 1966080 | tf_op jit(solution)/shard_map/reduce_scatter | solution.py:372
  660.0 462.8 %reduce-scatter.24.cloned.1.call-start = ((), (), s32[]{:S(2)}) async-start(), calls=%async_computation.20 | async-start | bytes 28311552 | tf_op jit(solution)/shard_map/reduce_scatter | solution.py:381
  700.7 494.1 %reduce-scatter.22.cloned.1.call-start = ((), (), s32[]{:S(2)}) async-start(), calls=%async_computation.19 | async-start | bytes 2654208 | tf_op jit(solution)/shard_map/reduce_scatter | solution.py:378
  706.1 699.1 %reduce-scatter.26.cloned.1.call-start = ((), (), s32[]{:S(2)}) async-start(), calls=%async_computation.21 | async-start | bytes 14155776 | tf_op jit(solution)/shard_map/reduce_scatter | solution.py:382
  715.5 54.4 %copy-start.16 = (f32[256,768]{1,0:T(8,128)S(1)}, f32[256,768]{1,0:T(8,128)}, u32[]{:S(2)}) copy-start(f32[256,768]{1,0:T(8,128)} %copy-done.15) | copy-start | bytes 2359300
  (58 other events, 338.5 us)
Sparse Core Ops, SparseCore 0:
  11.2 22.3 all-gather.6
  111.0 37.1 reduce-scatter.13
  149.8 19.6 all-gather.14
  171.6 19.6 all-gather.8
  193.6 176.4 all-gather.10
  372.3 97.1 all-gather.12
  499.0 19.8 reduce-scatter.27
  527.5 36.0 reduce-scatter.17
  567.9 19.6 all-gather.16
  590.1 28.1 reduce-scatter.15
  621.6 62.3 reduce-scatter.29
  686.6 27.2 reduce-scatter.19
  717.8 404.9 reduce-scatter.23
  1126.7 68.0 reduce-scatter.21
  1198.8 206.3 reduce-scatter.25
where the time goes:
time: 1420 us; the launch traced here: 1410 us
  waiting for transfers between devices  935 us (66%)
  local copies, waits for them, and re-layouts  133 us (9%)
  blocking collectives  116 us (8%)
  matrix products  113 us (8%)
  other arithmetic  83.7 us (6%)
  between operations  15.4 us (1%)
    reduce_scatter x1, waiting for transfers between devices, per_device(): lax.psum_scatter(input_side_grad, 'dp', scatter_dimension=2, tiled=True)  351 us
    reduce_scatter x1, waiting for transfers between devices, per_device(): lax.psum_scatter(output_side_grad, 'dp', scatter_dimension=2, tiled=True)  210 us
    all_gather x1, waiting for transfers between devices, per_device(): lax.all_gather(expert_input, 'dp', axis=2, tiled=True)  137 us
    all_gather x1, waiting for transfers between devices, per_device(): lax.all_gather(expert_output, 'dp', axis=2, tiled=True)  87.4 us
    reduce_scatter x1, waiting for transfers between devices, per_device(): lax.psum_scatter(attention_in_grad, 'dp', scatter_dimension=0, tiled=True)  66.6 us
    psum x1, blocking collectives, per_device(): lax.psum((first_gain_grad, second_gain_grad, router_grad, logit_carry_gra...  46.3 us
    all_gather x1, blocking collectives, per_device(): lax.all_gather(query_key_value, 'dp', axis=0, tiled=True)  38.8 us
    reduce_scatter x1, waiting for transfers between devices, per_device(): lax.psum_scatter(attention_part, 'mp', scatter_dimension=0, tiled=True)  36.4 us
  transfers between devices with their start and end apart: 15, of which 9 were waited for; matrix products, arithmetic and copies ran while one was open for 19% of the time, Pallas kernels for 0%

commit v1 on v0

--- a/solution.py
+++ b/solution.py
@@ -86,6 +86,38 @@
         expert_value
         + jnp.where(chosen_expert == NFFN + 2, constant_rows[0], 0.0)
         + jnp.where(chosen_expert == NFFN + 3, constant_rows[1], 0.0)
+    )
+
+
+def clusters():
+    groups = lax.axis_size("dp") // NFFN
+    near = [[group * NFFN + expert for expert in range(NFFN)] for group in range(groups)]
+    far = [[group * NFFN + expert for group in range(groups)] for expert in range(NFFN)]
+    return groups, near, far
+
+
+def swap(blocks):
+    _, near, _ = clusters()
+    return lax.all_to_all(blocks, "dp", 0, 0, axis_index_groups=near, tiled=True)
+
+
+def exchange(shard, dim):
+    groups, near, far = clusters()
+    own = lax.all_to_all(shard, "dp", 0, dim, axis_index_groups=near, tiled=True)
+    if groups > 1:
+        own = lax.all_gather(own, "dp", axis=dim, axis_index_groups=far, tiled=True)
+    return own
+
+
+def exchange_back(grads, dim):
+    groups, near, far = clusters()
+    if groups > 1:
+        grads = lax.psum_scatter(
+            grads, "dp", scatter_dimension=dim, axis_index_groups=far, tiled=True
+        )
+    grads = grads.astype(jnp.bfloat16)
+    return lax.all_to_all(grads, "dp", dim, 0, axis_index_groups=near, tiled=True).astype(
+        jnp.float32
     )
 
 
@@ -188,20 +220,19 @@
     gate_table = jnp.concatenate([gates.reshape(-1), jnp.zeros((1,), jnp.float32)])[
         assigned
     ].reshape(NFFN, CAP)
-    expert_in_rows, expert_out_rows = (
-        lax.all_gather(expert_input, "dp", axis=2, tiled=True),
-        lax.all_gather(expert_output, "dp", axis=2, tiled=True),
-    )
-    rows_in = rows_two[tokens_of].reshape(NFFN, CAP, model_width)
-    gate_up = jnp.einsum(
-        "ecd,ekdf->ekcf", rows_in, expert_in_rows, preferred_element_type=jnp.float32
-    )
-    gate_pre = gate_up[:, 0]
-    up_pre = gate_up[:, 1]
+    expert_in_rows = exchange(expert_input, 2)[0]
+    expert_out_rows = exchange(expert_output, 2)[0]
+    rows_in = swap(rows_two[tokens_of].reshape(NFFN, CAP, model_width))
+    rows_in = rows_in.reshape(NFFN * CAP, model_width)
+    gate_up = jnp.einsum("cd,kdf->kcf", rows_in, expert_in_rows, preferred_element_type=jnp.float32)
+    gate_pre = gate_up[0]
+    up_pre = gate_up[1]
     hidden_units = (jax.nn.silu(gate_pre) * up_pre).astype(jnp.bfloat16)
     expert_rows = jnp.einsum(
-        "ecf,efd->ecd", hidden_units, expert_out_rows, preferred_element_type=jnp.float32
-    )
+        "cf,fd->cd", hidden_units, expert_out_rows, preferred_element_type=jnp.float32
+    )
+    expert_rows = swap(expert_rows.astype(jnp.bfloat16).reshape(NFFN, CAP, model_width))
+    expert_rows = expert_rows.astype(jnp.float32)
     weighted = (expert_rows * gate_table[:, :, None]).reshape(NFFN * CAP, model_width)
     routed = jnp.zeros((group_rows, model_width), jnp.float32).at[tokens_of].add(weighted)
     routed_own = lax.psum_scatter(
@@ -230,22 +261,25 @@
     slot_grads = grad_rows_all[tokens_of].reshape(NFFN, CAP, model_width).astype(jnp.float32)
     expert_grad = (slot_grads * gate_table[:, :, None]).astype(jnp.bfloat16)
     gate_slot = jnp.sum(slot_grads * expert_rows, axis=-1)
+    out_grad = swap(expert_grad).reshape(NFFN * CAP, model_width)
     output_side_grad = jnp.einsum(
-        "ecf,ecd->efd", hidden_units, expert_grad, preferred_element_type=jnp.float32
+        "cf,cd->fd", hidden_units, out_grad, preferred_element_type=jnp.float32
     )
     units_grad = jnp.einsum(
-        "ecd,efd->ecf", expert_grad, expert_out_rows, preferred_element_type=jnp.float32
+        "cd,fd->cf", out_grad, expert_out_rows, preferred_element_type=jnp.float32
     )
     sigmoid_gate = jax.nn.sigmoid(gate_pre)
     gate_pre_grad = units_grad * up_pre * sigmoid_gate * (1.0 + gate_pre * (1.0 - sigmoid_gate))
     up_pre_grad = units_grad * gate_pre * sigmoid_gate
-    pre_grads = jnp.stack([gate_pre_grad, up_pre_grad], axis=1).astype(jnp.bfloat16)
+    pre_grads = jnp.stack([gate_pre_grad, up_pre_grad], axis=0).astype(jnp.bfloat16)
     input_side_grad = jnp.einsum(
-        "ecd,ekcf->ekdf", rows_in, pre_grads, preferred_element_type=jnp.float32
+        "cd,kcf->kdf", rows_in, pre_grads, preferred_element_type=jnp.float32
     )
     rows_grad = jnp.einsum(
-        "ekcf,ekdf->ecd", pre_grads, expert_in_rows, preferred_element_type=jnp.float32
-    )
+        "kcf,kdf->cd", pre_grads, expert_in_rows, preferred_element_type=jnp.float32
+    )
+    rows_grad = swap(rows_grad.astype(jnp.bfloat16).reshape(NFFN, CAP, model_width))
+    rows_grad = rows_grad.astype(jnp.float32)
     normed_part = (
         jnp.zeros((group_rows, model_width), jnp.float32)
         .at[tokens_of]
@@ -378,8 +412,8 @@
         lax.psum_scatter(attention_in_grad, "dp", scatter_dimension=0, tiled=True),
         lax.psum_scatter(output_weight_grad, "dp", scatter_dimension=1, tiled=True),
     )
-    expert_in_grad = lax.psum_scatter(input_side_grad, "dp", scatter_dimension=2, tiled=True)
-    expert_out_grad = lax.psum_scatter(output_side_grad, "dp", scatter_dimension=2, tiled=True)
+    expert_in_grad = exchange_back(input_side_grad[None], 2)
+    expert_out_grad = exchange_back(output_side_grad[None], 2)
     small_sums = lax.psum(
         (
             first_gain_grad,

time: 1420 us -> 861 us (0.61)
  waiting for transfers between devices: 935 us -> 283 us
  blocking collectives: 116 us -> 196 us
  starting transfers between devices: 1.4 us -> 31.1 us
  matrix products: 113 us -> 97.9 us
    reduce_scatter x2 -> x0, waiting for transfers between devices: 561 us -> none  [the longest x1 351 us: per_device(): lax.psum_scatter(input_side_grad, 'dp', scatter_dimension=2, tiled=True)]
    all_gather x2 -> x0, waiting for transfers between devices: 225 us -> none  [the longest x1 137 us: per_device(): lax.all_gather(expert_input, 'dp', axis=2, tiled=True)]
    all_to_all x0 -> x7, waiting for transfers between devices: none -> 188 us  [the longest x3 130 us: swap(): lax.all_to_all(blocks, 'dp', 0, 0, axis_index_groups=near, tiled=True)]
    all_to_all x0 -> x1, blocking collectives: none -> 85.1 us  [swap(): lax.all_to_all(blocks, 'dp', 0, 0, axis_index_groups=near, tiled=True)]
    reduce_scatter x1, waiting for transfers between devices: 66.6 us -> 0.01 us  [per_device(): lax.psum_scatter(attention_in_grad, 'dp', scatter_dimension=0, tiled=True)]
    all_to_all x0 -> x7, starting transfers between devices: none -> 30.1 us  [the longest x3 13.8 us: swap(): lax.all_to_all(blocks, 'dp', 0, 0, axis_index_groups=near, tiled=True)]
    dot_general x6, matrix products: 61 us -> 31.6 us  [the longest x1 6.75 us: per_device(): jnp.einsum('cd,kcf->kdf', rows_in, pre_grads, preferred_element_type=jnp....]
    transpose x1 -> x0, local copies, waits for them, and re-layouts: 25.1 us -> none  [per_device(): jnp.einsum('ecd,ekcf->ekdf', rows_in, pre_grads, preferred_element_type=j...]
  transfers between devices with their start and end apart: 15 -> 18, of which waited for: 9 -> 11; matrix products, arithmetic and copies ran while one was open for 19% -> 30% of each run, Pallas kernels for 0% -> 0%
where the time goes in v1:
time: 861 us; the launch traced here: 854 us
  waiting for transfers between devices  283 us (33%)
  blocking collectives  196 us (23%)
  local copies, waits for them, and re-layouts  126 us (15%)
  matrix products  97.9 us (11%)
  other arithmetic  92.3 us (11%)
  starting transfers between devices  31.1 us (4%)
  between operations  15.6 us (2%)
  loops' own time  13.3 us (2%)
    all_to_all x3, waiting for transfers between devices, swap(): lax.all_to_all(blocks, 'dp', 0, 0, axis_index_groups=near, tiled=True)  130 us
    all_to_all x1, blocking collectives, swap(): lax.all_to_all(blocks, 'dp', 0, 0, axis_index_groups=near, tiled=True)  85.1 us
    all_to_all x2, waiting for transfers between devices, exchange_back(): lax.all_to_all(grads, 'dp', dim, 0, axis_index_groups=near, tiled=True)  48 us
    psum x1, blocking collectives, per_device(): lax.psum((first_gain_grad, second_gain_grad, router_grad, logit_carry_gra...  40.4 us
    all_gather x1, blocking collectives, per_device(): lax.all_gather(query_key_value, 'dp', axis=0, tiled=True)  39.1 us
    reduce_scatter x1, waiting for transfers between devices, per_device(): lax.psum_scatter(attention_part, 'mp', scatter_dimension=0, tiled=True)  33.2 us
    reduce_scatter x1, waiting for transfers between devices, per_device(): lax.psum_scatter(normed_part, 'mp', scatter_dimension=0, tiled=True)  31.5 us
    all_gather x1, blocking collectives, per_device(): lax.all_gather(output_weight, 'dp', axis=1, tiled=True)  31.2 us
  transfers between devices with their start and end apart: 18, of which 11 were waited for; matrix products, arithmetic and copies ran while one was open for 30% of the time, Pallas kernels for 0%

profile of v1, /device:TPU:0, one launch (start us, length us, event | category | flops | bytes accessed | tf_op | source)
XLA Modules:
  0.0 854.5 jit_solution(2021750881868784335)
XLA Ops:
  12.7 39.1 %all_gather.19 = bf16[768,3,192]{2,1,0:T(4,128)(2,1)S(1)} all-gather(bf16[96,3,192]{2,1,0:T(4,128)(2,1)S(1)} %copy.138), channel_id=1, replica_groups=mesh['dp'=8,'mp'=4] {'dp'}, dimensions={0}, use_global_device_ids=true | all-gather | bytes 995328 | tf_op jit(solution)/shard_map/all_gather | solution.py:157
  52.8 31.2 %all_gather.20 = bf16[192,768]{0,1:T(8,128)(2,1)S(1)} all-gather(bf16[192,96]{0,1:T(8,128)(2,1)S(1)} %copy.143), channel_id=1, replica_groups=mesh['dp'=8,'mp'=4] {'dp'}, dimensions={1}, use_global_device_ids=true | all-gather | bytes 331776 | tf_op jit(solution)/shard_map/all_gather | solution.py:158
  87.8 19.1 %while.32 = (s32[]{:T(128)}, bf16[2,512,3,64]{1,3,2,0:T(8,128)(2,1)S(1)}, f32[2,3,512]{2,1,0:T(4,128)S(1)}, s32[2]{0:T(128)S(1)}, bf16[2,512,3,64]{1,3,2,0:T(8,1...) while((s32[]{:T(128)}, ...), condition=%wide.region_4.5_spmd.clone, body=%wide.region_1.4_spmd.clone.sunk | while | flops 422050816 | bytes 22411556 | solution.py:206
  113.6 33.2 %reduce-scatter.12.cloned.1.call-done = f32[256,768]{1,0:T(8,128)} async-done(((f32[1024,768]{1,0:T(8,128)}), f32[256,768]{1,0:T(8,128)}) %reduce-scatter.12.cloned.1.call-update) | async-done | bytes 786448 | tf_op jit(solution)/shard_map/reduce_scatter | solution.py:209
  154.9 8.3 scatter_custom_fusion
  163.9 5.9 all-gather.7.cloned.1.call-done
  169.8 11.7 %gather_fusion = bf16[2048,768]{1,0:T(8,128)(2,1)} fusion(bf16[1024,768]{1,0:T(8,128)(2,1)} %all-gather.7.cloned.1.call-done, s32[2048]{0:T(1024)S(1)} %get-tuple-element.523), kind=kCustom, calls=%fused_computation | custom fusion | bytes 6299648 | tf_op jit(solution)/shard_map/gather | solution.py:225
  181.4 5.5 all-to-all-start
  188.3 69.9 %all-to-all-done = bf16[8,256,768]{2,1,0:T(8,128)(2,1)} async-done(((bf16[8,256,768]{2,1,0:T(8,128)(2,1)}), bf16[8,256,768]{2,1,0:T(8,128)(2,1)}, u32[]{:S(2)}, u32[]{:S(2)}) %all-to-all-start) | async-done | bytes 3145760 | tf_op jit(solution)/shard_map/all_to_all | solution.py:101
  261.8 5.9 convolution_bitcast_fusion
  272.4 9.8 %all-to-all-done.2 = bf16[8,512,96]{1,2,0:T(8,128)(2,1)S(1)} async-done(((bf16[8,512,96]{1,2,0:T(8,128)(2,1)}), bf16[8,512,96]{1,2,0:T(8,128)(2,1)S(1)}, u32[]{:S(2)}, u32[]{:S(2)}) %all-to-all-start.2) | async-done | bytes 786464 | tf_op jit(solution)/shard_map/all_to_all | solution.py:106
  291.7 20.8 %all-gather.9.cloned.1.call-done = bf16[1024,768]{1,0:T(8,128)(2,1)} async-done(((bf16[256,768]{1,0:T(8,128)(2,1)}), bf16[1024,768]{1,0:T(8,128)(2,1)}) %all-gather.9.cloned.1.call-update) | async-done | bytes 1572880 | tf_op jit(solution)/shard_map/all_gather | solution.py:260
  312.6 11.7 %gather_fusion.2 = bf16[2048,768]{1,0:T(8,128)(2,1)} fusion(bf16[1024,768]{1,0:T(8,128)(2,1)} %all-gather.9.cloned.1.call-done, s32[2048]{0:T(1024)S(1)} %get-tuple-element.523), kind=kCustom, calls=%fused_computation.2 | custom fusion | bytes 6299648 | tf_op jit(solution)/shard_map/gather | solution.py:261
  324.8 16.8 %gather_fusion.3 = f32[2048]{0:T(1024)S(1)} fusion(f32[1024,12]{0,1:T(8,128)S(1)} %convolution_add_fusion.1, s32[2048]{0:T(1024)S(1)} %reshape.464), kind=kCustom, calls=%fused_computation.3 | custom fusion | bytes 32768 | tf_op jit(solution)/shard_map/jit(take_along_axis)/gather | solution.py:217
  342.9 11.8 %gather_fusion.1 = f32[2048]{0:T(1024)S(1)} fusion(f32[2049]{0:T(1024)S(1)} %pad_maximum_fusion.13, s32[2048]{0:T(1024)S(1)} %copy-done.63), kind=kCustom, calls=%fused_computation.1 | custom fusion | bytes 24576 | tf_op jit(solution)/shard_map/gather | solution.py:220
  354.7 5.7 all-to-all-done.3
  365.4 85.1 %all_to_all.68 = bf16[8,256,768]{2,1,0:T(8,128)(2,1)S(1)} all-to-all(bf16[8,256,768]{2,1,0:T(8,128)(2,1)S(1)} %get-tuple-element.525), channel_id=1, replica_groups={{0,4,8,12,16,20,24,28},{1,5,9,13,17,21,25,29},{2,6,10,14,18,22,26,30},{..., dimensions={0} | all-to-all | bytes 6291456 | tf_op jit(solution)/shard_map/all_to_all | solution.py:101
  450.5 6.3 fusion.68
  465.5 14.8 %scatter_custom_fusion.3 = f32[2049]{0:T(1024)S(1)} fusion(s32[2048]{0:T(1024)} %get-tuple-element.521, f32[2048]{0:T(1024)S(1)} %bitcast.399, f32[]{:T(128)} %constant.213.clone.1), kind=kCustom, calls=%fused_computation.243 | custom fusion | flops 2048 | bytes 8708 | tf_op jit(solution)/shard_map/scatter-add | solution.py:291
  481.6 54.1 %all-to-all-done.5 = bf16[8,256,768]{2,1,0:T(8,128)(2,1)S(1)} async-done(((bf16[8,256,768]{2,1,0:T(8,128)(2,1)}), bf16[8,256,768]{2,1,0:T(8,128)(2,1)S(1)}, u32[]{:S(2)}, u32[]{:S(2)}) %all-to-all-start.5) | async-done | bytes 3145760 | tf_op jit(solution)/shard_map/all_to_all | solution.py:101
  535.7 16.3 %scatter_custom_fusion.2 = f32[1024,768]{1,0:T(8,128)} fusion(s32[2048]{0:T(1024)} %get-tuple-element.524, bf16[2048,768]{1,0:T(8,128)(2,1)S(1)} %bitcast.329, f32[]{:T(128)} %constant.213.clone.1), kind=kCustom, calls=%fused_computation.70 | custom fusion | flops 3145728 | bytes 6291968 | tf_op jit(solution)/shard_map/scatter-add | solution.py:286
  556.9 31.5 %reduce-scatter.16.cloned.1.call-done = f32[256,768]{1,0:T(8,128)} async-done(((f32[1024,768]{1,0:T(8,128)}), f32[256,768]{1,0:T(8,128)}) %reduce-scatter.16.cloned.1.call-update) | async-done | bytes 786448 | tf_op jit(solution)/shard_map/reduce_scatter | solution.py:295
  592.5 15.5 %scatter_custom_fusion.1 = f32[1024,768]{1,0:T(8,128)S(1)} fusion(s32[2048]{0:T(1024)} %get-tuple-element.524, f32[2048,768]{1,0:T(8,128)} %bitcast.334, f32[]{:T(128)} %constant.213.clone.1), kind=kCustom, calls=%fused_computation.115 | custom fusion | flops 1572864 | bytes 3146240 | tf_op jit(solution)/shard_map/scatter-add | solution.py:237
  618.8 71.5 %while.33 = (s32[]{:T(128)}, f32[2,512,3,64]{1,0,3,2:T(2,128)}, f32[2,1024,3,64]{1,3,2,0:T(8,128)}, f32[2,1024,3,64]{1,3,2,0:T(8,128)}, s32[2]{0:T(128)S(1)}, /*...) while((s32[]{:T(128)}, f32[2,512,3,64]{1,0,3,2:T(2,128)}, ...), condition=%wide.region_34.35_spmd.clone, body=%wide.region_32.34_spmd.clone.sunk | while | flops 1031044096 | bytes 96782976 | solution.py:379
  637.9 8.1 dynamic_update_slice.51
  673.6 8.1 dynamic_update_slice.51
  707.5 5.4 reduce.22
  719.6 6.8 fusion.75
  729.4 10.8 %all-to-all-done.7 = bf16[8,2,24576]{2,1,0:T(2,128)(2,1)S(1)} async-done(((bf16[8,2,24576]{2,1,0:T(2,128)(2,1)}), bf16[8,2,24576]{2,1,0:T(2,128)(2,1)S(1)}, u32[]{:S(2)}, u32[]{:S(2)}) %all-to-all-start.7) | async-done | bytes 786464 | tf_op jit(solution)/shard_map/all_to_all | solution.py:119
  753.4 5.5 reshape.541
  761.9 37.3 %all-to-all-done.6 = bf16[1,2,768,512]{3,1,0,2:T(2,128)(2,1)S(1)} async-done(((bf16[1,2,768,512]{3,1,0,2:T(2,128)(2,1)}), bf16[1,2,768,512]{3,1,0,2:T(2,128)(2,1)S(1)}, u32[]{:S(2)}, u32[]{:S(2)}) %all-to-all-start.6) | async-done | bytes 1572896 | tf_op jit(solution)/shard_map/all_to_all | solution.py:119
  805.0 40.4 %all-reduce = (f32[768]{0:T(1024)}, f32[768]{0:T(1024)}, f32[768,12]{0,1:T(8,128)}, f32[12,12]{1,0:T(8,128)}, f32[768,4]{0,1:T(4,128)}, /*index=5*/f32[2,768]{1,0:T(2,128)}) all-reduce(f32[768]{0:T(1024)S(1)} %get-tuple-element.428, f32[768]{0:T(1024)S(1)} %get-tuple-element.424, ...), channel_id=1, replica_groups=mesh['dp'=8,'mp'=4] {'dp','mp'}, use_global_device_ids=true, to_apply=%region_42.43 | all-reduce | flops 15504 | bytes 124032 | tf_op jit(solution)/shard_map/psum | solution.py:417
  (395 shorter events, 192.5 us)
Async XLA Ops:
  7.2 284.2 %copy-start = (f32[1024,12]{0,1:T(8,128)S(1)}, f32[1024,12]{0,1:T(8,128)}, u32[]{:S(2)}) copy-start(f32[1024,12]{0,1:T(8,128)} %param.29) | copy-start | bytes 147460
  7.2 45.5 %copy-start.62 = (bf16[192,96]{1,0:T(8,128)(2,1)S(1)}, bf16[192,96]{1,0:T(8,128)(2,1)}, u32[]{:S(2)}) copy-start(bf16[192,96]{1,0:T(8,128)(2,1)} %param.20) | copy-start | bytes 110596
  7.2 77.4 %all-gather.5.cloned.1.call-start = ((), (), s32[]{:S(2)}) async-start(), calls=%async_computation.15 | async-start | bytes 1966080 | tf_op jit(solution)/shard_map/all_gather | solution.py:155
  11.6 135.2 %reduce-scatter.12.cloned.1.call-start = ((), (), s32[]{:S(2)}) async-start(), calls=%async_computation.16 | async-start | bytes 3932160 | tf_op jit(solution)/shard_map/reduce_scatter | solution.py:209
  52.7 34.5 %copy-start.42 = (bf16[768,3,192]{0,2,1:T(8,128)(2,1)}, bf16[768,3,192]{0,2,1:T(8,128)(2,1)S(1)}, u32[]{:S(2)}) copy-start(bf16[768,3,192]{0,2,1:T(8,128)(2,1)S(1)} %copy.139) | copy-start | bytes 2654212
  109.7 37.1 %copy-start.15 = (bf16[256,768]{1,0:T(8,128)(2,1)S(1)}, bf16[256,768]{1,0:T(8,128)(2,1)}, u32[]{:S(2)}) copy-start(bf16[256,768]{1,0:T(8,128)(2,1)} %param.18) | copy-start | bytes 1179652
  109.8 40.1 %copy-start.50 = (s32[1024,2]{0,1:T(2,128)S(1)}, s32[1024,2]{0,1:T(2,128)}, u32[]{:S(2)}) copy-start(s32[1024,2]{0,1:T(2,128)} %param.30) | copy-start | bytes 24580
  109.8 71.6 %all-to-all-start.1 = ((bf16[8,2,96,512]{3,2,1,0:T(8,128)(2,1)}), bf16[8,2,96,512]{3,2,1,0:T(8,128)(2,1)S(1)}, u32[]{:S(2)}, u32[]{:S(2)}) async-start(bf16[8,2,96,512]{3,2,1,0:T(8,128)(2,1)} %param.21), calls=%async_computation.2 | async-start | bytes 3145728 | tf_op jit(solution)/shard_map/all_to_all | solution.py:106
  113.6 56.2 %all-gather.7.cloned.1.call-start = ((), (), s32[]{:S(2)}) async-start(), calls=%async_computation.17 | async-start | bytes 1966080 | tf_op jit(solution)/shard_map/all_gather | solution.py:213
  113.6 36.3 %copy-start.52 = (f32[768]{0:T(1024)}, f32[768]{0:T(1024)S(1)}, u32[]{:S(2)}) copy-start(f32[768]{0:T(1024)S(1)} %convert_element_type.220) | copy-start | bytes 9220
  148.2 33.3 %copy-start.60 = (f32[256]{0:T(256)}, f32[256]{0:T(256)S(1)}, u32[]{:S(2)}) copy-start(f32[256]{0:T(256)S(1)} %add_rsqrt_fusion) | copy-start | bytes 3076
  181.4 76.7 %all-to-all-start = ((bf16[8,256,768]{2,1,0:T(8,128)(2,1)}), bf16[8,256,768]{2,1,0:T(8,128)(2,1)}, u32[]{:S(2)}, u32[]{:S(2)}) async-start(bf16[8,256,768]{2,1,0:T(8,128)(2,1)} %bitcast.10), calls=%async_computation.1 | async-start | bytes 6291456 | tf_op jit(solution)/shard_map/all_to_all | solution.py:101
  258.2 24.0 %all-to-all-start.2 = ((bf16[8,512,96]{1,2,0:T(8,128)(2,1)}), bf16[8,512,96]{1,2,0:T(8,128)(2,1)S(1)}, u32[]{:S(2)}, u32[]{:S(2)}) async-start(bf16[8,512,96]{1,2,0:T(8,128)(2,1)} %param.22), calls=%async_computation.3 | async-start | bytes 1572864 | tf_op jit(solution)/shard_map/all_to_all | solution.py:106
  285.7 74.7 %all-to-all-start.3 = ((bf16[8,256,768]{2,1,0:T(8,128)(2,1)}), bf16[8,256,768]{2,1,0:T(8,128)(2,1)}, u32[]{:S(2)}, u32[]{:S(2)}) async-start(bf16[8,256,768]{2,1,0:T(8,128)(2,1)} %bitcast.21), calls=%async_computation.4 | async-start | bytes 6291456 | tf_op jit(solution)/shard_map/all_to_all | solution.py:101
  290.3 22.2 %all-gather.9.cloned.1.call-start = ((), (), s32[]{:S(2)}) async-start(), calls=%async_computation.19 | async-start | bytes 1966080 | tf_op jit(solution)/shard_map/all_gather | solution.py:260
  291.7 32.6 %copy-start.1 = (bf16[1024,768]{1,0:T(8,128)(2,1)S(1)}, bf16[1024,768]{1,0:T(8,128)(2,1)}, u32[]{:S(2)}) copy-start(bf16[1024,768]{1,0:T(8,128)(2,1)} %all-gather.7.cloned.1.call-done) | copy-start | bytes 4718596
  365.4 85.1 %copy-start.45 = (bf16[8,512,96]{1,2,0:T(8,128)(2,1)S(1)}, bf16[8,512,96]{1,2,0:T(8,128)(2,1)}, u32[]{:S(2)}) copy-start(bf16[8,512,96]{1,2,0:T(8,128)(2,1)} %copy-done.44) | copy-start | bytes 2359300
  461.7 74.0 %all-to-all-start.5 = ((bf16[8,256,768]{2,1,0:T(8,128)(2,1)}), bf16[8,256,768]{2,1,0:T(8,128)(2,1)S(1)}, u32[]{:S(2)}, u32[]{:S(2)}) async-start(bf16[8,256,768]{2,1,0:T(8,128)(2,1)} %bitcast.339), calls=%async_computation.7 | async-start | bytes 6291456 | tf_op jit(solution)/shard_map/all_to_all | solution.py:101
  465.4 89.7 %reduce-scatter.22.cloned.1.call-start = ((), (), s32[]{:S(2)}) async-start(), calls=%async_computation.24 | async-start | bytes 655360
  481.6 106.8 %reduce-scatter.16.cloned.1.call-start = ((), (), s32[]{:S(2)}) async-start(), calls=%async_computation.20 | async-start | bytes 3932160 | tf_op jit(solution)/shard_map/reduce_scatter | solution.py:295
  552.1 60.2 %all-gather.11.cloned.1.call-start = ((), (), s32[]{:S(2)}) async-start(), calls=%async_computation.21 | async-start | bytes 1966080 | tf_op jit(solution)/shard_map/all_gather | solution.py:345
  553.5 37.0 %copy-start.69 = (pred[256]{0:T(512)(128)(4,1)}, pred[256]{0:T(512)(128)(4,1)S(1)}, u32[]{:S(2)}) copy-start(pred[256]{0:T(512)(128)(4,1)S(1)} %get-tuple-element.447) | copy-start | bytes 772
  553.5 38.9 %copy-start.75 = (pred[256]{0:T(512)(128)(4,1)}, pred[256]{0:T(512)(128)(4,1)S(1)}, u32[]{:S(2)}) copy-start(pred[256]{0:T(512)(128)(4,1)S(1)} %get-tuple-element.543) | copy-start | bytes 772
  556.3 36.1 %copy-start.79 = (f32[256,1]{0,1:T(1,128)}, f32[256,1]{0,1:T(1,128)S(1)}, u32[]{:S(2)}) copy-start(f32[256,1]{0,1:T(1,128)S(1)} %get-tuple-element.537) | copy-start | bytes 3076
  592.4 158.4 %reduce-scatter.14.cloned.1.call-start = ((), (), s32[]{:S(2)}) async-start(), calls=%async_computation.18 | async-start | bytes 1966080 | tf_op jit(solution)/shard_map/reduce_scatter | solution.py:238
  609.3 192.7 %reduce-scatter.24.cloned.1.call-start = ((), (), s32[]{:S(2)}) async-start(), calls=%async_computation.25 | async-start | bytes 884736
  618.3 185.3 %reduce-scatter.18.cloned.1.call-start = ((), (), s32[]{:S(2)}) async-start(), calls=%async_computation.22 | async-start | bytes 1966080 | tf_op jit(solution)/shard_map/reduce_scatter | solution.py:406
  714.4 25.8 %all-to-all-start.7 = ((bf16[8,2,24576]{2,1,0:T(2,128)(2,1)}), bf16[8,2,24576]{2,1,0:T(2,128)(2,1)S(1)}, u32[]{:S(2)}, u32[]{:S(2)}) async-start(bf16[8,2,24576]{2,1,0:T(2,128)(2,1)} %reshape.540), calls=%async_computation.12 | async-start | bytes 1572864 | tf_op jit(solution)/shard_map/all_to_all | solution.py:119
  740.2 59.0 %all-to-all-start.6 = ((bf16[1,2,768,512]{3,1,0,2:T(2,128)(2,1)}), bf16[1,2,768,512]{3,1,0,2:T(2,128)(2,1)S(1)}, u32[]{:S(2)}, u32[]{:S(2)}) async-start(bf16[1,2,768,512]{3,1,0,2:T(2,128)(2,1)} %copy.158), calls=%async_computation.11 | async-start | bytes 3145728 | tf_op jit(solution)/shard_map/all_to_all | solution.py:119
  743.9 103.8 %reduce-scatter.20.cloned.1.call-start = ((), (), s32[]{:S(2)}) async-start(), calls=%async_computation.23 | async-start | bytes 2654208 | tf_op jit(solution)/shard_map/reduce_scatter | solution.py:412
  799.9 45.5 %copy-start.18 = (bf16[256,768]{1,0:T(8,128)(2,1)S(1)}, bf16[256,768]{1,0:T(8,128)(2,1)}, u32[]{:S(2)}) copy-start(bf16[256,768]{1,0:T(8,128)(2,1)} %param.31) | copy-start | bytes 1179652
  800.0 45.5 %copy-start.21 = (f32[256,768]{1,0:T(8,128)S(1)}, f32[256,768]{1,0:T(8,128)}, u32[]{:S(2)}) copy-start(f32[256,768]{1,0:T(8,128)} %copy-done.20) | copy-start | bytes 2359300
  (83 other events, 438.2 us)
Sparse Core Ops, SparseCore 0:
  11.7 22.3 all-gather.4
  109.9 36.9 reduce-scatter.11
  150.1 19.6 all-gather.6
  292.5 20.0 all-gather.8
  481.7 22.0 reduce-scatter.21
  552.2 36.0 reduce-scatter.15
  592.6 19.6 all-gather.10
  615.5 28.1 reduce-scatter.13
  647.0 62.4 reduce-scatter.23
  712.1 27.1 reduce-scatter.17
  748.8 87.2 reduce-scatter.19

commit v2 on v1

--- a/solution.py
+++ b/solution.py
@@ -1,40 +1,313 @@
+import functools
+import numpy as np
 import jax
 import jax.numpy as jnp
 from jax import lax
 from jax.sharding import PartitionSpec as P
+from jax.experimental import pallas as pl
+from jax.experimental.pallas import tpu as pltpu
 
 HD = 64
 NFFN = 8
 NEXP = 12
 SEQ = 1024
 CAP = 256
-
+MP = 4
+QUARTER = CAP // MP
 
 epsilon = 1e-06
 rope_base = 10000.0
 highest = lax.Precision.HIGHEST
-
-
-def rope_tables(length, period, half):
-    positions = (jnp.arange(length, dtype=jnp.int32) % period).astype(jnp.float32)
-    frequency = rope_base ** (-jnp.arange(half, dtype=jnp.float32) / half)
-    angles = positions[:, None] * frequency[None, :]
-    return (jnp.cos(angles), jnp.sin(angles))
-
-
-def rotate(values, cosine, sine_table):
-    half = values.shape[-1] // 2
-    front_half = values[..., :half]
-    back_half = values[..., half:]
-    cosine = cosine[:, None, :]
-    sine_table = sine_table[:, None, :]
-    return jnp.concatenate(
-        [
-            front_half * cosine - back_half * sine_table,
-            back_half * cosine + front_half * sine_table,
+f32 = jnp.float32
+bf16 = jnp.bfloat16
+MESH = pl.DeviceIdType.MESH
+VM = pl.BlockSpec(memory_space=pltpu.VMEM)
+HB = pl.BlockSpec(memory_space=pl.ANY)
+NT = (((1,), (1,)), ((), ()))
+TN = (((0,), (0,)), ((), ()))
+
+
+def flip(index, distance):
+    out = index
+    bit = 1
+    while bit <= distance:
+        if distance & bit:
+            out = out + bit - 2 * bit * ((index // bit) % 2)
+        bit *= 2
+    return out
+
+
+def dotf(a, b, dims=None):
+    if dims is None:
+        return jnp.dot(a, b, preferred_element_type=f32)
+    return lax.dot_general(a, b, dims, preferred_element_type=f32)
+
+
+def remote(src, dst, send, recv, **where):
+    return pltpu.make_async_remote_copy(
+        src_ref=src, dst_ref=dst, send_sem=send, recv_sem=recv, device_id=where, device_id_type=MESH
+    )
+
+
+def greet(mp_me, near, base):
+    barrier = pltpu.get_barrier_semaphore()
+    for k in range(1, MP):
+        pl.semaphore_signal(barrier, inc=1, device_id={"mp": flip(mp_me, k)}, device_id_type=MESH)
+    for k in range(1, NFFN):
+        pl.semaphore_signal(
+            barrier, inc=1, device_id={"dp": base + flip(near, k)}, device_id_type=MESH
+        )
+    pl.semaphore_wait(barrier, MP - 1 + NFFN - 1)
+
+
+def rope_constants():
+    half = HD // 2
+    positions = np.arange(SEQ, dtype=np.float32)
+    frequency = (rope_base ** (-np.arange(half, dtype=np.float32) / half)).astype(np.float32)
+    angles = (positions[:, None] * frequency[None, :]).astype(np.float32)
+    cosine, sine = np.cos(angles), np.sin(angles)
+    return (
+        np.concatenate([cosine, cosine], axis=1),
+        np.concatenate([-sine, sine], axis=1),
+    )
+
+
+def swap_halves(x):
+    half = HD // 2
+    return jnp.concatenate([x[:, half:], x[:, :half]], axis=1)
+
+
+class Gather:
+    def __init__(self, ref, mp_me, send, recv):
+        self.me, self.core, self.chip = mp_me, flip(mp_me, 1), flip(mp_me, 2)
+        own = ref.at[mp_me]
+        far = ref.at[self.chip]
+        self.to_chip = remote(own, own, send.at[0], recv.at[0], mp=self.chip)
+        self.to_core = remote(own, own, send.at[1], recv.at[1], mp=self.core)
+        self.relay = remote(far, far, send.at[2], recv.at[2], mp=self.core)
+
+    def start(self):
+        self.to_chip.start()
+        self.to_core.start()
+
+    def forward(self):
+        self.to_chip.wait_recv()
+        self.relay.start()
+
+    def finish(self):
+        self.to_core.wait_recv()
+        self.relay.wait_recv()
+        self.to_chip.wait_send()
+        self.to_core.wait_send()
+        self.relay.wait_send()
+
+
+def attention_kernel(
+    inside,
+    x_ref, gain1_ref, gain2_ref, cos_ref, sin_ref, wshard_ref, win_shard, wout_shard,
+    rows1_ref, w_ref, q_ref, k_ref, v_ref, mixed_ref, lse_ref, hidden_ref, rows2_ref, *rest,
+):
+    if inside:
+        win_ref, wout_ref, *rest = rest
+    (part_ref, core_in, chip_out, chip_in, core_out,
+     sends, recvs, wsend, wrecv, esend, erecv, local) = rest
+    mp_me = lax.axis_index("mp")
+    dp_me = lax.axis_index("dp")
+    near = lax.rem(dp_me, NFFN)
+    base = dp_me - near
+    core, chip = flip(mp_me, 1), flip(mp_me, 2)
+    rows = x_ref.shape[0]
+    depth = w_ref.shape[1]
+    greet(mp_me, near, base)
+
+    tokens = x_ref[...].astype(f32)
+    scale = lax.rsqrt(jnp.mean(tokens * tokens, axis=-1, keepdims=True) + epsilon)
+    rows1_ref[mp_me] = (tokens * scale * gain1_ref[...]).astype(bf16)
+    gather1 = Gather(rows1_ref, mp_me, sends.at[pl.ds(0, 3)], recvs.at[pl.ds(0, 3)])
+    gather1.start()
+
+    if inside:
+        w_ref[near] = wshard_ref[...]
+        own = w_ref.at[near]
+        along = [
+            remote(own, own, wsend.at[k], wrecv.at[k], dp=base + flip(near, k)) for k in (2, 4, 6)
+        ]
+        for copy in along:
+            copy.start()
+        mate = base + flip(near, 1)
+        across = [remote(own, own, wsend.at[0], wrecv.at[0], dp=mate)]
+        across[0].start()
+        for k, copy in zip((2, 4, 6), along):
+            copy.wait_recv()
+            block = w_ref.at[flip(near, k)]
+            onward = remote(block, block, wsend.at[k + 1], wrecv.at[k + 1], dp=mate)
+            onward.start()
+            across.append(onward)
+        gather1.forward()
+        for copy in across:
+            copy.wait_recv()
+        for copy in along + across:
+            copy.wait_send()
+        experts = []
+        din = win_shard.shape[2]
+        place = pl.ds(pl.multiple_of(near * din, din), din)
+        for k in (6, 4, 7, 5, 2, 3, 1):
+            peer = flip(near, k)
+            for i, (src, dst) in enumerate(
+                [(win_shard.at[peer], win_ref.at[:, place]), (wout_shard.at[peer], wout_ref.at[place])]
+            ):
+                experts.append(
+                    remote(src, dst, esend.at[i, k], erecv.at[i, k], dp=base + peer)
+                )
+        for copy in experts:
+            copy.start()
+        mine = [
+            pltpu.make_async_copy(win_shard.at[near], win_ref.at[:, place], local.at[0]),
+            pltpu.make_async_copy(wout_shard.at[near], wout_ref.at[place], local.at[1]),
+        ]
+        for copy in mine:
+            copy.start()
+    else:
+        w_ref[...] = wshard_ref[...]
+        gather1.forward()
+    gather1.finish()
+
+    width = x_ref.shape[1]
+    w_all = w_ref[...].reshape(width, w_ref.shape[2])
+    heads = q_ref.shape[0]
+    cols = heads * HD
+
+    def project(i, carry):
+        at = pl.ds(pl.multiple_of(i * rows, rows), rows)
+        joint = dotf(rows1_ref[i], w_all[:, : 3 * cols])
+        cosine, sine = cos_ref[at], sin_ref[at]
+        for h in range(heads):
+            query = joint[:, h * HD : (h + 1) * HD]
+            key = joint[:, cols + h * HD : cols + (h + 1) * HD]
+            q_ref[h, at] = (query * cosine + swap_halves(query) * sine).astype(bf16)
+            k_ref[h, at] = (key * cosine + swap_halves(key) * sine).astype(bf16)
+            v_ref[h, at] = joint[:, 2 * cols + h * HD : 2 * cols + (h + 1) * HD].astype(bf16)
+        return carry
+
+    lax.fori_loop(0, MP, project, 0)
+    out_weight = w_all[:, 3 * cols :]
+
+    to_core = [
+        remote(core_out.at[j], core_in.at[j], sends.at[3 + j], recvs.at[3 + j], mp=core)
+        for j in range(2)
+    ]
+    to_chip = remote(chip_out, chip_in, sends.at[5], recvs.at[5], mp=chip)
+
+    def attend(step, carry):
+        block = flip(mp_me, 3)
+        block = jnp.where(step == 1, core, jnp.where(step == 2, chip, jnp.where(step == 3, mp_me, block)))
+        at = pl.ds(pl.multiple_of(block * rows, rows), rows)
+        row_ids = block * rows + lax.broadcasted_iota(jnp.int32, (rows, SEQ), 0)
+        seen = row_ids >= lax.broadcasted_iota(jnp.int32, (rows, SEQ), 1)
+        for h in range(heads):
+            scores = dotf(q_ref[h, at], k_ref[h], NT) * HD**-0.5
+            scores = jnp.where(seen, scores, -jnp.inf)
+            peak = jnp.max(scores, axis=-1, keepdims=True)
+            exponent = jnp.exp(scores - peak)
+            total = jnp.sum(exponent, axis=-1, keepdims=True)
+            probs = (exponent * (1.0 / total)).astype(bf16)
+            mixed_ref[at, h * HD : (h + 1) * HD] = dotf(probs, v_ref[h]).astype(bf16)
+            lse_ref[at, h : h + 1] = peak + jnp.log(total)
+        part = dotf(mixed_ref[at], out_weight, NT)
+
+        @pl.when(step == 0)
+        def _():
+            core_out[0] = part.astype(bf16)
+            to_core[0].start()
+
+        @pl.when(step == 1)
+        def _():
+            core_out[1] = part.astype(bf16)
+            to_core[1].start()
+
+        @pl.when(step == 2)
+        def _():
+            to_core[0].wait_recv()
+            chip_out[...] = (part + core_in[0].astype(f32)).astype(bf16)
+            to_chip.start()
+
+        @pl.when(step == 3)
+        def _():
+            part_ref[...] = part
+
+        return carry
+
+    lax.fori_loop(0, MP, attend, 0)
+    to_core[1].wait_recv()
+    partial = part_ref[...] + core_in[1].astype(f32)
+    to_chip.wait_recv()
+    hidden = x_ref[...].astype(f32) + (partial + chip_in[...].astype(f32))
+    hidden_ref[...] = hidden
+    scale2 = lax.rsqrt(jnp.mean(hidden * hidden, axis=-1, keepdims=True) + epsilon)
+    rows2_ref[mp_me] = (hidden * scale2 * gain2_ref[...]).astype(bf16)
+    gather2 = Gather(rows2_ref, mp_me, sends.at[pl.ds(6, 3)], recvs.at[pl.ds(6, 3)])
+    gather2.start()
+    for copy in to_core + [to_chip]:
+        copy.wait_send()
+    gather2.forward()
+    gather2.finish()
+    if inside:
+        for copy in experts:
+            copy.wait_recv()
+        for copy in experts:
+            copy.wait_send()
+        for copy in mine:
+            copy.wait()
+
+
+def attention(x, gain1, gain2, wshard, win, wout, groups):
+    rows, width = x.shape
+    cos, sin = rope_constants()
+    inside = groups == 1
+    cols = wshard.shape[-1]
+    depth = width // NFFN
+    hidden_cols = win.shape[-1]
+    heads = cols // 4 // HD
+    sd = jax.ShapeDtypeStruct
+    outs = [
+        sd((MP, rows, width), bf16),
+        sd((NFFN, depth, cols), bf16),
+        sd((heads, SEQ, HD), bf16),
+        sd((heads, SEQ, HD), bf16),
+        sd((heads, SEQ, HD), bf16),
+        sd((SEQ, heads * HD), bf16),
+        sd((SEQ, 128), f32),
+        sd((rows, width), f32),
+        sd((MP, rows, width), bf16),
+    ]
+    specs = [VM] * len(outs)
+    if inside:
+        outs += [sd((2, width, hidden_cols), bf16), sd((width, hidden_cols), bf16)]
+        specs += [HB, HB]
+    else:
+        wshard = wshard.reshape(NFFN, depth, cols)
+    dma = pltpu.SemaphoreType.DMA
+    return pl.pallas_call(
+        functools.partial(attention_kernel, inside),
+        out_shape=outs,
+        in_specs=[VM] * 6 + [HB, HB],
+        out_specs=specs,
+        scratch_shapes=[
+            pltpu.VMEM((rows, width), f32),
+            pltpu.VMEM((2, rows, width), bf16),
+            pltpu.VMEM((rows, width), bf16),
+            pltpu.VMEM((rows, width), bf16),
+            pltpu.VMEM((2, rows, width), bf16),
+            dma((9,)), dma((9,)),
+            dma((8,)), dma((8,)),
+            dma((2, 8)), dma((2, 8)),
+            dma((2,)),
         ],
-        axis=-1,
-    )
+        compiler_params=pltpu.CompilerParams(
+            collective_id=0, has_side_effects=True, vmem_limit_bytes=56 * 2**20
+        ),
+        name="attention_forward",
+    )(x, gain1, gain2, jnp.asarray(cos), jnp.asarray(sin), wshard, win, wout)
 
 
 def rotate_back(grads, cosine, sine_table):
@@ -151,26 +424,37 @@
     gain_two = second_gain.astype(jnp.float32)
     tokens = inputs.astype(jnp.float32)
     scale_one = lax.rsqrt(jnp.mean(tokens * tokens, axis=-1, keepdims=True) + epsilon)
-    normed_one = (tokens * scale_one * gain_one).astype(jnp.bfloat16)
-    rows_one = lax.all_gather(normed_one, "mp", axis=0, tiled=True)
-    attention_in, attention_out = (
-        lax.all_gather(query_key_value, "dp", axis=0, tiled=True),
-        lax.all_gather(output_weight, "dp", axis=1, tiled=True),
-    )
-    joint_proj = jnp.einsum(
-        "td,dkf->tkf", rows_one, attention_in, preferred_element_type=jnp.float32
-    )
-    cosine, sine_table = rope_tables(group_rows, SEQ, HD // 2)
-    queries = rotate(
-        joint_proj[:, 0].reshape(group_rows, heads_here, HD), cosine, sine_table
-    ).astype(jnp.bfloat16)
-    keys_turned = rotate(
-        joint_proj[:, 1].reshape(group_rows, heads_here, HD), cosine, sine_table
-    ).astype(jnp.bfloat16)
-    values_heads = joint_proj[:, 2].reshape(group_rows, heads_here, HD).astype(jnp.bfloat16)
-    query_blocks = queries.reshape(block_count, block_rows, heads_here, HD)
-    key_seqs = keys_turned.reshape(sequences, SEQ, heads_here, HD)
-    value_seqs = values_heads.reshape(sequences, SEQ, heads_here, HD)
+    cos, sin = rope_constants()
+    cosine, sine_table = jnp.asarray(cos[:, : HD // 2]), jnp.asarray(sin[:, HD // 2 :])
+    groups, _, _ = clusters()
+    shard = jnp.concatenate(
+        [query_key_value.reshape(query_key_value.shape[0], -1), output_weight.T], axis=1
+    )
+    expert_output_t = expert_output.transpose(0, 2, 1)
+    if groups > 1:
+        shard = lax.all_gather(shard, "dp", axis=0, tiled=True)
+        expert_in_rows = exchange(expert_input, 2)[0]
+        expert_out_t = exchange(expert_output_t, 1)[0]
+    got = attention(
+        inputs, gain_one[None], gain_two[None], shard, expert_input, expert_output_t, groups
+    )
+    if groups == 1:
+        expert_in_rows, expert_out_t = got[9:]
+    rows_one = got[0].reshape(group_rows, model_width)
+    weights_all = got[1].reshape(model_width, -1)
+    attention_in = weights_all[:, : 3 * heads_here * HD].reshape(model_width, 3, heads_here * HD)
+    attention_out = weights_all[:, 3 * heads_here * HD :].T
+    query_blocks, key_seqs, value_seqs = (
+        part.transpose(1, 0, 2).reshape(-1, rows, heads_here, HD)
+        for part, rows in zip(got[2:5], (block_rows, SEQ, SEQ))
+    )
+    mixed = got[5]
+    log_totals = got[6][:, :heads_here].reshape(block_count, block_rows, heads_here)
+    log_totals = log_totals.transpose(0, 2, 1)
+    hidden = got[7]
+    scale_two = lax.rsqrt(jnp.mean(hidden * hidden, axis=-1, keepdims=True) + epsilon)
+    rows_two = got[8].reshape(group_rows, model_width)
+    normed_two = lax.dynamic_slice_in_dim(rows_two, offset, shard_rows, 0)
     key_positions = jnp.arange(SEQ, dtype=jnp.int32)
 
     def block_scores(block_index):
@@ -192,25 +476,6 @@
             value_seqs[seq_index],
         )
 
-    def attend_block(block_index):
-        scores, query_rows, key_rows, value_rows = block_scores(block_index)
-        row_peak = jnp.max(scores, axis=-1, keepdims=True)
-        exponent = jnp.exp(scores - row_peak)
-        row_total = jnp.sum(exponent, axis=-1, keepdims=True)
-        attention_weights = (exponent / row_total).astype(jnp.bfloat16)
-        mixed_rows = jnp.einsum(
-            "hqk,khd->qhd", attention_weights, value_rows, preferred_element_type=jnp.float32
-        )
-        return (mixed_rows, (row_peak + jnp.log(row_total))[..., 0])
-
-    mixed_blocks, log_totals = lax.map(attend_block, jnp.arange(block_count, dtype=jnp.int32))
-    mixed = mixed_blocks.reshape(group_rows, heads_here * HD).astype(jnp.bfloat16)
-    attention_part = jnp.dot(mixed, attention_out, preferred_element_type=jnp.float32)
-    attended = lax.psum_scatter(attention_part, "mp", scatter_dimension=0, tiled=True)
-    hidden = tokens + attended
-    scale_two = lax.rsqrt(jnp.mean(hidden * hidden, axis=-1, keepdims=True) + epsilon)
-    normed_two = (hidden * scale_two * gain_two).astype(jnp.bfloat16)
-    rows_two = lax.all_gather(normed_two, "mp", axis=0, tiled=True)
     logits = jnp.dot(rows_two, router_weight, preferred_element_type=jnp.float32) + jnp.dot(
         previous_logits, logit_carry, precision=highest
     )
@@ -220,8 +485,6 @@
     gate_table = jnp.concatenate([gates.reshape(-1), jnp.zeros((1,), jnp.float32)])[
         assigned
     ].reshape(NFFN, CAP)
-    expert_in_rows = exchange(expert_input, 2)[0]
-    expert_out_rows = exchange(expert_output, 2)[0]
     rows_in = swap(rows_two[tokens_of].reshape(NFFN, CAP, model_width))
     rows_in = rows_in.reshape(NFFN * CAP, model_width)
     gate_up = jnp.einsum("cd,kdf->kcf", rows_in, expert_in_rows, preferred_element_type=jnp.float32)
@@ -229,7 +492,7 @@
     up_pre = gate_up[1]
     hidden_units = (jax.nn.silu(gate_pre) * up_pre).astype(jnp.bfloat16)
     expert_rows = jnp.einsum(
-        "cf,fd->cd", hidden_units, expert_out_rows, preferred_element_type=jnp.float32
+        "cf,df->cd", hidden_units, expert_out_t, preferred_element_type=jnp.float32
     )
     expert_rows = swap(expert_rows.astype(jnp.bfloat16).reshape(NFFN, CAP, model_width))
     expert_rows = expert_rows.astype(jnp.float32)
@@ -266,7 +529,7 @@
         "cf,cd->fd", hidden_units, out_grad, preferred_element_type=jnp.float32
     )
     units_grad = jnp.einsum(
-        "cd,fd->cf", out_grad, expert_out_rows, preferred_element_type=jnp.float32
+        "cd,df->cf", out_grad, expert_out_t, preferred_element_type=jnp.float32
     )
     sigmoid_gate = jax.nn.sigmoid(gate_pre)
     gate_pre_grad = units_grad * up_pre * sigmoid_gate * (1.0 + gate_pre * (1.0 - sigmoid_gate))

time: 861 us -> 764 us (0.89)
  waiting for transfers between devices: 283 us -> 151 us
  Pallas kernels: 0 us -> 81.6 us
  matrix products: 97.9 us -> 74.4 us
  starting transfers between devices: 31.1 us -> 17.7 us
    pallas_call x0 -> x1, Pallas kernels: none -> 81.6 us  [attention(): pl.pallas_call(functools.partial(attention_kernel, inside), out_shape=out...]
    all_gather x2 -> x0, blocking collectives: 70.2 us -> none  [the longest x1 39.1 us: per_device(): lax.all_gather(query_key_value, 'dp', axis=0, tiled=True)]
    all_to_all x3 -> x2, waiting for transfers between devices: 130 us -> 62 us  [swap(): lax.all_to_all(blocks, 'dp', 0, 0, axis_index_groups=near, tiled=True)]
    all_to_all x1 -> x2, blocking collectives: 85.1 us -> 150 us  [swap(): lax.all_to_all(blocks, 'dp', 0, 0, axis_index_groups=near, tiled=True)]
    reduce_scatter x1 -> x0, waiting for transfers between devices: 33.2 us -> none  [per_device(): lax.psum_scatter(attention_part, 'mp', scatter_dimension=0, tiled=True)]
    all_gather x1, waiting for transfers between devices: 20.8 us -> 0.02 us  [per_device(): grad_rows_all = lax.all_gather(cotangent, 'mp', axis=0, tiled=True)]
    dot_general x4 -> x2, matrix products: 11.9 us -> 2.05 us  [block_scores(): jnp.einsum('qhd,khd->hqk', query_rows, key_rows, preferred_element_type=j...]
    all_to_all x2 -> x0, waiting for transfers between devices: 9.77 us -> none  [exchange(): lax.all_to_all(shard, 'dp', 0, dim, axis_index_groups=near, tiled=True)]
  transfers between devices with their start and end apart: 18 -> 12, of which waited for: 11 -> 6; matrix products, arithmetic and copies ran while one was open for 30% -> 29% of each run, Pallas kernels for 0% -> 0%
where the time goes in v2:
time: 764 us; the launch traced here: 754 us
  blocking collectives  190 us (25%)
  waiting for transfers between devices  151 us (20%)
  local copies, waits for them, and re-layouts  128 us (17%)
  other arithmetic  88.2 us (12%)
  Pallas kernels  81.6 us (11%)
  matrix products  74.4 us (10%)
  starting transfers between devices  17.7 us (2%)
  between operations  15.2 us (2%)
    all_to_all x2, blocking collectives, swap(): lax.all_to_all(blocks, 'dp', 0, 0, axis_index_groups=near, tiled=True)  150 us
    pallas_call x1, Pallas kernels, attention(): pl.pallas_call(functools.partial(attention_kernel, inside), out_shape=out...  81.6 us
    all_to_all x2, waiting for transfers between devices, swap(): lax.all_to_all(blocks, 'dp', 0, 0, axis_index_groups=near, tiled=True)  62 us
    all_to_all x2, waiting for transfers between devices, exchange_back(): lax.all_to_all(grads, 'dp', dim, 0, axis_index_groups=near, tiled=True)  49.3 us
    psum x1, blocking collectives, per_device(): lax.psum((first_gain_grad, second_gain_grad, router_grad, logit_carry_gra...  40.4 us
    reduce_scatter x1, waiting for transfers between devices, per_device(): lax.psum_scatter(normed_part, 'mp', scatter_dimension=0, tiled=True)  28.3 us
    unnamed x94, local copies, waits for them, and re-layouts  26 us
    gather x5, local copies, waits for them, and re-layouts, per_device(): chosen = jnp.take_along_axis(logits, routes, axis=1)  17.9 us
  transfers between devices with their start and end apart: 12, of which 6 were waited for; matrix products, arithmetic and copies ran while one was open for 29% of the time, Pallas kernels for 0%

profile of v2, /device:TPU:0, one launch (start us, length us, event | category | flops | bytes accessed | tf_op | source)
XLA Modules:
  0.0 754.0 jit_solution(5413852684494892107)
XLA Ops:
  18.9 8.1 %scatter_custom_fusion = s32[2049]{0:T(1024)S(1)} fusion(s32[2048]{0:T(1024)S(1)} %bitcast.361, s32[2048]{0:T(1024)S(1)} %iota.29, s32[]{:T(128)} %constant.146.clone.1), kind=kCustom, calls=%fused_computation.217 | custom fusion | bytes 8200 | tf_op jit(solution)/shard_map/scatter | solution.py:340
  28.3 81.6 %attention_forward.1 = (bf16[4,256,768]{2,1,0:T(8,128)(2,1)}, bf16[8,96,768]{2,1,0:T(8,128)(2,1)}, bf16[3,1024,64]{2,1,0:T(8,128)(2,1)}, bf16[3,1024,64]{2,1,0:T...) custom-call(bf16[256,768]{1,0:T(8,128)(2,1)} %x_ref.1, ...), custom_call_target="tpu_custom_call" | custom-call | tf_op jit(solution)/shard_map/attention_forward/pallas_call | solution.py:290
  109.9 10.1 %gather_fusion = bf16[2048,768]{1,0:T(8,128)(2,1)S(1)} fusion(bf16[1024,768]{1,0:T(8,128)(2,1)} %bitcast.282, s32[2048]{0:T(1024)S(1)} %get-tuple-element.400), kind=kCustom, calls=%fused_computation | custom fusion | bytes 6299648 | tf_op jit(solution)/shard_map/gather | solution.py:488
  120.0 75.4 %all_to_all.38 = bf16[8,256,768]{2,1,0:T(8,128)(2,1)S(1)} all-to-all(bf16[8,256,768]{2,1,0:T(8,128)(2,1)S(1)} %bitcast.291), channel_id=1, replica_groups={{0,4,8,12,16,20,24,28},{1,5,9,13,17,21,25,29},{2,6,10,14,18,22,26,30},{..., dimensions={0} | all-to-all | bytes 6291456 | tf_op jit(solution)/shard_map/all_to_all | solution.py:374
  198.9 4.4 convolution_convert_fusion
  203.3 4.6 all-to-all-start.1
  210.0 16.8 %gather_fusion.3 = f32[2048]{0:T(1024)S(1)} fusion(f32[1024,12]{0,1:T(8,128)S(1)} %convolution_add_fusion.1, s32[2048]{0:T(1024)S(1)} %reshape.323), kind=kCustom, calls=%fused_computation.3 | custom fusion | bytes 32768 | tf_op jit(solution)/shard_map/jit(take_along_axis)/gather | solution.py:482
  228.1 11.8 %gather_fusion.1 = f32[2048]{0:T(1024)S(1)} fusion(f32[2049]{0:T(1024)S(1)} %pad_maximum_fusion.13, s32[2048]{0:T(1024)S(1)} %copy-done.28), kind=kCustom, calls=%fused_computation.1 | custom fusion | bytes 24576 | tf_op jit(solution)/shard_map/gather | solution.py:485
  240.0 10.1 %gather_fusion.2 = bf16[2048,768]{1,0:T(8,128)(2,1)S(1)} fusion(bf16[1024,768]{1,0:T(8,128)(2,1)} %all-gather.3.cloned.1.call-done, s32[2048]{0:T(1024)S(1)} %copy-done.27), kind=kCustom, calls=%fused_computation.2 | custom fusion | bytes 6299648 | tf_op jit(solution)/shard_map/gather | solution.py:524
  250.0 27.7 %all-to-all-done.1 = bf16[8,256,768]{2,1,0:T(8,128)(2,1)} async-done(((bf16[8,256,768]{2,1,0:T(8,128)(2,1)}), bf16[8,256,768]{2,1,0:T(8,128)(2,1)}, u32[]{:S(2)}, u32[]{:S(2)}) %all-to-all-start.1) | async-done | bytes 3145760 | tf_op jit(solution)/shard_map/all_to_all | solution.py:374
  277.7 5.0 fusion.36
  282.7 74.5 %all_to_all.39 = bf16[8,256,768]{2,1,0:T(8,128)(2,1)S(1)} all-to-all(bf16[8,256,768]{2,1,0:T(8,128)(2,1)S(1)} %get-tuple-element.402), channel_id=1, replica_groups={{0,4,8,12,16,20,24,28},{1,5,9,13,17,21,25,29},{2,6,10,14,18,22,26,30},{..., dimensions={0} | all-to-all | bytes 6291456 | tf_op jit(solution)/shard_map/all_to_all | solution.py:374
  357.3 6.7 fusion.54
  364.0 5.0 bitcast_convert_fusion
  372.7 14.8 %scatter_custom_fusion.3 = f32[2049]{0:T(1024)S(1)} fusion(s32[2048]{0:T(1024)} %get-tuple-element.398, f32[2048]{0:T(1024)S(1)} %bitcast.360, f32[]{:T(128)} %constant.145.clone.1), kind=kCustom, calls=%fused_computation.215 | custom fusion | flops 2048 | bytes 8708 | tf_op jit(solution)/shard_map/scatter-add | solution.py:554
  388.8 16.5 %scatter_custom_fusion.1 = f32[1024,768]{1,0:T(8,128)} fusion(s32[2048]{0:T(1024)} %get-tuple-element.401, f32[2048,768]{1,0:T(8,128)} %bitcast.295, f32[]{:T(128)} %constant.145.clone.1), kind=kCustom, calls=%fused_computation.95 | custom fusion | flops 1572864 | bytes 3146240 | tf_op jit(solution)/shard_map/scatter-add | solution.py:500
  408.6 34.4 %all-to-all-done.3 = bf16[8,256,768]{2,1,0:T(8,128)(2,1)S(1)} async-done(((bf16[8,256,768]{2,1,0:T(8,128)(2,1)}), bf16[8,256,768]{2,1,0:T(8,128)(2,1)S(1)}, u32[]{:S(2)}, u32[]{:S(2)}) %all-to-all-start.3) | async-done | bytes 3145760 | tf_op jit(solution)/shard_map/all_to_all | solution.py:374
  442.9 16.2 %scatter_custom_fusion.2 = f32[1024,768]{1,0:T(8,128)} fusion(s32[2048]{0:T(1024)} %get-tuple-element.401, bf16[2048,768]{1,0:T(8,128)(2,1)S(1)} %bitcast.290, f32[]{:T(128)} %constant.145.clone.1), kind=kCustom, calls=%fused_computation.50 | custom fusion | flops 3145728 | bytes 6291968 | tf_op jit(solution)/shard_map/scatter-add | solution.py:549
  467.8 28.3 %reduce-scatter.13.cloned.1.call-done = f32[256,768]{1,0:T(8,128)} async-done(((f32[1024,768]{1,0:T(8,128)}), f32[256,768]{1,0:T(8,128)}) %reduce-scatter.13.cloned.1.call-update) | async-done | bytes 786448 | tf_op jit(solution)/shard_map/reduce_scatter | solution.py:558
  509.4 10.8 %all-gather.5.cloned.1.call-done = bf16[1024,768]{1,0:T(8,128)(2,1)} async-done(((bf16[256,768]{1,0:T(8,128)(2,1)}), bf16[1024,768]{1,0:T(8,128)(2,1)}) %all-gather.5.cloned.1.call-update) | async-done | bytes 1572880 | tf_op jit(solution)/shard_map/all_gather | solution.py:608
  528.6 52.4 %while.17 = (s32[]{:T(128)}, f32[2,512,3,64]{1,0,3,2:T(2,128)}, f32[2,1024,3,64]{1,3,2,0:T(8,128)}, f32[2,1024,3,64]{1,3,2,0:T(8,128)}, s32[2]{0:T(128)S(1)}, /*...) while((s32[]{:T(128)}, f32[2,512,3,64]{1,0,3,2:T(2,128)}, ...), condition=%wide.region_29.30_spmd.clone, body=%wide.region_27.29_spmd.clone.sunk | while | flops 1031044096 | bytes 67418504 | solution.py:642
  547.0 8.1 %dynamic_update_slice.30 = f32[2,512,3,64]{1,0,3,2:T(2,128)} dynamic-update-slice(f32[2,512,3,64]{1,0,3,2:T(2,128)} %get-tuple-element.499, f32[1,512,3,64]{1,0,3,2:T(1,128)S(1)} %copy.228, s32[]{:T(128)S(6)} %copy.236, s32[]{:T(128)} %constant.149.clone.1..sunk, s32[]{:T(128)} %constant.149.clone.1..sunk, s32[]{:T(128)} %constant.149.clone.1..sunk) | dynamic-update-slice | bytes 786436 | tf_op jit(solution)/shard_map/while/body/jit(dynamic_update_index_in_dim)/dynamic_update_slice | solution.py:642
  573.0 8.1 %dynamic_update_slice.30 = f32[2,512,3,64]{1,0,3,2:T(2,128)} dynamic-update-slice(f32[2,512,3,64]{1,0,3,2:T(2,128)} %get-tuple-element.499, f32[1,512,3,64]{1,0,3,2:T(1,128)S(1)} %copy.228, s32[]{:T(128)S(6)} %copy.236, s32[]{:T(128)} %constant.149.clone.1..sunk, s32[]{:T(128)} %constant.149.clone.1..sunk, s32[]{:T(128)} %constant.149.clone.1..sunk) | dynamic-update-slice | bytes 786436 | tf_op jit(solution)/shard_map/while/body/jit(dynamic_update_index_in_dim)/dynamic_update_slice | solution.py:642
  591.1 7.6 %fusion.63 = bf16[1,512,768]{2,1,0:T(8,128)(2,1)} fusion(bf16[2048,768]{1,0:T(8,128)(2,1)} %bitcast.299, f32[2,2048,512]{1,2,0:T(8,128)} %copy-done.39), kind=kOutput, calls=%fused_computation.99 | convolution fusion | flops 1617297408 | bytes 12320768 | tf_op jit(solution)/shard_map/cf,cd->fd/dot_general | solution.py:528
  602.9 6.3 reduce.22
  612.5 5.5 all-to-all-start.5
  618.0 7.8 %fusion.59 = bf16[1,2,768,512]{2,3,1,0:T(8,128)(2,1)} fusion(bf16[2048,768,1]{1,0,2:T(8,128)(2,1)} %bitcast.297, bf16[1,2048,512]{1,2,0:T(8,128)(2,1)} %copy-done.41, bf16[1,2048,512]{1,2,0:T(8,128)(2,1)} %copy-done.40), kind=kOutput, calls=%fused_computation.97 | convolution fusion | flops 3224109056 | bytes 8912896 | tf_op jit(solution)/shard_map/cd,kcf->kdf/dot_general | solution.py:538
  625.8 4.9 copy.186
  630.7 7.9 %all-to-all-done.5 = bf16[8,2,24576]{2,1,0:T(2,128)(2,1)S(1)} async-done(((bf16[8,2,24576]{2,1,0:T(2,128)(2,1)}), bf16[8,2,24576]{2,1,0:T(2,128)(2,1)S(1)}, u32[]{:S(2)}, u32[]{:S(2)}) %all-to-all-start.5) | async-done | bytes 786464 | tf_op jit(solution)/shard_map/all_to_all | solution.py:392
  643.2 4.6 fusion.100
  657.0 41.4 %all-to-all-done.4 = bf16[1,2,768,512]{3,1,0,2:T(2,128)(2,1)S(1)} async-done(((bf16[1,2,768,512]{3,1,0,2:T(2,128)(2,1)}), bf16[1,2,768,512]{3,1,0,2:T(2,128)(2,1)S(1)}, u32[]{:S(2)}, u32[]{:S(2)}) %all-to-all-start.4) | async-done | bytes 1572896 | tf_op jit(solution)/shard_map/all_to_all | solution.py:392
  704.2 40.4 %all-reduce = (f32[768]{0:T(1024)}, f32[768]{0:T(1024)}, f32[768,12]{0,1:T(8,128)}, f32[12,12]{1,0:T(8,128)}, f32[768,4]{0,1:T(4,128)}, /*index=5*/f32[2,768]{1,0:T(2,128)}) all-reduce(f32[768]{0:T(1024)S(1)} %get-tuple-element.333, f32[768]{0:T(1024)S(1)} %get-tuple-element.331, ...), channel_id=1, replica_groups=mesh['dp'=8,'mp'=4] {'dp','mp'}, use_global_device_ids=true, to_apply=%region_37.38 | all-reduce | flops 15504 | bytes 124032 | tf_op jit(solution)/shard_map/psum | solution.py:680
  (245 shorter events, 126.6 us)
Async XLA Ops:
  7.2 202.0 %copy-start = (f32[1024,12]{0,1:T(8,128)S(1)}, f32[1024,12]{0,1:T(8,128)}, u32[]{:S(2)}) copy-start(f32[1024,12]{0,1:T(8,128)} %param.31) | copy-start | bytes 147460
  27.6 92.4 %copy-start.26 = (s32[2048]{0:T(1024)}, s32[2048]{0:T(1024)S(1)}, u32[]{:S(2)}) copy-start(s32[2048]{0:T(1024)S(1)} %get-tuple-element.400) | copy-start | bytes 24580
  120.0 75.4 %copy-start.35 = (bf16[2,768,512]{2,1,0:T(8,128)(2,1)S(1)}, bf16[2,768,512]{2,1,0:T(8,128)(2,1)}, u32[]{:S(2)}) copy-start(bf16[2,768,512]{2,1,0:T(8,128)(2,1)} %get-tuple-element.165) | copy-start | bytes 4718596
  203.3 5.4 copy-start.20
  203.3 5.9 copy-start.30
  203.3 6.2 copy-start.1
  203.3 6.2 copy-start.24
  203.3 74.4 %all-to-all-start.1 = ((bf16[8,256,768]{2,1,0:T(8,128)(2,1)}), bf16[8,256,768]{2,1,0:T(8,128)(2,1)}, u32[]{:S(2)}, u32[]{:S(2)}) async-start(bf16[8,256,768]{2,1,0:T(8,128)(2,1)} %bitcast.300), calls=%async_computation.1 | async-start | bytes 6291456 | tf_op jit(solution)/shard_map/all_to_all | solution.py:374
  207.9 32.0 %all-gather.3.cloned.1.call-start = ((), (), s32[]{:S(2)}) async-start(), calls=%async_computation.13 | async-start | bytes 1966080 | tf_op jit(solution)/shard_map/all_gather | solution.py:523
  210.0 17.5 %copy-start.21 = (s32[1024,2]{0,1:T(2,128)S(1)}, s32[1024,2]{0,1:T(2,128)}, u32[]{:S(2)}) copy-start(s32[1024,2]{0,1:T(2,128)} %param.32) | copy-start | bytes 24580
  210.0 18.1 %copy-start.28 = (s32[2048]{0:T(1024)S(1)}, s32[2048]{0:T(1024)}, u32[]{:S(2)}) copy-start(s32[2048]{0:T(1024)} %get-tuple-element.399) | copy-start | bytes 24580
  228.1 11.8 %copy-start.27 = (s32[2048]{0:T(1024)S(1)}, s32[2048]{0:T(1024)}, u32[]{:S(2)}) copy-start(s32[2048]{0:T(1024)} %copy-done.26) | copy-start | bytes 24580
  282.7 74.6 %copy-start.38 = (bf16[768,512]{1,0:T(8,128)(2,1)S(1)}, bf16[768,512]{1,0:T(8,128)(2,1)}, u32[]{:S(2)}) copy-start(bf16[768,512]{1,0:T(8,128)(2,1)} %get-tuple-element.167) | copy-start | bytes 2359300
  357.2 6.7 copy-start.11
  357.2 6.7 copy-start.36
  368.9 74.0 %all-to-all-start.3 = ((bf16[8,256,768]{2,1,0:T(8,128)(2,1)}), bf16[8,256,768]{2,1,0:T(8,128)(2,1)S(1)}, u32[]{:S(2)}, u32[]{:S(2)}) async-start(bf16[8,256,768]{2,1,0:T(8,128)(2,1)} %bitcast.301), calls=%async_computation.4 | async-start | bytes 6291456 | tf_op jit(solution)/shard_map/all_to_all | solution.py:374
  372.6 90.0 %reduce-scatter.19.cloned.1.call-start = ((), (), s32[]{:S(2)}) async-start(), calls=%async_computation.18 | async-start | bytes 655360
  388.8 76.4 %reduce-scatter.11.cloned.1.call-start = ((), (), s32[]{:S(2)}) async-start(), calls=%async_computation.12 | async-start | bytes 1966080 | tf_op jit(solution)/shard_map/reduce_scatter | solution.py:501
  408.5 87.5 %reduce-scatter.13.cloned.1.call-start = ((), (), s32[]{:S(2)}) async-start(), calls=%async_computation.14 | async-start | bytes 3932160 | tf_op jit(solution)/shard_map/reduce_scatter | solution.py:558
  459.2 6.0 copy-start.3
  459.2 61.0 %all-gather.5.cloned.1.call-start = ((), (), s32[]{:S(2)}) async-start(), calls=%async_computation.15 | async-start | bytes 1966080 | tf_op jit(solution)/shard_map/all_gather | solution.py:608
  496.1 5.9 copy-start.16
  500.5 200.7 %reduce-scatter.21.cloned.1.call-start = ((), (), s32[]{:S(2)}) async-start(), calls=%async_computation.19 | async-start | bytes 884736
  528.6 174.2 %reduce-scatter.15.cloned.1.call-start = ((), (), s32[]{:S(2)}) async-start(), calls=%async_computation.16 | async-start | bytes 1966080 | tf_op jit(solution)/shard_map/reduce_scatter | solution.py:669
  581.0 5.9 copy-start.22
  581.0 5.9 copy-start.23
  612.5 26.1 %all-to-all-start.5 = ((bf16[8,2,24576]{2,1,0:T(2,128)(2,1)}), bf16[8,2,24576]{2,1,0:T(2,128)(2,1)S(1)}, u32[]{:S(2)}, u32[]{:S(2)}) async-start(bf16[8,2,24576]{2,1,0:T(2,128)(2,1)} %reshape.397), calls=%async_computation.9 | async-start | bytes 1572864 | tf_op jit(solution)/shard_map/all_to_all | solution.py:392
  639.5 59.0 %all-to-all-start.4 = ((bf16[1,2,768,512]{3,1,0,2:T(2,128)(2,1)}), bf16[1,2,768,512]{3,1,0,2:T(2,128)(2,1)S(1)}, u32[]{:S(2)}, u32[]{:S(2)}) async-start(bf16[1,2,768,512]{3,1,0,2:T(2,128)(2,1)} %copy.186), calls=%async_computation.8 | async-start | bytes 3145728 | tf_op jit(solution)/shard_map/all_to_all | solution.py:392
  643.1 103.8 %reduce-scatter.17.cloned.1.call-start = ((), (), s32[]{:S(2)}) async-start(), calls=%async_computation.17 | async-start | bytes 2654208 | tf_op jit(solution)/shard_map/reduce_scatter | solution.py:675
  699.2 45.5 %copy-start.4 = (f32[256,768]{1,0:T(8,128)S(1)}, f32[256,768]{1,0:T(8,128)}, u32[]{:S(2)}) copy-start(f32[256,768]{1,0:T(8,128)} %get-tuple-element.164) | copy-start | bytes 2359300
  699.2 45.5 %copy-start.6 = (bf16[256,768]{1,0:T(8,128)(2,1)S(1)}, bf16[256,768]{1,0:T(8,128)(2,1)}, u32[]{:S(2)}) copy-start(bf16[256,768]{1,0:T(8,128)(2,1)} %param.33) | copy-start | bytes 1179652
  699.2 45.4 %copy-start.8 = (f32[256,768]{1,0:T(8,128)S(1)}, f32[256,768]{1,0:T(8,128)}, u32[]{:S(2)}) copy-start(f32[256,768]{1,0:T(8,128)} %copy-done.7) | copy-start | bytes 2359300
  (24 other events, 53.5 us)
Sparse Core Ops, SparseCore 0:
  210.3 20.0 all-gather.2
  388.9 22.6 reduce-scatter.18
  414.8 28.1 reduce-scatter.10
  459.3 36.6 reduce-scatter.12
  500.6 19.6 all-gather.4
  528.7 62.4 reduce-scatter.20
  593.7 27.1 reduce-scatter.14
  648.4 86.7 reduce-scatter.16

commit v3 on v2

v3 whole, which is shorter than its diff:
```python
import functools
import numpy as np
import jax
import jax.numpy as jnp
from jax import lax
from jax.sharding import PartitionSpec as P
from jax.experimental import pallas as pl
from jax.experimental.pallas import tpu as pltpu

HD = 64
NFFN = 8
NEXP = 12
SEQ = 1024
CAP = 256
MP = 4
QUARTER = CAP // MP

epsilon = 1e-06
rope_base = 10000.0
highest = lax.Precision.HIGHEST
f32 = jnp.float32
bf16 = jnp.bfloat16
MESH = pl.DeviceIdType.MESH
VM = pl.BlockSpec(memory_space=pltpu.VMEM)
HB = pl.BlockSpec(memory_space=pl.ANY)
NT = (((1,), (1,)), ((), ()))
TN = (((0,), (0,)), ((), ()))


def flip(index, distance):
    out = index
    bit = 1
    while bit <= distance:
        if distance & bit:
            out = out + bit - 2 * bit * ((index // bit) % 2)
        bit *= 2
    return out


def dotf(a, b, dims=None):
    if dims is None:
        return jnp.dot(a, b, preferred_element_type=f32)
    return lax.dot_general(a, b, dims, preferred_element_type=f32)


def remote(src, dst, send, recv, **where):
    return pltpu.make_async_remote_copy(
        src_ref=src, dst_ref=dst, send_sem=send, recv_sem=recv, device_id=where, device_id_type=MESH
    )


def greet(mp_me, near, base):
    barrier = pltpu.get_barrier_semaphore()
    for k in range(1, MP):
        pl.semaphore_signal(barrier, inc=1, device_id={"mp": flip(mp_me, k)}, device_id_type=MESH)
    for k in range(1, NFFN):
        pl.semaphore_signal(
            barrier, inc=1, device_id={"dp": base + flip(near, k)}, device_id_type=MESH
        )
    pl.semaphore_wait(barrier, MP - 1 + NFFN - 1)


def rope_constants():
    half = HD // 2
    positions = np.arange(SEQ, dtype=np.float32)
    frequency = (rope_base ** (-np.arange(half, dtype=np.float32) / half)).astype(np.float32)
    angles = (positions[:, None] * frequency[None, :]).astype(np.float32)
    cosine, sine = np.cos(angles), np.sin(angles)
    return (
        np.concatenate([cosine, cosine], axis=1),
        np.concatenate([-sine, sine], axis=1),
    )


def swap_halves(x):
    half = HD // 2
    return jnp.concatenate([x[:, half:], x[:, :half]], axis=1)


class Gather:
    def __init__(self, ref, mp_me, send, recv):
        self.me, self.core, self.chip = mp_me, flip(mp_me, 1), flip(mp_me, 2)
        own = ref.at[mp_me]
        far = ref.at[self.chip]
        self.to_chip = remote(own, own, send.at[0], recv.at[0], mp=self.chip)
        self.to_core = remote(own, own, send.at[1], recv.at[1], mp=self.core)
        self.relay = remote(far, far, send.at[2], recv.at[2], mp=self.core)

    def start(self):
        self.to_chip.start()
        self.to_core.start()

    def forward(self):
        self.to_chip.wait_recv()
        self.relay.start()

    def finish(self):
        self.to_core.wait_recv()
        self.relay.wait_recv()
        self.to_chip.wait_send()
        self.to_core.wait_send()
        self.relay.wait_send()


def attention_kernel(
    inside,
    x_ref, gain1_ref, gain2_ref, cos_ref, sin_ref, wshard_ref, win_shard, wout_shard,
    rows1_ref, w_ref, q_ref, k_ref, v_ref, mixed_ref, lse_ref, hidden_ref, rows2_ref, *rest,
):
    if inside:
        win_ref, wout_ref, *rest = rest
    (part_ref, core_in, chip_out, chip_in, core_out,
     sends, recvs, wsend, wrecv, esend, erecv, local) = rest
    mp_me = lax.axis_index("mp")
    dp_me = lax.axis_index("dp")
    near = lax.rem(dp_me, NFFN)
    base = dp_me - near
    core, chip = flip(mp_me, 1), flip(mp_me, 2)
    rows = x_ref.shape[0]
    depth = w_ref.shape[1]
    greet(mp_me, near, base)

    tokens = x_ref[...].astype(f32)
    scale = lax.rsqrt(jnp.mean(tokens * tokens, axis=-1, keepdims=True) + epsilon)
    rows1_ref[mp_me] = (tokens * scale * gain1_ref[...]).astype(bf16)
    gather1 = Gather(rows1_ref, mp_me, sends.at[pl.ds(0, 3)], recvs.at[pl.ds(0, 3)])
    gather1.start()

    if inside:
        w_ref[near] = wshard_ref[...]
        own = w_ref.at[near]
        along = [
            remote(own, own, wsend.at[k], wrecv.at[k], dp=base + flip(near, k)) for k in (2, 4, 6)
        ]
        for copy in along:
            copy.start()
        mate = base + flip(near, 1)
        across = [remote(own, own, wsend.at[0], wrecv.at[0], dp=mate)]
        across[0].start()
        for k, copy in zip((2, 4, 6), along):
            copy.wait_recv()
            block = w_ref.at[flip(near, k)]
            onward = remote(block, block, wsend.at[k + 1], wrecv.at[k + 1], dp=mate)
            onward.start()
            across.append(onward)
        gather1.forward()
        for copy in across:
            copy.wait_recv()
        for copy in along + across:
            copy.wait_send()
        experts = []
        din = win_shard.shape[2]
        place = pl.ds(pl.multiple_of(near * din, din), din)
        for k in (6, 4, 7, 5, 2, 3, 1):
            peer = flip(near, k)
            for i, (src, dst) in enumerate(
                [(win_shard.at[peer], win_ref.at[:, place]), (wout_shard.at[peer], wout_ref.at[place])]
            ):
                experts.append(
                    remote(src, dst, esend.at[i, k], erecv.at[i, k], dp=base + peer)
                )
        for copy in experts:
            copy.start()
        mine = [
            pltpu.make_async_copy(win_shard.at[near], win_ref.at[:, place], local.at[0]),
            pltpu.make_async_copy(wout_shard.at[near], wout_ref.at[place], local.at[1]),
        ]
        for copy in mine:
            copy.start()
    else:
        w_ref[...] = wshard_ref[...]
        gather1.forward()
    gather1.finish()

    width = x_ref.shape[1]
    w_all = w_ref[...].reshape(width, w_ref.shape[2])
    heads = q_ref.shape[0]
    cols = heads * HD

    def project(i, carry):
        at = pl.ds(pl.multiple_of(i * rows, rows), rows)
        joint = dotf(rows1_ref[i], w_all[:, : 3 * cols])
        cosine, sine = cos_ref[at], sin_ref[at]
        for h in range(heads):
            query = joint[:, h * HD : (h + 1) * HD]
            key = joint[:, cols + h * HD : cols + (h + 1) * HD]
            q_ref[h, at] = (query * cosine + swap_halves(query) * sine).astype(bf16)
            k_ref[h, at] = (key * cosine + swap_halves(key) * sine).astype(bf16)
            v_ref[h, at] = joint[:, 2 * cols + h * HD : 2 * cols + (h + 1) * HD].astype(bf16)
        return carry

    lax.fori_loop(0, MP, project, 0)
    out_weight = w_all[:, 3 * cols :]

    to_core = [
        remote(core_out.at[j], core_in.at[j], sends.at[3 + j], recvs.at[3 + j], mp=core)
        for j in range(2)
    ]
    to_chip = remote(chip_out, chip_in, sends.at[5], recvs.at[5], mp=chip)

    def attend(step, carry):
        block = flip(mp_me, 3)
        block = jnp.where(step == 1, core, jnp.where(step == 2, chip, jnp.where(step == 3, mp_me, block)))
        at = pl.ds(pl.multiple_of(block * rows, rows), rows)
        row_ids = block * rows + lax.broadcasted_iota(jnp.int32, (rows, SEQ), 0)
        seen = row_ids >= lax.broadcasted_iota(jnp.int32, (rows, SEQ), 1)
        for h in range(heads):
            scores = dotf(q_ref[h, at], k_ref[h], NT) * HD**-0.5
            scores = jnp.where(seen, scores, -jnp.inf)
            peak = jnp.max(scores, axis=-1, keepdims=True)
            exponent = jnp.exp(scores - peak)
            total = jnp.sum(exponent, axis=-1, keepdims=True)
            probs = (exponent * (1.0 / total)).astype(bf16)
            mixed_ref[at, h * HD : (h + 1) * HD] = dotf(probs, v_ref[h]).astype(bf16)
            lse_ref[at, h : h + 1] = peak + jnp.log(total)
        part = dotf(mixed_ref[at], out_weight, NT)

        @pl.when(step == 0)
        def _():
            core_out[0] = part.astype(bf16)
            to_core[0].start()

        @pl.when(step == 1)
        def _():
            core_out[1] = part.astype(bf16)
            to_core[1].start()

        @pl.when(step == 2)
        def _():
            to_core[0].wait_recv()
            chip_out[...] = (part + core_in[0].astype(f32)).astype(bf16)
            to_chip.start()

        @pl.when(step == 3)
        def _():
            part_ref[...] = part

        return carry

    lax.fori_loop(0, MP, attend, 0)
    to_core[1].wait_recv()
    partial = part_ref[...] + core_in[1].astype(f32)
    to_chip.wait_recv()
    hidden = x_ref[...].astype(f32) + (partial + chip_in[...].astype(f32))
    hidden_ref[...] = hidden
    scale2 = lax.rsqrt(jnp.mean(hidden * hidden, axis=-1, keepdims=True) + epsilon)
    rows2_ref[mp_me] = (hidden * scale2 * gain2_ref[...]).astype(bf16)
    gather2 = Gather(rows2_ref, mp_me, sends.at[pl.ds(6, 3)], recvs.at[pl.ds(6, 3)])
    gather2.start()
    for copy in to_core + [to_chip]:
        copy.wait_send()
    gather2.forward()
    gather2.finish()
    if inside:
        for copy in experts:
            copy.wait_recv()
        for copy in experts:
            copy.wait_send()
        for copy in mine:
            copy.wait()


def attention(x, gain1, gain2, wshard, win, wout, groups):
    rows, width = x.shape
    cos, sin = rope_constants()
    inside = groups == 1
    cols = wshard.shape[-1]
    depth = width // NFFN
    hidden_cols = win.shape[-1]
    heads = cols // 4 // HD
    sd = jax.ShapeDtypeStruct
    outs = [
        sd((MP, rows, width), bf16),
        sd((NFFN, depth, cols), bf16),
        sd((heads, SEQ, HD), bf16),
        sd((heads, SEQ, HD), bf16),
        sd((heads, SEQ, HD), bf16),
        sd((SEQ, heads * HD), bf16),
        sd((SEQ, 128), f32),
        sd((rows, width), f32),
        sd((MP, rows, width), bf16),
    ]
    specs = [VM] * len(outs)
    if inside:
        outs += [sd((2, width, hidden_cols), bf16), sd((width, hidden_cols), bf16)]
        specs += [HB, HB]
    else:
        wshard = wshard.reshape(NFFN, depth, cols)
    dma = pltpu.SemaphoreType.DMA
    return pl.pallas_call(
        functools.partial(attention_kernel, inside),
        out_shape=outs,
        in_specs=[VM] * 6 + [HB, HB],
        out_specs=specs,
        scratch_shapes=[
            pltpu.VMEM((rows, width), f32),
            pltpu.VMEM((2, rows, width), bf16),
            pltpu.VMEM((rows, width), bf16),
            pltpu.VMEM((rows, width), bf16),
            pltpu.VMEM((2, rows, width), bf16),
            dma((9,)), dma((9,)),
            dma((8,)), dma((8,)),
            dma((2, 8)), dma((2, 8)),
            dma((2,)),
        ],
        compiler_params=pltpu.CompilerParams(
            collective_id=0, has_side_effects=True, vmem_limit_bytes=56 * 2**20
        ),
        name="attention_forward",
    )(x, gain1, gain2, jnp.asarray(cos), jnp.asarray(sin), wshard, win, wout)


def pack3(value):
    high = value.astype(bf16).astype(f32)
    rest = value - high
    mid = rest.astype(bf16).astype(f32)
    low = (rest - mid).astype(bf16).astype(f32)
    lane = lax.broadcasted_iota(jnp.int32, (value.shape[0], 128), 1)
    return jnp.where(
        lane == 0, high, jnp.where(lane == 1, mid, jnp.where(lane == 2, low, 0.0))
    ).astype(bf16)


def unpack3(parts):
    return jnp.sum(parts.astype(f32), axis=-1, keepdims=True)


def exact(left, right, dims=None):
    high = left.astype(bf16)
    rest = left - high.astype(f32)
    mid = rest.astype(bf16)
    low = (rest - mid.astype(f32)).astype(bf16)
    return dotf(high, right, dims) + (dotf(mid, right, dims) + dotf(low, right, dims))


class Scatter:
    def __init__(self, mp_me, core_out, core_in, chip_out, chip_in, send, recv):
        self.me, self.core, self.chip = mp_me, flip(mp_me, 1), flip(mp_me, 2)
        self.core_out, self.core_in = core_out, core_in
        self.chip_out, self.chip_in = chip_out, chip_in
        self.to_core = [
            remote(core_out.at[j], core_in.at[j], send.at[j], recv.at[j], mp=self.core)
            for j in range(2)
        ]
        self.to_chip = remote(chip_out, chip_in, send.at[2], recv.at[2], mp=self.chip)

    def run(self, blocks):
        for j, block in enumerate((flip(self.me, 3), self.core)):
            self.core_out[j] = blocks(block).astype(bf16)
            self.to_core[j].start()
        term = blocks(self.chip)
        self.to_core[0].wait_recv()
        self.chip_out[...] = (term + self.core_in[0].astype(f32)).astype(bf16)
        self.to_chip.start()
        term = blocks(self.me)
        self.to_core[1].wait_recv()
        term = term + self.core_in[1].astype(f32)
        self.to_chip.wait_recv()
        return term + self.chip_in[...].astype(f32)

    def drain(self):
        for copy in self.to_core + [self.to_chip]:
            copy.wait_send()


def expert_kernel(
    rows2_ref, hidden_ref, cot_ref, gain2_ref, router_ref, mix_ref, values_ref, prior_ref,
    carry_ref, previous_ref, routes_ref, routes_own_ref, prior_own_ref, win_ref, wout_ref,
    residual_ref, hgrad_ref, agrad_ref, lgrad_ref, small_ref, carry_grad_ref, pick_ref, gate_ref,
    outq_ref, dwin_ref, dwout_ref,
    cot_all, place_ref, gates_ref, msgx, msgc, xs, cs, pre_ref, units_ref, pgrad_ref,
    ocore_out, ocore_in, ochip_out, ochip_in,
    gpart_ref, gcore_out, gcore_in, gchip_out, gchip_in, gret,
    score_out, score_in, ncore_out, ncore_in, nchip_out, nchip_in,
    csend, crecv, xsend, xrecv, dsend, drecv, xgs, xgr, cgs, cgr, osend, orecv,
    gsend, grecv, rsend, rrecv, ssend, srecv, nsend, nrecv,
):
    mp_me = lax.axis_index("mp")
    dp_me = lax.axis_index("dp")
    near = lax.rem(dp_me, NFFN)
    base = dp_me - near
    core, chip = flip(mp_me, 1), flip(mp_me, 2)
    far = flip(mp_me, 3)
    rows, width = cot_ref.shape
    everyone = MP * rows
    greet(mp_me, near, base)
    cot_all[mp_me] = cot_ref[...]
    gather = Gather(cot_all, mp_me, csend, crecv)
    gather.start()

    tokens = rows2_ref[...].reshape(everyone, width)
    logits = dotf(router_ref[...], tokens, NT) + prior_ref[...]
    ids = lax.broadcasted_iota(jnp.int32, (16, everyone), 0)
    chosen = (ids == routes_ref[0:1]) | (ids == routes_ref[1:2])
    masked = jnp.where(chosen, logits, -jnp.inf)
    exponent = jnp.exp(masked - jnp.max(masked, axis=0, keepdims=True))
    gates_ref[...] = exponent / jnp.sum(exponent, axis=0, keepdims=True)
    earlier = lax.broadcasted_iota(jnp.int32, (everyone, everyone), 0) < lax.broadcasted_iota(
        jnp.int32, (everyone, everyone), 1
    )
    counts = dotf(
        jnp.where(chosen, 1.0, 0.0).astype(bf16), jnp.where(earlier, 1.0, 0.0).astype(bf16)
    )
    place_ref[...] = jnp.where(chosen, counts, -1.0)
    wanted = (lax.broadcasted_iota(jnp.int32, (QUARTER, everyone), 0) + QUARTER * mp_me).astype(f32)

    def x_copy(k):
        return remote(
            msgx.at[lax.rem(near + k, NFFN)], xs.at[near, mp_me], xsend.at[k], xrecv.at[k],
            dp=base + lax.rem(near + k, NFFN),
        )

    def c_copy(k):
        return remote(
            msgc.at[lax.rem(near + k, NFFN)], cs.at[near, mp_me], dsend.at[k], drecv.at[k],
            dp=base + lax.rem(near + k, NFFN),
        )

    def send_x(i, carry):
        k = lax.rem(i + 1, NFFN)
        expert = lax.rem(near + k, NFFN)
        pick = wanted == place_ref[pl.ds(expert, 1)]
        onehot = jnp.where(pick, 1.0, 0.0).astype(bf16)
        gate = jnp.sum(
            jnp.where(pick, gates_ref[pl.ds(expert, 1)], 0.0), axis=1, keepdims=True
        )
        pick_ref[expert] = onehot
        gate_ref[expert] = jnp.broadcast_to(gate, (QUARTER, 128))
        block = dotf(onehot, tokens).astype(bf16)
        extra = pack3(gate)
        msgx[expert, :, :width] = block
        msgx[expert, :, width:] = extra

        @pl.when(k > 0)
        def _():
            x_copy(k).start()

        @pl.when(k == 0)
        def _():
            xs[near, mp_me] = msgx[expert]

        return carry

    lax.fori_loop(0, NFFN, send_x, 0)
    gather.forward()
    gather.finish()

    def send_c(i, carry):
        k = lax.rem(i + 1, NFFN)
        expert = lax.rem(near + k, NFFN)
        msgc[expert] = dotf(pick_ref[expert], cot_all[...].reshape(everyone, width)).astype(bf16)

        @pl.when(k > 0)
        def _():
            c_copy(k).start()

        @pl.when(k == 0)
        def _():
            cs[near, mp_me] = msgc[expert]

        return carry

    lax.fori_loop(0, NFFN, send_c, 0)

    def source(k):
        return lax.rem(near - k + NFFN, NFFN)

    def scatter_at(k, bufs, send, recv):
        core_out, core_in, chip_out, chip_in = bufs
        slot = lax.rem(k, 3)
        return Scatter(
            mp_me, core_out.at[slot], core_in.at[k], chip_out.at[slot], chip_in.at[k],
            send.at[k], recv.at[k],
        )

    obufs = (ocore_out, ocore_in, ochip_out, ochip_in)
    gbufs = (gcore_out, gcore_in, gchip_out, gchip_in)
    hidden_cols = wout_ref.shape[1]

    def forward_step(i, carry):
        @pl.when(i < NFFN)
        def _():
            @pl.when(i > 0)
            def _():
                x_copy(i).wait_recv()

            Gather(xs.at[source(i)], mp_me, xgs.at[i], xgr.at[i]).start()

        @pl.when((i >= 1) & (i < NFFN + 1))
        def _():
            k = i - 1
            Gather(xs.at[source(k)], mp_me, xgs.at[k], xgr.at[k]).forward()

        @pl.when((i >= 2) & (i < NFFN + 2))
        def _():
            k = i - 2
            src = source(k)
            at = pl.ds(pl.multiple_of(src * CAP, CAP), CAP)
            Gather(xs.at[src], mp_me, xgs.at[k], xgr.at[k]).finish()
            x = xs[src].reshape(CAP, width + 128)[:, :width]
            gate_pre = dotf(x, win_ref[0])
            up_pre = dotf(x, win_ref[1])
            pre_ref[0, at] = gate_pre
            pre_ref[1, at] = up_pre
            units = (gate_pre * jax.nn.sigmoid(gate_pre) * up_pre).astype(bf16)
            units_ref[at] = units
            slot = lax.rem(k, 3)
            gpart_ref[slot, :, :, :width] = dotf(units, wout_ref[...], NT).reshape(
                MP, QUARTER, width
            )
            ocore_out[slot, 0] = gpart_ref[slot, far, :, :width].astype(bf16)
            ocore_out[slot, 1] = gpart_ref[slot, core, :, :width].astype(bf16)
            trip = scatter_at(k, obufs, osend, orecv)
            trip.to_core[0].start()
            trip.to_core[1].start()

        @pl.when((i >= 3) & (i < NFFN + 3))
        def _():
            k = i - 3
            trip = scatter_at(k, obufs, osend, orecv)
            trip.to_core[0].wait_recv()
            ochip_out[lax.rem(k, 3)] = (
                gpart_ref[lax.rem(k, 3), chip, :, :width] + ocore_in[k, 0].astype(f32)
            ).astype(bf16)
            trip.to_chip.start()

        @pl.when(i >= 4)
        def _():
            k = i - 4
            trip = scatter_at(k, obufs, osend, orecv)
            trip.to_core[1].wait_recv()
            trip.to_chip.wait_recv()
            outq_ref[source(k)] = (
                gpart_ref[lax.rem(k, 3), mp_me, :, :width]
                + ocore_in[k, 1].astype(f32)
                + ochip_in[k].astype(f32)
            ).astype(bf16)
            trip.drain()

        return carry

    lax.fori_loop(0, NFFN + 4, forward_step, 0)

    def g_copy(k):
        return remote(
            msgx.at[lax.rem(near + k, NFFN)], gret.at[near], rsend.at[k], rrecv.at[k], dp=base + source(k)
        )

    def seal(ref, index, total):
        ref[index + (slice(None), slice(0, width))] = total[:, :width].astype(bf16)
        ref[index + (slice(None), slice(width, None))] = pack3(unpack3(total[:, width:]))

    def backward_step(i, carry):
        @pl.when(i < NFFN)
        def _():
            @pl.when(i > 0)
            def _():
                c_copy(i).wait_recv()

            Gather(cs.at[source(i)], mp_me, cgs.at[i], cgr.at[i]).start()

        @pl.when((i >= 1) & (i < NFFN + 1))
        def _():
            k = i - 1
            Gather(cs.at[source(k)], mp_me, cgs.at[k], cgr.at[k]).forward()

        @pl.when((i >= 2) & (i < NFFN + 2))
        def _():
            k = i - 2
            src = source(k)
            at = pl.ds(pl.multiple_of(src * CAP, CAP), CAP)
            Gather(cs.at[src], mp_me, cgs.at[k], cgr.at[k]).finish()
            gate = unpack3(xs[src].reshape(CAP, width + 128)[:, width:])
            c = cs[src].reshape(CAP, width)
            gate_pre = pre_ref[0, at]
            up_pre = pre_ref[1, at]
            raw = dotf(c, wout_ref[...])
            score = jnp.sum(units_ref[at].astype(f32) * raw, axis=1, keepdims=True)
            units_grad = raw * gate
            cs[src] = (c.astype(f32) * gate).astype(bf16).reshape(MP, QUARTER, width)
            sig = jax.nn.sigmoid(gate_pre)
            gate_grad = (units_grad * up_pre * sig * (1.0 + gate_pre * (1.0 - sig))).astype(bf16)
            up_grad = (units_grad * (gate_pre * sig)).astype(bf16)
            pgrad_ref[at, :hidden_cols] = gate_grad
            pgrad_ref[at, hidden_cols:] = up_grad
            slot = lax.rem(k, 3)
            back = dotf(gate_grad, win_ref[0], NT) + dotf(up_grad, win_ref[1], NT)
            gpart_ref[slot, :, :, :width] = back.reshape(MP, QUARTER, width)
            gpart_ref[slot, :, :, width:] = pack3(score).astype(f32).reshape(MP, QUARTER, 128)
            seal(gcore_out, (slot, 0), gpart_ref[slot, far])
            seal(gcore_out, (slot, 1), gpart_ref[slot, core])
            trip = scatter_at(k, gbufs, gsend, grecv)
            trip.to_core[0].start()
            trip.to_core[1].start()

        @pl.when((i >= 3) & (i < NFFN + 3))
        def _():
            k = i - 3
            trip = scatter_at(k, gbufs, gsend, grecv)
            trip.to_core[0].wait_recv()
            seal(gchip_out, (lax.rem(k, 3),), gpart_ref[lax.rem(k, 3), chip] + gcore_in[k, 0].astype(f32))
            trip.to_chip.start()

        @pl.when(i >= 4)
        def _():
            k = i - 4
            trip = scatter_at(k, gbufs, gsend, grecv)
            trip.to_core[1].wait_recv()
            trip.to_chip.wait_recv()
            total = (
                gpart_ref[lax.rem(k, 3), mp_me]
                + gcore_in[k, 1].astype(f32)
                + gchip_in[k].astype(f32)
            )
            trip.drain()

            @pl.when(k > 0)
            def _():
                x_copy(k).wait_send()

            seal(msgx, (lax.rem(near + k, NFFN),), total)

            @pl.when(k > 0)
            def _():
                g_copy(k).start()

            @pl.when(k == 0)
            def _():
                gret[near] = msgx[near]

        return carry

    lax.fori_loop(0, NFFN + 4, backward_step, 0)

    def weights_step(j, carry):
        at = pl.ds(pl.multiple_of(j * 128, 128), 128)
        x = xs[:, :, :, at].reshape(NFFN * CAP, 128)
        both = dotf(x, pgrad_ref[...], TN)
        dwin_ref[0, at] = both[:, :hidden_cols].astype(bf16)
        dwin_ref[1, at] = both[:, hidden_cols:].astype(bf16)
        c = cs[:, :, :, at].reshape(NFFN * CAP, 128)
        dwout_ref[at] = dotf(c, units_ref[...], TN).astype(bf16)
        return carry

    lax.fori_loop(0, width // 128, weights_step, 0)

    def returned(k, carry):
        g_copy(k).wait_recv()
        return carry

    lax.fori_loop(1, NFFN, returned, 0)
    ret = gret[...].reshape(NFFN * QUARTER, width + 128)
    slots = unpack3(ret[:, width:])
    picks = pick_ref[...].reshape(NFFN * QUARTER, everyone)
    for expert in range(NFFN):
        at = slice(expert * QUARTER, (expert + 1) * QUARTER)
        row = jnp.sum(picks[at].astype(f32) * slots[at], axis=0, keepdims=True)
        for q in range(MP):
            score_out[q, expert : expert + 1] = row[:, q * rows : (q + 1) * rows]
    score_copies = [
        remote(score_out.at[flip(mp_me, k)], score_in.at[k], ssend.at[k], srecv.at[k], mp=flip(mp_me, k))
        for k in range(1, MP)
    ]
    for copy in score_copies:
        copy.start()

    def grad_block(q):
        at = pl.ds(pl.multiple_of(q * rows, rows), rows)
        return dotf(
            pick_ref[:, :, at].reshape(NFFN * QUARTER, rows), ret[:, :width], TN
        )

    trip = Scatter(mp_me, ncore_out, ncore_in, nchip_out, nchip_in, nsend, nrecv)
    normed_grad = trip.run(grad_block)

    n_bf = rows2_ref[mp_me]
    n = n_bf.astype(f32)
    cot = cot_ref[...].astype(f32)
    hidden = hidden_ref[...]
    lane = lax.broadcasted_iota(jnp.int32, (rows, 128), 1)
    own_logits = dotf(n_bf, router_ref[...], NT) + prior_own_ref[...]
    lane16 = lax.broadcasted_iota(jnp.int32, (rows, 16), 1)
    own_chosen = (lane16 == routes_own_ref[:, 0:1]) | (lane16 == routes_own_ref[:, 1:2])
    own_masked = jnp.where(own_chosen, own_logits, -jnp.inf)
    own_exp = jnp.exp(own_masked - jnp.max(own_masked, axis=1, keepdims=True))
    own_gates = own_exp / jnp.sum(own_exp, axis=1, keepdims=True)
    copy_gate = own_gates[:, NFFN + 1 : NFFN + 2]
    const_gates = [own_gates[:, NFFN + 2 : NFFN + 3], own_gates[:, NFFN + 3 : NFFN + 4]]
    mix_logits = dotf(n_bf, mix_ref[...], NT)
    with_normed = jnp.sum(cot * n, axis=1, keepdims=True)
    residual = hidden + copy_gate * n
    normed_grad = normed_grad + copy_gate * cot
    local_scores = jnp.where(lane == NFFN + 1, with_normed, 0.0)
    mix_grads = jnp.zeros((rows, 128), f32)
    for c in range(2):
        first, second = mix_logits[:, 2 * c : 2 * c + 1], mix_logits[:, 2 * c + 1 : 2 * c + 2]
        top = jnp.maximum(first, second)
        first, second = jnp.exp(first - top), jnp.exp(second - top)
        share = 1.0 / (first + second)
        first, second = first * share, second * share
        constant = values_ref[c : c + 1].astype(f32)
        with_constant = jnp.sum(cot * constant, axis=1, keepdims=True)
        gate = const_gates[c]
        residual = residual + gate * (first * n + second * constant)
        local_scores = jnp.where(
            lane == NFFN + 2 + c, first * with_normed + second * with_constant, local_scores
        )
        normed_grad = normed_grad + (first * gate) * cot
        small_ref[20 + c : 21 + c] = jnp.sum((second * gate) * cot, axis=0, keepdims=True)
        grad_first, grad_second = gate * with_normed, gate * with_constant
        mean = first * grad_first + second * grad_second
        mix_grads = jnp.where(lane == 2 * c, first * (grad_first - mean), mix_grads)
        mix_grads = jnp.where(lane == 2 * c + 1, second * (grad_second - mean), mix_grads)
    residual_ref[...] = residual

    for copy in score_copies:
        copy.wait_recv()
    ffn_scores = (score_out[mp_me] + score_in[1]) + (score_in[2] + score_in[3])
    scores = local_scores.T[:16] + jnp.concatenate([ffn_scores, jnp.zeros((8, rows), f32)], axis=0)
    own_at = pl.ds(pl.multiple_of(mp_me * rows, rows), rows)
    gates_t = gates_ref[:, own_at]
    logit_grad = gates_t * (scores - jnp.sum(gates_t * scores, axis=0, keepdims=True))
    lgrad_ref[...] = lax.dot_general(
        carry_ref[...], logit_grad, (((1,), (0,)), ((), ())),
        preferred_element_type=f32, precision=highest,
    )
    carry_grad_ref[...] = lax.dot_general(
        previous_ref[...], logit_grad, NT, preferred_element_type=f32, precision=highest
    )
    stacked = jnp.concatenate([logit_grad, mix_grads.T[:16]], axis=0)
    heads = jnp.concatenate([router_ref[...], mix_ref[...]], axis=0)
    feature_grads = exact(stacked, n_bf)
    small_ref[0:20] = feature_grads[0:20]
    normed_grad = normed_grad + exact(stacked, heads, TN)
    scale = lax.rsqrt(jnp.mean(hidden * hidden, axis=-1, keepdims=True) + epsilon)
    scaled = hidden * scale
    small_ref[22:23] = jnp.sum(normed_grad * scaled, axis=0, keepdims=True)
    small_ref[23:24] = jnp.zeros((1, width), f32)
    weighted = normed_grad * gain2_ref[...]
    hidden_grad = cot + scale * (
        weighted - scaled * jnp.mean(weighted * scaled, axis=-1, keepdims=True)
    )
    hgrad_ref[...] = hidden_grad
    agrad_ref[...] = hidden_grad.astype(bf16)

    trip.drain()
    for copy in score_copies:
        copy.wait_send()

    def drain(k, carry):
        c_copy(k).wait_send()
        g_copy(k).wait_send()
        return carry

    lax.fori_loop(1, NFFN, drain, 0)


def experts(
    rows2, hidden, cot, gain2, router_t, mix_t, values, prior_t, carry, previous_t, routes_t,
    routes_own, prior_own, win, wout,
):
    rows, width = cot.shape
    everyone = MP * rows
    cols = wout.shape[1]
    sd = jax.ShapeDtypeStruct
    vm = pltpu.VMEM
    dma = pltpu.SemaphoreType.DMA
    outs = [
        sd((rows, width), f32),
        sd((rows, width), f32),
        sd((rows, width), bf16),
        sd((16, rows), f32),
        sd((24, width), f32),
        sd((16, 16), f32),
        sd((NFFN, QUARTER, everyone), bf16),
        sd((NFFN, QUARTER, 128), f32),
        sd((NFFN, QUARTER, width), bf16),
        sd((2, width, cols), bf16),
        sd((width, cols), bf16),
    ]
    wide = width + 128
    return pl.pallas_call(
        expert_kernel,
        out_shape=outs,
        in_specs=[VM] * 15,
        out_specs=[VM] * len(outs),
        scratch_shapes=[
            vm((MP, rows, width), bf16),
            vm((16, everyone), f32),
            vm((16, everyone), f32),
            vm((NFFN, QUARTER, wide), bf16),
            vm((NFFN, QUARTER, width), bf16),
            vm((NFFN, MP, QUARTER, wide), bf16),
            vm((NFFN, MP, QUARTER, width), bf16),
            vm((2, NFFN * CAP, cols), f32),
            vm((NFFN * CAP, cols), bf16),
            vm((NFFN * CAP, 2 * cols), bf16),
            vm((3, 2, QUARTER, width), bf16),
            vm((NFFN, 2, QUARTER, width), bf16),
            vm((3, QUARTER, width), bf16),
            vm((NFFN, QUARTER, width), bf16),
            vm((3, MP, QUARTER, wide), f32),
            vm((3, 2, QUARTER, wide), bf16),
            vm((NFFN, 2, QUARTER, wide), bf16),
            vm((3, QUARTER, wide), bf16),
            vm((NFFN, QUARTER, wide), bf16),
            vm((NFFN, QUARTER, wide), bf16),
            vm((MP, 8, rows), f32),
            vm((MP, 8, rows), f32),
            vm((2, rows, width), bf16),
            vm((2, rows, width), bf16),
            vm((rows, width), bf16),
            vm((rows, width), bf16),
            dma((3,)), dma((3,)),
            dma((8,)), dma((8,)),
            dma((8,)), dma((8,)),
            dma((8, 3)), dma((8, 3)),
            dma((8, 3)), dma((8, 3)),
            dma((8, 3)), dma((8, 3)),
            dma((8, 3)), dma((8, 3)),
            dma((8,)), dma((8,)),
            dma((4,)), dma((4,)),
            dma((3,)), dma((3,)),
        ],
        compiler_params=pltpu.CompilerParams(
            collective_id=1, has_side_effects=True, vmem_limit_bytes=60 * 2**20
        ),
        name="experts",
    )(
        rows2, hidden, cot, gain2, router_t, mix_t, values, prior_t, carry, previous_t, routes_t,
        routes_own, prior_own, win, wout,
    )


def back_kernel(
    inside,
    agrad_ref, hgrad_ref, x_ref, gain1_ref, cos_ref, sin_ref, rows1_ref, w_ref, q_ref, k_ref, v_ref,
    mixed_ref, lse_ref, pick_ref, gate_ref, residual_ref, outq_ref, small_ref, carry_ref,
    dwin_ref, dwout_ref,
    output_ref, xgrad_ref, wgrad_ref, sums_ref, first_ref, *rest,
):
    if inside:
        dwin_own, dwout_own, *rest = rest
    (agrad_all, mgrad_ref, joint_ref, key_acc, value_acc, grads_ref, wsend_ref, wrecv_ref,
     ret_ref, ocore_out, ocore_in, ochip_out, ochip_in, xcore_out, xcore_in, xchip_out, xchip_in,
     sum_out, sum_in, first_mp, first_dp, first_out,
     asend, arecv, osend, orecv, esend, erecv, local, rsend, rrecv, xsend, xrecv, wsend, wrecv,
     ssend, srecv, fsend, frecv) = rest
    mp_me = lax.axis_index("mp")
    dp_me = lax.axis_index("dp")
    near = lax.rem(dp_me, NFFN)
    base = dp_me - near
    rows, width = agrad_ref.shape
    everyone = MP * rows
    heads = q_ref.shape[0]
    cols = heads * HD
    greet(mp_me, near, base)

    agrad_all[mp_me] = agrad_ref[...]
    gather = Gather(agrad_all, mp_me, asend, arecv)
    gather.start()
    returns = [
        remote(outq_ref.at[flip(near, k)], ret_ref.at[near], osend.at[k], orecv.at[k],
               dp=base + flip(near, k))
        for k in range(1, NFFN)
    ]
    for copy in returns:
        copy.start()
    ret_ref[near] = outq_ref[near]

    sum_out[0, 0:24] = small_ref[...]
    sum_out[0, 24:40] = jnp.zeros((16, width), f32)
    sum_out[0, 24:40, 0:16] = carry_ref[...]
    places = [{"mp": flip(mp_me, 1)}, {"mp": flip(mp_me, 2)}] + [
        {"dp": base + flip(near, k)} for k in (1, 2, 4)
    ]
    stages = [
        remote(sum_out.at[j], sum_in.at[j], ssend.at[j], srecv.at[j], **where)
        for j, where in enumerate(places)
    ]

    def stage(j):
        if j > 0:
            stages[j - 1].wait_recv()
            total = sum_out[j - 1] + sum_in[j - 1]
            if j == len(stages):
                sums_ref[...] = total
                return
            sum_out[j] = total
        stages[j].start()

    stage(0)
    moved = []
    if inside:
        din = dwin_own.shape[2]
        for k in (6, 4, 7, 5, 2, 3, 1):
            peer = flip(near, k)
            place = pl.ds(pl.multiple_of(peer * din, din), din)
            moved.append(
                remote(dwin_ref.at[:, place], dwin_own.at[near], esend.at[0, k], erecv.at[0, k],
                       dp=base + peer)
            )
            moved.append(
                remote(dwout_ref.at[place], dwout_own.at[near], esend.at[1, k], erecv.at[1, k],
                       dp=base + peer)
            )
        place = pl.ds(pl.multiple_of(near * din, din), din)
        mine = [
            pltpu.make_async_copy(dwin_ref.at[:, place], dwin_own.at[near], local.at[0]),
            pltpu.make_async_copy(dwout_ref.at[place], dwout_own.at[near], local.at[1]),
        ]
        for copy in moved + mine:
            copy.start()
    gather.forward()
    stage(1)
    gather.finish()

    w_all = w_ref[...].reshape(width, w_ref.shape[2])
    out_weight = w_all[:, 3 * cols :]
    for i in range(MP):
        mgrad_ref[i * rows : (i + 1) * rows] = dotf(agrad_all[i], out_weight).astype(bf16)
    grads_ref[:, 3 * cols :] = dotf(agrad_all[...].reshape(everyone, width), mixed_ref[...], TN)

    combine = Scatter(mp_me, ocore_out, ocore_in, ochip_out, ochip_in, rsend, rrecv)

    def out_block(q):
        at = pl.ds(pl.multiple_of(q * rows, rows), rows)
        weighted = (ret_ref[...].astype(f32) * gate_ref[:, :, 0:1]).astype(bf16)
        return dotf(
            pick_ref[:, :, at].reshape(NFFN * QUARTER, rows),
            weighted.reshape(NFFN * QUARTER, width), TN,
        )

    def head_back(h):
        lanes = slice(h * HD, (h + 1) * HD)
        for b in range(MP):
            at = slice(b * rows, (b + 1) * rows)
            seen = (b + 1) * rows
            query = q_ref[h, at]
            keys = k_ref[h, :seen]
            out_grad = mgrad_ref[at, lanes]
            scores = dotf(query, keys, NT) * HD**-0.5
            allowed = b * rows + lax.broadcasted_iota(
                jnp.int32, (rows, seen), 0
            ) >= lax.broadcasted_iota(jnp.int32, (rows, seen), 1)
            probs = jnp.where(allowed, jnp.exp(scores - lse_ref[at, h : h + 1]), 0.0)
            probs_grad = dotf(out_grad, v_ref[h, :seen], NT)
            inner = jnp.sum(probs * probs_grad, axis=1, keepdims=True)
            score_grad = (probs * (probs_grad - inner)).astype(bf16)
            query_grad = dotf(score_grad, keys) * HD**-0.5
            joint_ref[at, lanes] = (
                query_grad * cos_ref[at] - swap_halves(query_grad) * sin_ref[at]
            ).astype(bf16)
            key_grad = dotf(score_grad, query, TN) * HD**-0.5
            value_grad = dotf(probs.astype(bf16), out_grad, TN)
            if b == 0:
                key_acc[...] = jnp.zeros_like(key_acc)
                value_acc[...] = jnp.zeros_like(value_acc)
            key_acc[:seen] += key_grad
            value_acc[:seen] += value_grad
        key_grad = key_acc[...]
        joint_ref[:, cols + h * HD : cols + (h + 1) * HD] = (
            key_grad * cos_ref[...] - swap_halves(key_grad) * sin_ref[...]
        ).astype(bf16)
        joint_ref[:, 2 * cols + h * HD : 2 * cols + (h + 1) * HD] = value_acc[...].astype(bf16)

    for h in range(heads):
        head_back(h)
        if h == 0:
            stage(2)
            for copy in returns:
                copy.wait_recv()
            for j, q in enumerate((flip(mp_me, 3), flip(mp_me, 1))):
                ocore_out[j] = out_block(q).astype(bf16)
                combine.to_core[j].start()
            combine.to_core[0].wait_recv()
            ochip_out[...] = (
                out_block(combine.chip) + ocore_in[0].astype(f32)
            ).astype(bf16)
            combine.to_chip.start()
        if h == min(1, heads - 1):
            stage(3)
    combine.to_core[1].wait_recv()
    combine.to_chip.wait_recv()
    routed = out_block(mp_me) + ocore_in[1].astype(f32) + ochip_in[...].astype(f32)
    output_ref[...] = (residual_ref[...] + routed).astype(bf16)

    depth = width // NFFN
    grads_ref[:, : 3 * cols] = dotf(
        rows1_ref[...].reshape(everyone, width), joint_ref[...], TN
    )
    if inside:
        for p in range(NFFN):
            wsend_ref[p] = grads_ref[p * depth : (p + 1) * depth].astype(bf16)
        wcopies = [
            remote(wsend_ref.at[flip(near, k)], wrecv_ref.at[near], wsend.at[k], wrecv.at[k],
                   dp=base + flip(near, k))
            for k in (6, 4, 7, 5, 2, 3, 1)
        ]
        for copy in wcopies:
            copy.start()
        wrecv_ref[near] = wsend_ref[near]
    else:
        wgrad_ref[...] = grads_ref[...]
    stage(4)

    trip = Scatter(mp_me, xcore_out, xcore_in, xchip_out, xchip_in, xsend, xrecv)

    def x_block(q):
        at = pl.ds(pl.multiple_of(q * rows, rows), rows)
        return dotf(joint_ref[at], w_all[:, : 3 * cols], NT)

    normed_grad = trip.run(x_block)
    tokens = x_ref[...].astype(f32)
    scale = lax.rsqrt(jnp.mean(tokens * tokens, axis=-1, keepdims=True) + epsilon)
    scaled = tokens * scale
    first_out[0] = jnp.sum(normed_grad * scaled, axis=0, keepdims=True)
    firsts = [
        remote(first_out.at[0], first_mp.at[k], fsend.at[k], frecv.at[k], mp=flip(mp_me, k))
        for k in range(1, MP)
    ]
    for copy in firsts:
        copy.start()
    weighted = normed_grad * gain1_ref[...]
    xgrad_ref[...] = hgrad_ref[...] + scale * (
        weighted - scaled * jnp.mean(weighted * scaled, axis=-1, keepdims=True)
    )
    for copy in firsts:
        copy.wait_recv()
    first_out[1] = first_out[0] + first_mp[1] + first_mp[2] + first_mp[3]
    seconds = [
        remote(first_out.at[1], first_dp.at[k], fsend.at[MP + k], frecv.at[MP + k],
               dp=base + flip(near, k))
        for k in range(1, NFFN)
    ]
    for copy in seconds:
        copy.start()
    stage(5)
    if inside:
        for copy in wcopies:
            copy.wait_recv()
        total = wrecv_ref[0].astype(f32)
        for p in range(1, NFFN):
            total = total + wrecv_ref[p].astype(f32)
        wgrad_ref[...] = total
    for copy in seconds:
        copy.wait_recv()
    total = first_out[1]
    for k in range(1, NFFN):
        total = total + first_dp[k]
    first_ref[...] = total

    for copy in moved:
        copy.wait_recv()
    if inside:
        for copy in mine:
            copy.wait()
        for copy in wcopies:
            copy.wait_send()
    for copy in moved + returns + stages + firsts + seconds:
        copy.wait_send()
    combine.drain()
    trip.drain()


def attention_back(
    agrad, hgrad, x, gain1, rows1, w, q, k, v, mixed, lse, pick, gate, residual, outq, small,
    carry_grad, dwin, dwout, groups,
):
    rows, width = x.shape
    everyone = MP * rows
    cos, sin = rope_constants()
    inside = groups == 1
    cols = w.shape[-1]
    heads = q.shape[0]
    depth = width // NFFN
    hidden_cols = dwout.shape[-1]
    sd = jax.ShapeDtypeStruct
    vm = pltpu.VMEM
    dma = pltpu.SemaphoreType.DMA
    outs = [
        sd((rows, width), bf16),
        sd((rows, width), f32),
        sd((depth if inside else width, cols), f32),
        sd((40, width), f32),
        sd((1, width), f32),
    ]
    specs = [VM] * len(outs)
    if inside:
        outs += [sd((NFFN, 2, depth, hidden_cols), bf16), sd((NFFN, depth, hidden_cols), bf16)]
        specs += [HB, HB]
    return pl.pallas_call(
        functools.partial(back_kernel, inside),
        out_shape=outs,
        in_specs=[VM] * 19 + [HB, HB],
        out_specs=specs,
        scratch_shapes=[
            vm((MP, rows, width), bf16),
            vm((everyone, heads * HD), bf16),
            vm((everyone, 3 * heads * HD), bf16),
            vm((everyone, HD), f32),
            vm((everyone, HD), f32),
            vm((width, cols), f32),
            vm((NFFN, depth, cols), bf16),
            vm((NFFN, depth, cols), bf16),
            vm((NFFN, QUARTER, width), bf16),
            vm((2, rows, width), bf16),
            vm((2, rows, width), bf16),
            vm((rows, width), bf16),
            vm((rows, width), bf16),
            vm((2, rows, width), bf16),
            vm((2, rows, width), bf16),
            vm((rows, width), bf16),
            vm((rows, width), bf16),
            vm((5, 40, width), f32),
            vm((5, 40, width), f32),
            vm((MP, 1, width), f32),
            vm((NFFN, 1, width), f32),
            vm((2, 1, width), f32),
            dma((3,)), dma((3,)),
            dma((8,)), dma((8,)),
            dma((2, 8)), dma((2, 8)), dma((2,)),
            dma((3,)), dma((3,)),
            dma((3,)), dma((3,)),
            dma((8,)), dma((8,)),
            dma((5,)), dma((5,)),
            dma((MP + NFFN,)), dma((MP + NFFN,)),
        ],
        compiler_params=pltpu.CompilerParams(
            collective_id=2, has_side_effects=True, vmem_limit_bytes=60 * 2**20
        ),
        name="attention_backward",
    )(
        agrad, hgrad, x, gain1, jnp.asarray(cos), jnp.asarray(sin), rows1, w, q, k, v, mixed, lse,
        pick, gate, residual, outq, small, carry_grad, dwin, dwout,
    )


def clusters():
    groups = lax.axis_size("dp") // NFFN
    near = [[group * NFFN + expert for expert in range(NFFN)] for group in range(groups)]
    far = [[group * NFFN + expert for group in range(groups)] for expert in range(NFFN)]
    return groups, near, far


def exchange(shard, dim):
    _, near, far = clusters()
    own = lax.all_to_all(shard, "dp", 0, dim, axis_index_groups=near, tiled=True)
    return lax.all_gather(own, "dp", axis=dim, axis_index_groups=far, tiled=True)


def exchange_back(grads, dim):
    _, near, far = clusters()
    grads = lax.psum_scatter(
        grads.astype(f32), "dp", scatter_dimension=dim, axis_index_groups=far, tiled=True
    )
    return lax.all_to_all(grads.astype(bf16), "dp", dim, 0, axis_index_groups=near, tiled=True)


def per_device(
    inputs,
    query_key_value,
    output_weight,
    expert_input,
    expert_output,
    first_gain,
    second_gain,
    router_weight,
    logit_carry,
    constant_mix,
    constant_values,
    previous_logits,
    routes,
    cotangent,
):
    rows, width = inputs.shape
    offset = lax.axis_index("mp") * rows
    groups, _, far = clusters()
    gain_one = first_gain.astype(f32)[None]
    gain_two = second_gain.astype(f32)[None]

    def own(array):
        return lax.dynamic_slice_in_dim(array, offset, rows, 0)

    def sixteen(array):
        return jnp.pad(array.T, ((0, 16 - array.shape[1]), (0, 0)))

    prior = jnp.dot(previous_logits, logit_carry, precision=highest)
    routes_t = jnp.pad(routes.T, ((0, 6), (0, 0)), constant_values=-1)
    routes_own = jnp.pad(own(routes), ((0, 0), (0, 126)), constant_values=-1)
    prior_own = jnp.pad(own(prior), ((0, 0), (0, 16 - NEXP)))
    carry = jnp.pad(logit_carry, ((0, 16 - NEXP), (0, 16 - NEXP)))
    shard_depth = query_key_value.shape[0]
    shard = jnp.concatenate(
        [query_key_value.reshape(shard_depth, -1), output_weight.T], axis=1
    )
    cols = output_weight.shape[0]
    expert_output_t = expert_output.transpose(0, 2, 1)
    if groups > 1:
        shard = lax.all_gather(shard, "dp", axis=0, tiled=True)
        win = exchange(expert_input, 2)[0]
        wout = exchange(expert_output_t, 1)[0]
    got = attention(inputs, gain_one, gain_two, shard, expert_input, expert_output_t, groups)
    rows1, w, q, k, v, mixed, lse, hidden, rows2 = got[:9]
    if groups == 1:
        win, wout = got[9:]
    (residual, hidden_grad, attended_grad, logits_grad, small, carry_grad, pick, gate, outq, dwin,
     dwout) = experts(
        rows2, hidden, cotangent, gain_two, sixteen(router_weight), sixteen(constant_mix),
        constant_values, sixteen(prior), carry, sixteen(own(previous_logits)), routes_t,
        routes_own, prior_own, win, wout,
    )
    output, input_grad, weight_grad, sums, first_grad, *expert_grads = attention_back(
        attended_grad, hidden_grad, inputs, gain_one, rows1, w, q, k, v, mixed, lse, pick, gate,
        residual, outq, small, carry_grad, dwin, dwout, groups,
    )
    if groups > 1:
        weight_grad = lax.psum_scatter(weight_grad, "dp", scatter_dimension=0, tiled=True)
        expert_grads = [exchange_back(dwin[None], 2), exchange_back(dwout[None], 1)]
        sums, first_grad = lax.psum((sums, first_grad), "dp", axis_index_groups=far)
    expert_in_grad = expert_grads[0].astype(f32)
    expert_out_grad = expert_grads[1].transpose(0, 2, 1).astype(f32)
    return (
        output,
        input_grad,
        logits_grad[:NEXP].T,
        weight_grad[:, : 3 * cols].reshape(shard_depth, 3, cols),
        weight_grad[:, 3 * cols :].T,
        expert_in_grad,
        expert_out_grad,
        first_grad[0],
        sums[22],
        sums[:NEXP].T,
        sums[24 : 24 + NEXP, :NEXP],
        sums[16:20].T,
        sums[20:22],
    )


def solution(mesh):
    in_specs = (
        P(("dp", "mp"), None),
        P("dp", None, "mp"),
        P("mp", "dp"),
        P(None, None, "dp", "mp"),
        P(None, "mp", "dp"),
        P(),
        P(),
        P(),
        P(),
        P(),
        P(),
        P("dp", None),
        P("dp", None),
        P(("dp", "mp"), None),
    )
    out_specs = (
        P(("dp", "mp"), None),
        P(("dp", "mp"), None),
        P(("dp", "mp"), None),
        P("dp", None, "mp"),
        P("mp", "dp"),
        P(None, None, "dp", "mp"),
        P(None, "mp", "dp"),
        P(),
        P(),
        P(),
        P(),
        P(),
        P(),
    )
    return jax.shard_map(
        per_device, mesh=mesh, in_specs=in_specs, out_specs=out_specs, check_vma=False
    )
```

time: 764 us -> 361 us (0.47); the launches traced: 754 us -> 360 us
  Pallas kernels: 81.6 us -> 326 us
  blocking collectives: 190 us -> 0 us
  waiting for transfers between devices: 151 us -> 0 us
  local copies, waits for them, and re-layouts: 128 us -> 26.8 us
  other arithmetic: 88.2 us -> 5.55 us
  matrix products: 74.4 us -> 1.09 us
  starting transfers between devices: 17.7 us -> 0 us
  between operations: 15.2 us -> 0.75 us
    pallas_call x0 -> x2, Pallas kernels: none -> 245 us  [the longest x1 133 us: experts(): pl.pallas_call(expert_kernel, out_shape=outs, in_specs=[VM] * 15, out_spe...]
    all_to_all x2 -> x0, blocking collectives: 150 us -> none  [swap(): lax.all_to_all(blocks, 'dp', 0, 0, axis_index_groups=near, tiled=True)]
    all_to_all x4 -> x0, waiting for transfers between devices: 111 us -> none  [the longest x2 62 us: swap(): lax.all_to_all(blocks, 'dp', 0, 0, axis_index_groups=near, tiled=True)]
    dot_general x28 -> x1, matrix products: 71.2 us -> 1.09 us  [per_device(): prior = jnp.dot(previous_logits, logit_carry, precision=highest)]
    gather x8 -> x0, local copies, waits for them, and re-layouts: 49.9 us -> none  [the longest x5 17.9 us: per_device(): chosen = jnp.take_along_axis(logits, routes, axis=1)]
    scatter-add x3 -> x0, other arithmetic: 47.5 us -> none  [the longest x1 16.5 us: per_device(): jnp.zeros((group_rows, model_width), jnp.float32).at[tokens_of]]
    psum x1 -> x0, blocking collectives: 40.4 us -> none  [per_device(): lax.psum((first_gain_grad, second_gain_grad, router_grad, logit_carry_gra...]
    reduce_scatter x4 -> x0, waiting for transfers between devices: 28.3 us -> none  [the longest x1 28.3 us: per_device(): lax.psum_scatter(normed_part, 'mp', scatter_dimension=0, tiled=True)]
  transfers between devices with their start and end apart: 12 -> 0, of which waited for: 6 -> 0; matrix products, arithmetic and copies ran while one was open for 29% -> 0% of each run, Pallas kernels for 0% -> 0%
where the time goes in v3:
time: 361 us; the launch traced here: 360 us
  Pallas kernels  326 us (90%)
  local copies, waits for them, and re-layouts  26.8 us (7%)
  other arithmetic  5.55 us (2%)
    pallas_call x1, Pallas kernels, experts(): pl.pallas_call(expert_kernel, out_shape=outs, in_specs=[VM] * 15, out_spe...  133 us
    pallas_call x1, Pallas kernels, attention_back(): pl.pallas_call(functools.partial(back_kernel, inside), out_shape=outs, in...  112 us
    pallas_call x1, Pallas kernels, attention(): pl.pallas_call(functools.partial(attention_kernel, inside), out_shape=out...  81.7 us

profile of v3, /device:TPU:0, one launch (start us, length us, event | category | flops | bytes accessed | tf_op | source)
XLA Modules:
  0.0 360.5 jit_solution(10447488668181515457)
XLA Ops:
  0.6 0.7 constant_dynamic-slice_fusion.1
  1.3 1.3 reshape.34.gain1_ref
  2.6 1.3 reshape.35.gain2_ref
  3.9 1.3 pad.35.carry_ref
  5.2 1.4 pad.32.router_ref
  6.5 1.3 pad.33.mix_ref
  7.8 1.3 pad.37.routes_ref
  9.1 0.9 copy.38
  10.0 1.1 fusion
  11.1 0.7 dynamic-slice_bitcast_fusion
  12.5 0.6 pad.34.prior_ref
  13.2 0.7 pad.38.routes_own_ref
  14.0 0.7 pad.39.prior_own_ref
  14.7 1.1 copy.37
  15.9 0.8 pad_maximum_fusion.wshard_ref
  16.7 81.7 %attention_forward.1 = (bf16[4,256,768]{2,1,0:T(8,128)(2,1)}, bf16[8,96,768]{2,1,0:T(8,128)(2,1)}, bf16[3,1024,64]{2,1,0:T(8,128)(2,1)}, bf16[3,1024,64]{2,1,0:T...) custom-call(bf16[256,768]{1,0:T(8,128)(2,1)} %x_ref.3, ...), custom_call_target="tpu_custom_call" | custom-call | tf_op jit(solution)/shard_map/attention_forward/pallas_call | solution.py:290
  98.3 132.7 %experts.1 = (f32[256,768]{1,0:T(8,128)}, f32[256,768]{1,0:T(8,128)}, bf16[256,768]{1,0:T(8,128)(2,1)}, f32[16,256]{1,0:T(8,128)}, f32[24,768]{1,0:T(8,128)}, /*...) custom-call(bf16[4,256,768]{2,1,0:T(8,128)(2,1)} %get-tuple-element., ...), custom_call_target="tpu_custom_call" | custom-call | tf_op jit(solution)/shard_map/experts/pallas_call | solution.py:782
  231.0 111.9 %attention_backward.1 = (bf16[256,768]{1,0:T(8,128)(2,1)}, f32[256,768]{1,0:T(8,128)}, f32[96,768]{1,0:T(8,128)}, f32[40,768]{1,0:T(8,128)}, f32[1,768]{1,0:T(1,...) custom-call(bf16[256,768]{1,0:T(8,128)(2,1)} %get-tuple-element.46.agrad_ref, ...), custom_call_target="tpu_custom_call" | custom-call | tf_op jit(solution)/shard_map/attention_backward/pallas_call | solution.py:1092
  343.0 1.3 reduce
  344.3 1.3 slice_reduce_fusion
  345.7 1.3 slice.31
  347.0 1.3 slice.29
  348.3 1.3 slice_bitcast_fusion.3
  349.6 1.4 slice_bitcast_fusion.1
  351.7 1.0 slice_bitcast_fusion
  352.7 1.0 slice.25
  353.6 0.7 copy.44
  354.5 0.9 copy.43
  355.4 1.4 convert_bitcast_fusion
  356.8 2.1 convert_element_type.23
  358.9 0.7 copy.49
  359.6 0.9 copy.50
  (16 shorter events, 1.8 us)
Async XLA Ops:
  231.0 120.0 %copy-start.4 = (f32[16,256]{1,0:T(8,128)S(1)}, f32[16,256]{1,0:T(8,128)}, u32[]{:S(2)}) copy-start(f32[16,256]{1,0:T(8,128)} %get-tuple-element.65) | copy-start | bytes 49156
  343.0 12.4 %copy-start.2 = (bf16[8,96,512]{2,1,0:T(8,128)(2,1)S(1)}, bf16[8,96,512]{2,1,0:T(8,128)(2,1)}, u32[]{:S(2)}) copy-start(bf16[8,96,512]{2,1,0:T(8,128)(2,1)} %get-tuple-element.68) | copy-start | bytes 2359300
  354.5 2.2 copy-start
  356.8 2.1 copy-start.3
  356.8 2.8 copy-start.1

commit v4 on v3

v4 whole, which is shorter than its diff:
```python
import functools
import numpy as np
import jax
import jax.numpy as jnp
from jax import lax
from jax.sharding import PartitionSpec as P
from jax.experimental import pallas as pl
from jax.experimental.pallas import tpu as pltpu

HD = 64
NFFN = 8
NEXP = 12
SEQ = 1024
CAP = 256
MP = 4
QUARTER = CAP // MP

epsilon = 1e-06
rope_base = 10000.0
highest = lax.Precision.HIGHEST
f32 = jnp.float32
bf16 = jnp.bfloat16
MESH = pl.DeviceIdType.MESH
VM = pl.BlockSpec(memory_space=pltpu.VMEM)
HB = pl.BlockSpec(memory_space=pl.ANY)
NT = (((1,), (1,)), ((), ()))
TN = (((0,), (0,)), ((), ()))


def flip(index, distance):
    out = index
    bit = 1
    while bit <= distance:
        if distance & bit:
            out = out + bit - 2 * bit * ((index // bit) % 2)
        bit *= 2
    return out


def dotf(a, b, dims=None):
    if dims is None:
        return jnp.dot(a, b, preferred_element_type=f32)
    return lax.dot_general(a, b, dims, preferred_element_type=f32)


def remote(src, dst, send, recv, **where):
    return pltpu.make_async_remote_copy(
        src_ref=src, dst_ref=dst, send_sem=send, recv_sem=recv, device_id=where, device_id_type=MESH
    )


def greet(mp_me, near, base):
    barrier = pltpu.get_barrier_semaphore()
    for k in range(1, MP):
        pl.semaphore_signal(barrier, inc=1, device_id={"mp": flip(mp_me, k)}, device_id_type=MESH)
    for k in range(1, NFFN):
        pl.semaphore_signal(
            barrier, inc=1, device_id={"dp": base + flip(near, k)}, device_id_type=MESH
        )
    pl.semaphore_wait(barrier, MP - 1 + NFFN - 1)


def rope_constants():
    half = HD // 2
    positions = np.arange(SEQ, dtype=np.float32)
    frequency = (rope_base ** (-np.arange(half, dtype=np.float32) / half)).astype(np.float32)
    angles = (positions[:, None] * frequency[None, :]).astype(np.float32)
    cosine, sine = np.cos(angles), np.sin(angles)
    return (
        np.concatenate([cosine, cosine], axis=1),
        np.concatenate([-sine, sine], axis=1),
    )


def swap_halves(x):
    half = HD // 2
    return jnp.concatenate([x[:, half:], x[:, :half]], axis=1)


class Gather:
    def __init__(self, ref, mp_me, send, recv):
        self.me, self.core, self.chip = mp_me, flip(mp_me, 1), flip(mp_me, 2)
        own = ref.at[mp_me]
        far = ref.at[self.chip]
        self.to_chip = remote(own, own, send.at[0], recv.at[0], mp=self.chip)
        self.to_core = remote(own, own, send.at[1], recv.at[1], mp=self.core)
        self.relay = remote(far, far, send.at[2], recv.at[2], mp=self.core)

    def start(self):
        self.to_chip.start()
        self.to_core.start()

    def forward(self):
        self.to_chip.wait_recv()
        self.relay.start()

    def finish(self):
        self.to_core.wait_recv()
        self.relay.wait_recv()
        self.to_chip.wait_send()
        self.to_core.wait_send()
        self.relay.wait_send()


def pack3(value):
    high = value.astype(bf16).astype(f32)
    rest = value - high
    mid = rest.astype(bf16).astype(f32)
    low = (rest - mid).astype(bf16).astype(f32)
    lane = lax.broadcasted_iota(jnp.int32, (value.shape[0], 128), 1)
    return jnp.where(
        lane == 0, high, jnp.where(lane == 1, mid, jnp.where(lane == 2, low, 0.0))
    ).astype(bf16)


def unpack3(parts):
    return jnp.sum(parts.astype(f32), axis=-1, keepdims=True)


def exact(left, right, dims=None):
    high = left.astype(bf16)
    rest = left - high.astype(f32)
    mid = rest.astype(bf16)
    low = (rest - mid.astype(f32)).astype(bf16)
    return dotf(high, right, dims) + (dotf(mid, right, dims) + dotf(low, right, dims))


class Scatter:
    def __init__(self, mp_me, core_out, core_in, chip_out, chip_in, send, recv):
        self.me, self.core, self.chip = mp_me, flip(mp_me, 1), flip(mp_me, 2)
        self.core_out, self.core_in = core_out, core_in
        self.chip_out, self.chip_in = chip_out, chip_in
        self.to_core = [
            remote(core_out.at[j], core_in.at[j], send.at[j], recv.at[j], mp=self.core)
            for j in range(2)
        ]
        self.to_chip = remote(chip_out, chip_in, send.at[2], recv.at[2], mp=self.chip)

    def run(self, blocks):
        for j, block in enumerate((flip(self.me, 3), self.core)):
            self.core_out[j] = blocks(block).astype(bf16)
            self.to_core[j].start()
        term = blocks(self.chip)
        self.to_core[0].wait_recv()
        self.chip_out[...] = (term + self.core_in[0].astype(f32)).astype(bf16)
        self.to_chip.start()
        term = blocks(self.me)
        self.to_core[1].wait_recv()
        term = term + self.core_in[1].astype(f32)
        self.to_chip.wait_recv()
        return term + self.chip_in[...].astype(f32)

    def drain(self):
        for copy in self.to_core + [self.to_chip]:
            copy.wait_send()


def forward_kernel(
    inside,
    x_ref, cot_ref, params_ref, routing_ref, cos_ref, sin_ref, wshard_ref, win_shard, wout_shard,
    rows1_ref, w_ref, q_ref, k_ref, v_ref, mixed_ref, lse_ref,
    residual_ref, hgrad_ref, agrad_ref, lgrad_ref, small_ref, pick_ref, gate_ref, outp_ref, dw_ref,
    rows2_ref, hidden_ref, sum_ref, core_in, chip_out, chip_in, core_out,
    cot_all, place_ref, gates_ref, prior_ref, msgx, msgc, xs, cs, units_ref, pgrad_ref,
    part_ref, keep_ref, gcore_out, gcore_in, gchip_out, gchip_in, gret, score_out, score_in,
    ncore_in, nchip_in,
    sends, recvs, wsend, wrecv, esend, erecv, local,
    csend, crecv, xsend, xrecv, dsend, drecv, xgs, xgr, cgs, cgr, gsend, grecv,
    rsend, rrecv, ssend, srecv, nsend, nrecv,
):
    mp_me = lax.axis_index("mp")
    dp_me = lax.axis_index("dp")
    near = lax.rem(dp_me, NFFN)
    base = dp_me - near
    core, chip, far = flip(mp_me, 1), flip(mp_me, 2), flip(mp_me, 3)
    rows, width = x_ref.shape
    everyone = MP * rows
    greet(mp_me, near, base)

    tokens = x_ref[...].astype(f32)
    scale = lax.rsqrt(jnp.mean(tokens * tokens, axis=-1, keepdims=True) + epsilon)
    rows1_ref[mp_me] = (tokens * scale * params_ref[23:24]).astype(bf16)
    gather1 = Gather(rows1_ref, mp_me, sends.at[pl.ds(0, 3)], recvs.at[pl.ds(0, 3)])
    gather1.start()
    if inside:
        w_ref[near] = wshard_ref[...]
        own = w_ref.at[near]
        along = [
            remote(own, own, wsend.at[k], wrecv.at[k], dp=base + flip(near, k)) for k in (2, 4, 6)
        ]
        for copy in along:
            copy.start()
        mate = base + flip(near, 1)
        across = [remote(own, own, wsend.at[0], wrecv.at[0], dp=mate)]
        across[0].start()
    cot_all[mp_me] = cot_ref[...]
    cot_gather = Gather(cot_all, mp_me, csend, crecv)
    cot_gather.start()

    ids = lax.broadcasted_iota(jnp.int32, (16, everyone), 0).astype(f32)
    chosen = (ids == routing_ref[16:17]) | (ids == routing_ref[17:18])
    earlier = lax.broadcasted_iota(jnp.int32, (everyone, everyone), 0) < lax.broadcasted_iota(
        jnp.int32, (everyone, everyone), 1
    )
    counts = dotf(
        jnp.where(chosen, 1.0, 0.0).astype(bf16), jnp.where(earlier, 1.0, 0.0).astype(bf16)
    )
    place_ref[...] = jnp.where(chosen, counts, -1.0)
    wanted = (lax.broadcasted_iota(jnp.int32, (QUARTER, everyone), 0) + QUARTER * mp_me).astype(f32)

    def target(k):
        return lax.rem(near + k, NFFN)

    def choose(k, carried):
        pick = wanted == place_ref[pl.ds(target(k), 1)]
        pick_ref[k] = jnp.where(pick, 1.0, 0.0).astype(bf16)
        return carried

    lax.fori_loop(0, NFFN, choose, 0)
    carry = params_ref[24:40, 0:16]
    prior_ref[...] = lax.dot_general(
        carry, routing_ref[0:16], TN, preferred_element_type=f32, precision=highest
    )

    if inside:
        for k, copy in zip((2, 4, 6), along):
            copy.wait_recv()
            block = w_ref.at[flip(near, k)]
            onward = remote(block, block, wsend.at[k + 1], wrecv.at[k + 1], dp=mate)
            onward.start()
            across.append(onward)
        gather1.forward()
        for copy in across:
            copy.wait_recv()
        for copy in along + across:
            copy.wait_send()
        weights = []
        din = win_shard.shape[2]
        place = pl.ds(pl.multiple_of(near * din, din), din)
        for k in (4, 2, 6, 5, 7, 3, 1):
            peer = flip(near, k)
            for i, (src, dst) in enumerate([
                (win_shard.at[peer], dw_ref.at[0:2, place]),
                (wout_shard.at[peer], dw_ref.at[2, place]),
            ]):
                weights.append(
                    remote(src, dst, esend.at[i, k], erecv.at[i, k], dp=base + peer)
                )
        first = 4
        for copy in weights[:first]:
            copy.start()
        mine = [
            pltpu.make_async_copy(win_shard.at[near], dw_ref.at[0:2, place], local.at[0]),
            pltpu.make_async_copy(wout_shard.at[near], dw_ref.at[2, place], local.at[1]),
        ]
        for copy in mine:
            copy.start()
    else:
        w_ref[...] = wshard_ref[...]
        mine = [
            pltpu.make_async_copy(win_shard, dw_ref.at[0:2], local.at[0]),
            pltpu.make_async_copy(wout_shard, dw_ref.at[2], local.at[1]),
        ]
        for copy in mine:
            copy.start()
        gather1.forward()
    gather1.finish()

    cot_gather.forward()
    cot_gather.finish()

    def c_copy(k):
        return remote(
            msgc.at[k], cs.at[k, mp_me], dsend.at[k], drecv.at[k], dp=base + target(k)
        )

    def send(picked, ref, copy, lanes):
        def half(i, carried):
            start = 4 - 4 * i
            blocks = dotf(pick_ref[pl.ds(start, 4)].reshape(4 * QUARTER, everyone), picked())
            ref[(pl.ds(start, 4),) + lanes] = blocks.astype(bf16).reshape(4, QUARTER, width)

            def go(k, inner):
                @pl.when(k > 0)
                def _():
                    copy(k).start()

                return inner

            return lax.fori_loop(start, start + 4, go, carried)

        lax.fori_loop(0, 2, half, 0)

    send(lambda: cot_all[...].reshape(everyone, width), msgc, c_copy, ())
    cs[0, mp_me] = msgc[0]
    if inside:
        for copy in weights[first:]:
            copy.start()

    w_all = w_ref[...].reshape(width, w_ref.shape[2])
    heads = q_ref.shape[0]
    cols = heads * HD

    def project(i, carry):
        at = pl.ds(pl.multiple_of(i * rows, rows), rows)
        joint = dotf(rows1_ref[i], w_all[:, : 3 * cols])
        cosine, sine = cos_ref[at], sin_ref[at]
        for h in range(heads):
            query = joint[:, h * HD : (h + 1) * HD]
            key = joint[:, cols + h * HD : cols + (h + 1) * HD]
            q_ref[h, at] = (query * cosine + swap_halves(query) * sine).astype(bf16)
            k_ref[h, at] = (key * cosine + swap_halves(key) * sine).astype(bf16)
            v_ref[h, at] = joint[:, 2 * cols + h * HD : 2 * cols + (h + 1) * HD].astype(bf16)
        return carry

    lax.fori_loop(0, MP, project, 0)
    out_weight = w_all[:, 3 * cols :]

    to_core = [
        remote(core_out.at[j], core_in.at[j], sends.at[3 + j], recvs.at[3 + j], mp=core)
        for j in range(2)
    ]
    to_chip = remote(chip_out, chip_in, sends.at[5], recvs.at[5], mp=chip)

    def attend(step, carry):
        block = flip(mp_me, 3)
        block = jnp.where(step == 1, core, jnp.where(step == 2, chip, jnp.where(step == 3, mp_me, block)))
        at = pl.ds(pl.multiple_of(block * rows, rows), rows)
        row_ids = block * rows + lax.broadcasted_iota(jnp.int32, (rows, SEQ), 0)
        seen = row_ids >= lax.broadcasted_iota(jnp.int32, (rows, SEQ), 1)
        for h in range(heads):
            scores = dotf(q_ref[h, at], k_ref[h], NT) * HD**-0.5
            scores = jnp.where(seen, scores, -jnp.inf)
            peak = jnp.max(scores, axis=-1, keepdims=True)
            exponent = jnp.exp(scores - peak)
            total = jnp.sum(exponent, axis=-1, keepdims=True)
            probs = (exponent * (1.0 / total)).astype(bf16)
            mixed_ref[at, h * HD : (h + 1) * HD] = dotf(probs, v_ref[h]).astype(bf16)
            lse_ref[at, h : h + 1] = peak + jnp.log(total)
        part = dotf(mixed_ref[at], out_weight, NT)

        @pl.when(step == 0)
        def _():
            core_out[0] = part.astype(bf16)
            to_core[0].start()

        @pl.when(step == 1)
        def _():
            core_out[1] = part.astype(bf16)
            to_core[1].start()

        @pl.when(step == 2)
        def _():
            to_core[0].wait_recv()
            chip_out[...] = (part + core_in[0].astype(f32)).astype(bf16)
            to_chip.start()

        @pl.when(step == 3)
        def _():
            sum_ref[...] = part

        return carry

    lax.fori_loop(0, MP, attend, 0)
    to_core[1].wait_recv()
    partial = sum_ref[...] + core_in[1].astype(f32)
    to_chip.wait_recv()
    hidden = x_ref[...].astype(f32) + (partial + chip_in[...].astype(f32))
    hidden_ref[...] = hidden
    scale2 = lax.rsqrt(jnp.mean(hidden * hidden, axis=-1, keepdims=True) + epsilon)
    rows2_ref[mp_me] = (hidden * scale2 * params_ref[22:23]).astype(bf16)
    gather2 = Gather(rows2_ref, mp_me, sends.at[pl.ds(6, 3)], recvs.at[pl.ds(6, 3)])
    gather2.start()
    for copy in to_core + [to_chip]:
        copy.wait_send()
    gather2.forward()

    def turn(i):
        return lax.rem(i + 4, NFFN)

    def c_gather(k):
        return Gather(cs.at[k], mp_me, cgs.at[k], cgr.at[k])

    def at_step(i, first, body):
        @pl.when((i >= first) & (i < NFFN + first))
        def _():
            body(turn(i - first))

    def cot_step(i, carried):
        def arrived(k):
            @pl.when(k > 0)
            def _():
                c_copy(k).wait_recv()

            c_gather(k).start()

        at_step(i, 0, arrived)
        at_step(i, 1, lambda k: c_gather(k).forward())
        return carried

    lax.fori_loop(0, NFFN + 1, cot_step, 0)
    gather2.finish()

    router = params_ref[0:16].astype(bf16)
    mix = params_ref[16:20].astype(bf16)
    tokens = rows2_ref[...].reshape(everyone, width)
    logits = dotf(router, tokens, NT) + prior_ref[...]
    masked = jnp.where(place_ref[...] >= 0.0, logits, -jnp.inf)
    exponent = jnp.exp(masked - jnp.max(masked, axis=0, keepdims=True))
    gates_ref[...] = exponent / jnp.sum(exponent, axis=0, keepdims=True)

    def weigh(k, carried):
        gate = jnp.sum(
            pick_ref[k].astype(f32) * gates_ref[pl.ds(target(k), 1)], axis=1, keepdims=True
        )
        gate_ref[k] = jnp.broadcast_to(gate, (QUARTER, 128))
        msgx[k, :, width:] = pack3(gate)
        return carried

    lax.fori_loop(0, NFFN, weigh, 0)

    def x_copy(k):
        return remote(
            msgx.at[k], xs.at[k, mp_me], xsend.at[k], xrecv.at[k], dp=base + target(k)
        )

    send(
        lambda: rows2_ref[...].reshape(everyone, width), msgx, x_copy,
        (slice(None), slice(0, width)),
    )
    xs[0, mp_me] = msgx[0]

    def x_gather(k):
        return Gather(xs.at[k], mp_me, xgs.at[k], xgr.at[k])

    def slots_of(k):
        return pl.ds(pl.multiple_of(k * CAP, CAP), CAP)

    def x_step(i, carried):
        def arrived(k):
            @pl.when(k > 0)
            def _():
                x_copy(k).wait_recv()

            x_gather(k).start()

        def passed(k):
            x_gather(k).forward()

        at_step(i, 0, arrived)
        at_step(i, 1, passed)
        return carried

    lax.fori_loop(0, NFFN + 1, x_step, 0)
    if inside:
        for copy in weights:
            copy.wait_recv()
    for copy in mine:
        copy.wait()

    def r_trip(k):
        slot = lax.rem(k, 4)
        return Scatter(
            mp_me, gcore_out.at[slot], gcore_in.at[k], gchip_out.at[slot], gchip_in.at[k],
            gsend.at[k], grecv.at[k],
        )

    def g_copy(k):
        return remote(
            msgx.at[k], gret.at[k], rsend.at[k], rrecv.at[k],
            dp=base + lax.rem(near - k + NFFN, NFFN),
        )

    def seal(ref, index, total):
        ref[index + (slice(None), slice(0, width))] = total[:, :width].astype(bf16)
        ref[index + (slice(None), slice(width, None))] = pack3(unpack3(total[:, width:]))

    def expert_step(i, carried):
        def compute(k):
            c_gather(k).finish()
            x_gather(k).finish()
            x = xs[k].reshape(CAP, width + 128)[:, :width]
            gate = unpack3(xs[k].reshape(CAP, width + 128)[:, width:])
            c = cs[k].reshape(CAP, width)
            gate_pre = dotf(x, dw_ref[0])
            up_pre = dotf(x, dw_ref[1])
            sig = jax.nn.sigmoid(gate_pre)
            units = (gate_pre * sig * up_pre).astype(bf16)
            units_ref[slots_of(k)] = units
            outp_ref[k] = dotf(units, dw_ref[2], NT).astype(bf16).reshape(MP, QUARTER, width)
            raw = dotf(c, dw_ref[2])
            score = jnp.sum(units.astype(f32) * raw, axis=1, keepdims=True)
            units_grad = raw * gate
            gate_grad = (units_grad * up_pre * sig * (1.0 + gate_pre * (1.0 - sig))).astype(bf16)
            up_grad = (units_grad * (gate_pre * sig)).astype(bf16)
            pgrad_ref[0, slots_of(k)] = gate_grad
            pgrad_ref[1, slots_of(k)] = up_grad
            back = dotf(gate_grad, dw_ref[0], NT) + dotf(up_grad, dw_ref[1], NT)
            cs[k] = (c.astype(f32) * gate).astype(bf16).reshape(MP, QUARTER, width)
            part_ref[:, :, :width] = back.reshape(MP, QUARTER, width)
            part_ref[:, :, width:] = pack3(score).astype(f32).reshape(MP, QUARTER, 128)
            slot = lax.rem(k, 4)
            gcore_out[slot, 0] = part_ref[far].astype(bf16)
            gcore_out[slot, 1] = part_ref[core].astype(bf16)
            keep_ref[slot, 0] = part_ref[chip]
            keep_ref[slot, 1] = part_ref[mp_me]
            for copy in r_trip(k).to_core:
                copy.start()

        def across(k):
            trip = r_trip(k)
            trip.to_core[0].wait_recv()
            seal(gchip_out, (lax.rem(k, 4),), keep_ref[lax.rem(k, 4), 0] + gcore_in[k, 0].astype(f32))
            trip.to_chip.start()

        def away(k):
            trip = r_trip(k)
            trip.to_core[1].wait_recv()
            trip.to_chip.wait_recv()
            total = (
                keep_ref[lax.rem(k, 4), 1]
                + gcore_in[k, 1].astype(f32)
                + gchip_in[k].astype(f32)
            )
            trip.drain()

            @pl.when(k > 0)
            def _():
                x_copy(k).wait_send()

            seal(msgx, (k,), total)

            @pl.when(k > 0)
            def _():
                g_copy(k).start()

            @pl.when(k == 0)
            def _():
                gret[0] = msgx[0]

        at_step(i, 4, away)
        at_step(i, 0, compute)
        at_step(i, 2, across)
        return carried

    lax.fori_loop(0, NFFN + 4, expert_step, 0)

    def weights_step(j, carried):
        at = pl.ds(pl.multiple_of(j * 128, 128), 128)
        x = xs[:, :, :, at].reshape(NFFN * CAP, 128)
        c = cs[:, :, :, at].reshape(NFFN * CAP, 128)
        dw_ref[0, at] = dotf(x, pgrad_ref[0], TN).astype(bf16)
        dw_ref[1, at] = dotf(x, pgrad_ref[1], TN).astype(bf16)
        dw_ref[2, at] = dotf(c, units_ref[...], TN).astype(bf16)
        return carried

    lax.fori_loop(0, width // 128, weights_step, 0)

    n_bf = rows2_ref[mp_me]
    n = n_bf.astype(f32)
    cot = cot_ref[...].astype(f32)
    hidden = hidden_ref[...]
    lane = lax.broadcasted_iota(jnp.int32, (rows, 128), 1)
    own_at = pl.ds(pl.multiple_of(mp_me * rows, rows), rows)
    gates_t = gates_ref[:, own_at]
    own_gates = jnp.concatenate([gates_t, jnp.zeros((112, rows), f32)], axis=0).T
    copy_gate = own_gates[:, NFFN + 1 : NFFN + 2]
    const_gates = [own_gates[:, NFFN + 2 : NFFN + 3], own_gates[:, NFFN + 3 : NFFN + 4]]
    mix_logits = dotf(n_bf, mix, NT)
    with_normed = jnp.sum(cot * n, axis=1, keepdims=True)
    residual = hidden + copy_gate * n
    local_grad = copy_gate * cot
    local_scores = jnp.where(lane == NFFN + 1, with_normed, 0.0)
    mix_grads = jnp.zeros((rows, 128), f32)
    for c in range(2):
        first, second = mix_logits[:, 2 * c : 2 * c + 1], mix_logits[:, 2 * c + 1 : 2 * c + 2]
        top = jnp.maximum(first, second)
        first, second = jnp.exp(first - top), jnp.exp(second - top)
        share = 1.0 / (first + second)
        first, second = first * share, second * share
        constant = params_ref[20 + c : 21 + c]
        with_constant = jnp.sum(cot * constant, axis=1, keepdims=True)
        gate = const_gates[c]
        residual = residual + gate * (first * n + second * constant)
        local_scores = jnp.where(
            lane == NFFN + 2 + c, first * with_normed + second * with_constant, local_scores
        )
        local_grad = local_grad + (first * gate) * cot
        small_ref[20 + c : 21 + c] = jnp.sum((second * gate) * cot, axis=0, keepdims=True)
        grad_first, grad_second = gate * with_normed, gate * with_constant
        mean = first * grad_first + second * grad_second
        mix_grads = jnp.where(lane == 2 * c, first * (grad_first - mean), mix_grads)
        mix_grads = jnp.where(lane == 2 * c + 1, second * (grad_second - mean), mix_grads)
    residual_ref[...] = residual

    def returned(k, carried):
        g_copy(k).wait_recv()
        return carried

    lax.fori_loop(1, NFFN, returned, 0)
    ret = gret[...].reshape(NFFN * QUARTER, width + 128)
    score_out[...] = jnp.zeros_like(score_out)

    def give_scores(k, carried):
        slots = unpack3(gret[k, :, width:])
        row = jnp.sum(pick_ref[k].astype(f32) * slots, axis=0, keepdims=True)
        for q in range(MP):
            score_out[q, pl.ds(target(k), 1)] = row[:, q * rows : (q + 1) * rows]
        return carried

    lax.fori_loop(0, NFFN, give_scores, 0)
    score_copies = [
        remote(score_out.at[flip(mp_me, k)], score_in.at[k], ssend.at[k], srecv.at[k], mp=flip(mp_me, k))
        for k in range(1, MP)
    ]
    for copy in score_copies:
        copy.start()

    def grad_block(q):
        at = pl.ds(pl.multiple_of(q * rows, rows), rows)
        return dotf(
            pick_ref[:, :, at].reshape(NFFN * QUARTER, rows), ret[:, :width], TN
        )

    trip = Scatter(mp_me, core_out, ncore_in, chip_out, nchip_in, nsend, nrecv)
    normed_grad = trip.run(grad_block) + local_grad

    for copy in score_copies:
        copy.wait_recv()
    ffn_scores = (score_out[mp_me] + score_in[1]) + (score_in[2] + score_in[3])
    scores = local_scores.T[:16] + jnp.concatenate([ffn_scores, jnp.zeros((8, rows), f32)], axis=0)
    logit_grad = gates_t * (scores - jnp.sum(gates_t * scores, axis=0, keepdims=True))
    lgrad_ref[...] = lax.dot_general(
        carry, logit_grad, (((1,), (0,)), ((), ())),
        preferred_element_type=f32, precision=highest,
    )
    small_ref[24:40] = jnp.zeros((16, width), f32)
    small_ref[24:40, 0:16] = lax.dot_general(
        routing_ref[0:16, own_at], logit_grad, NT, preferred_element_type=f32, precision=highest
    )
    stacked = jnp.concatenate([logit_grad, mix_grads.T[:16]], axis=0)
    heads = params_ref[0:32]
    sublane = lax.broadcasted_iota(jnp.int32, (32, width), 0)
    heads = jnp.where(sublane < 20, heads, 0.0).astype(bf16)
    feature_grads = exact(stacked, n_bf)
    small_ref[0:20] = feature_grads[0:20]
    normed_grad = normed_grad + exact(stacked, heads, TN)
    scale = lax.rsqrt(jnp.mean(hidden * hidden, axis=-1, keepdims=True) + epsilon)
    scaled = hidden * scale
    small_ref[22:23] = jnp.sum(normed_grad * scaled, axis=0, keepdims=True)
    small_ref[23:24] = jnp.zeros((1, width), f32)
    weighted = normed_grad * params_ref[22:23]
    hidden_grad = cot + scale * (
        weighted - scaled * jnp.mean(weighted * scaled, axis=-1, keepdims=True)
    )
    hgrad_ref[...] = hidden_grad
    agrad_ref[...] = hidden_grad.astype(bf16)

    trip.drain()
    for copy in score_copies:
        copy.wait_send()

    def drain(k, carried):
        c_copy(k).wait_send()
        g_copy(k).wait_send()
        return carried

    lax.fori_loop(1, NFFN, drain, 0)
    if inside:
        for copy in weights:
            copy.wait_send()


def forward(x, cot, params, routing, wshard, win, wout, groups):
    rows, width = x.shape
    cos, sin = rope_constants()
    inside = groups == 1
    cols = wshard.shape[-1]
    depth = width // NFFN
    hidden_cols = win.shape[-1]
    heads = cols // 4 // HD
    everyone = MP * rows
    slots = NFFN * CAP
    wide = width + 128
    sd = jax.ShapeDtypeStruct
    vm = pltpu.VMEM
    dma = pltpu.SemaphoreType.DMA
    outs = [
        sd((MP, rows, width), bf16),
        sd((NFFN, depth, cols), bf16),
        sd((heads, SEQ, HD), bf16),
        sd((heads, SEQ, HD), bf16),
        sd((heads, SEQ, HD), bf16),
        sd((SEQ, heads * HD), bf16),
        sd((SEQ, 128), f32),
        sd((rows, width), f32),
        sd((rows, width), f32),
        sd((rows, width), bf16),
        sd((16, rows), f32),
        sd((40, width), f32),
        sd((NFFN, QUARTER, everyone), bf16),
        sd((NFFN, QUARTER, 128), f32),
        sd((NFFN, MP, QUARTER, width), bf16),
        sd((3, width, hidden_cols), bf16),
    ]
    if not inside:
        wshard = wshard.reshape(NFFN, depth, cols)
    return pl.pallas_call(
        functools.partial(forward_kernel, inside),
        out_shape=outs,
        in_specs=[VM] * 7 + [HB, HB],
        out_specs=[VM] * len(outs),
        scratch_shapes=[
            vm((MP, rows, width), bf16),
            vm((rows, width), f32),
            vm((rows, width), f32),
            vm((2, rows, width), bf16),
            vm((rows, width), bf16),
            vm((rows, width), bf16),
            vm((2, rows, width), bf16),
            vm((MP, rows, width), bf16),
            vm((16, everyone), f32),
            vm((16, everyone), f32),
            vm((16, everyone), f32),
            vm((NFFN, QUARTER, wide), bf16),
            vm((NFFN, QUARTER, width), bf16),
            vm((NFFN, MP, QUARTER, wide), bf16),
            vm((NFFN, MP, QUARTER, width), bf16),
            vm((slots, hidden_cols), bf16),
            vm((2, slots, hidden_cols), bf16),
            vm((MP, QUARTER, wide), f32),
            vm((4, 2, QUARTER, wide), f32),
            vm((4, 2, QUARTER, wide), bf16),
            vm((NFFN, 2, QUARTER, wide), bf16),
            vm((4, QUARTER, wide), bf16),
            vm((NFFN, QUARTER, wide), bf16),
            vm((NFFN, QUARTER, wide), bf16),
            vm((MP, 8, rows), f32),
            vm((MP, 8, rows), f32),
            vm((2, rows, width), bf16),
            vm((rows, width), bf16),
            dma((9,)), dma((9,)),
            dma((8,)), dma((8,)),
            dma((2, 8)), dma((2, 8)),
            dma((2,)),
            dma((3,)), dma((3,)),
            dma((8,)), dma((8,)),
            dma((8,)), dma((8,)),
            dma((8, 3)), dma((8, 3)),
            dma((8, 3)), dma((8, 3)),
            dma((8, 3)), dma((8, 3)),
            dma((8,)), dma((8,)),
            dma((4,)), dma((4,)),
            dma((3,)), dma((3,)),
        ],
        compiler_params=pltpu.CompilerParams(
            collective_id=0, has_side_effects=True, vmem_limit_bytes=60 * 2**20
        ),
        name="forward",
    )(x, cot, params, routing, jnp.asarray(cos), jnp.asarray(sin), wshard, win, wout)


def back_kernel(
    inside,
    agrad_ref, hgrad_ref, x_ref, params_ref, cos_ref, sin_ref, rows1_ref, w_ref, q_ref, k_ref, v_ref,
    mixed_ref, lse_ref, pick_ref, gate_ref, residual_ref, outp_ref, small_ref, dw_ref,
    output_ref, xgrad_ref, wgrad_ref, sums_ref, first_ref, dw_own,
    agrad_all, mgrad_ref, joint_ref, key_acc, value_acc, grads_ref, across_out, across_in,
    along_out, along_in, ret_ref, ocore_out, ocore_in, ochip_out, ochip_in,
    xcore_out, xcore_in, xchip_out, xchip_in, sum_out, sum_in, first_mp, first_dp, first_out,
    pcore_in, pchip_out, pchip_in, outq_ref,
    asend, arecv, osend, orecv, esend, erecv, psend, precv, local, rsend, rrecv, xsend, xrecv,
    wsend, wrecv, ssend, srecv, fsend, frecv,
):
    mp_me = lax.axis_index("mp")
    dp_me = lax.axis_index("dp")
    near = lax.rem(dp_me, NFFN)
    base = dp_me - near
    rows, width = agrad_ref.shape
    everyone = MP * rows
    heads = q_ref.shape[0]
    cols = heads * HD
    greet(mp_me, near, base)

    agrad_all[mp_me] = agrad_ref[...]
    gather = Gather(agrad_all, mp_me, asend, arecv)
    gather.start()
    core, chip, far = flip(mp_me, 1), flip(mp_me, 2), flip(mp_me, 3)
    din = dw_own.shape[2]

    def rows_of(index):
        return pl.ds(pl.multiple_of(index * din, din), din)

    if inside:
        moved = [
            remote(dw_ref.at[:, rows_of(flip(near, k))], dw_own.at[near], esend.at[k],
                   erecv.at[k], dp=base + flip(near, k))
            for k in (4, 6, 5, 7, 2, 3, 1)
        ]
        mine = [pltpu.make_async_copy(dw_ref.at[:, rows_of(near)], dw_own.at[near], local.at[0])]
    else:
        moved = []
        mine = [
            pltpu.make_async_copy(dw_ref.at[:, rows_of(p)], dw_own.at[p], local.at[p])
            for p in range(NFFN)
        ]
    for copy in moved + mine:
        copy.start()

    p_core = [
        remote(outp_ref.at[:, far], pcore_in.at[0], psend.at[0], precv.at[0], mp=core),
        remote(outp_ref.at[:, core], pcore_in.at[1], psend.at[1], precv.at[1], mp=core),
    ]
    for copy in p_core:
        copy.start()
    parts = (slice(4, 8), slice(0, 4))
    p_chip = [
        remote(pchip_out.at[part], pchip_in.at[part], psend.at[2 + j], precv.at[2 + j], mp=chip)
        for j, part in enumerate(parts)
    ]
    returns = {
        k: remote(outq_ref.at[k], ret_ref.at[k], osend.at[k], orecv.at[k],
                  dp=base + lax.rem(near - k + NFFN, NFFN))
        for k in range(1, NFFN)
    }

    def results_across():
        p_core[0].wait_recv()
        for j, part in enumerate(parts):
            pchip_out[part] = (
                outp_ref[part, chip].astype(f32) + pcore_in[0, part].astype(f32)
            ).astype(bf16)
            p_chip[j].start()

    def results_away(j):
        part = parts[j]
        if j == 0:
            p_core[1].wait_recv()
        p_chip[j].wait_recv()
        outq_ref[part] = (
            outp_ref[part, mp_me].astype(f32)
            + (pcore_in[1, part].astype(f32) + pchip_in[part].astype(f32))
        ).astype(bf16)
        for k in range(part.start, part.stop):
            if k > 0:
                returns[k].start()
            else:
                ret_ref[0] = outq_ref[0]

    sum_out[0] = small_ref[...]
    places = [{"mp": flip(mp_me, 1)}, {"mp": flip(mp_me, 2)}] + [
        {"dp": base + flip(near, k)} for k in (1, 2, 4)
    ]
    stages = [
        remote(sum_out.at[j], sum_in.at[j], ssend.at[j], srecv.at[j], **where)
        for j, where in enumerate(places)
    ]

    def stage(j):
        if j > 0:
            stages[j - 1].wait_recv()
            total = sum_out[j - 1] + sum_in[j - 1]
            if j == len(stages):
                sums_ref[...] = total
                return
            sum_out[j] = total
        stages[j].start()

    stage(0)
    gather.forward()
    stage(1)
    gather.finish()

    w_all = w_ref[...].reshape(width, w_ref.shape[2])
    out_weight = w_all[:, 3 * cols :]
    for i in range(MP):
        mgrad_ref[i * rows : (i + 1) * rows] = dotf(agrad_all[i], out_weight).astype(bf16)
    grads_ref[:, 3 * cols :] = dotf(agrad_all[...].reshape(everyone, width), mixed_ref[...], TN)

    combine = Scatter(mp_me, ocore_out, ocore_in, ochip_out, ochip_in, rsend, rrecv)

    def out_block(q):
        at = pl.ds(pl.multiple_of(q * rows, rows), rows)
        weighted = (ret_ref[...].astype(f32) * gate_ref[:, :, 0:1]).astype(bf16)
        return dotf(
            pick_ref[:, :, at].reshape(NFFN * QUARTER, rows),
            weighted.reshape(NFFN * QUARTER, width), TN,
        )

    def head_back(h):
        lanes = slice(h * HD, (h + 1) * HD)
        for b in range(MP):
            at = slice(b * rows, (b + 1) * rows)
            seen = (b + 1) * rows
            query = q_ref[h, at]
            keys = k_ref[h, :seen]
            out_grad = mgrad_ref[at, lanes]
            scores = dotf(query, keys, NT) * HD**-0.5
            allowed = b * rows + lax.broadcasted_iota(
                jnp.int32, (rows, seen), 0
            ) >= lax.broadcasted_iota(jnp.int32, (rows, seen), 1)
            probs = jnp.where(allowed, jnp.exp(scores - lse_ref[at, h : h + 1]), 0.0)
            probs_grad = dotf(out_grad, v_ref[h, :seen], NT)
            inner = jnp.sum(probs * probs_grad, axis=1, keepdims=True)
            score_grad = (probs * (probs_grad - inner)).astype(bf16)
            query_grad = dotf(score_grad, keys) * HD**-0.5
            joint_ref[at, lanes] = (
                query_grad * cos_ref[at] - swap_halves(query_grad) * sin_ref[at]
            ).astype(bf16)
            key_grad = dotf(score_grad, query, TN) * HD**-0.5
            value_grad = dotf(probs.astype(bf16), out_grad, TN)
            if b == 0:
                key_acc[...] = jnp.zeros_like(key_acc)
                value_acc[...] = jnp.zeros_like(value_acc)
            key_acc[:seen] += key_grad
            value_acc[:seen] += value_grad
        key_grad = key_acc[...]
        joint_ref[:, cols + h * HD : cols + (h + 1) * HD] = (
            key_grad * cos_ref[...] - swap_halves(key_grad) * sin_ref[...]
        ).astype(bf16)
        joint_ref[:, 2 * cols + h * HD : 2 * cols + (h + 1) * HD] = value_acc[...].astype(bf16)

    last = heads - 1
    for h in range(heads):
        head_back(h)
        if h == 0:
            stage(2)
            results_across()
        if h == min(1, last):
            results_away(0)
        if h == last:
            stage(3)
            results_away(1)

    depth = width // NFFN
    grads_ref[:, : 3 * cols] = dotf(
        rows1_ref[...].reshape(everyone, width), joint_ref[...], TN
    )
    if inside:
        lean = lax.rem(near, 2)
        tall = grads_ref[...].reshape(NFFN // 2, 2, depth, grads_ref.shape[1])
        keep = jnp.where(lean == 0, tall[:, 0], tall[:, 1])
        across_out[...] = jnp.where(lean == 0, tall[:, 1], tall[:, 0]).astype(bf16)
        over = remote(across_out, across_in, wsend.at[0], wrecv.at[0], dp=base + flip(near, 1))
        over.start()
    else:
        wgrad_ref[...] = grads_ref[...]
    stage(4)

    trip = Scatter(mp_me, xcore_out, xcore_in, xchip_out, xchip_in, xsend, xrecv)

    def x_block(q):
        at = pl.ds(pl.multiple_of(q * rows, rows), rows)
        return dotf(joint_ref[at], w_all[:, : 3 * cols], NT)

    normed_grad = trip.run(x_block)
    if inside:
        over.wait_recv()
        along_out[...] = (keep + across_in[...].astype(f32)).astype(bf16)
        up = near // 2
        alongs = [
            remote(along_out.at[flip(near, k) // 2], along_in.at[k // 2], wsend.at[k], wrecv.at[k],
                   dp=base + flip(near, k))
            for k in (4, 6, 2)
        ]
        for copy in alongs:
            copy.start()
    tokens = x_ref[...].astype(f32)
    scale = lax.rsqrt(jnp.mean(tokens * tokens, axis=-1, keepdims=True) + epsilon)
    scaled = tokens * scale
    first_out[0] = jnp.sum(normed_grad * scaled, axis=0, keepdims=True)
    firsts = [
        remote(first_out.at[0], first_mp.at[k], fsend.at[k], frecv.at[k], mp=flip(mp_me, k))
        for k in range(1, MP)
    ]
    for copy in firsts:
        copy.start()
    weighted = normed_grad * params_ref[23:24]
    xgrad_ref[...] = hgrad_ref[...] + scale * (
        weighted - scaled * jnp.mean(weighted * scaled, axis=-1, keepdims=True)
    )
    for copy in firsts:
        copy.wait_recv()
    first_out[1] = first_out[0] + first_mp[1] + first_mp[2] + first_mp[3]
    seconds = [
        remote(first_out.at[1], first_dp.at[k], fsend.at[MP + k], frecv.at[MP + k],
               dp=base + flip(near, k))
        for k in range(1, NFFN)
    ]
    for copy in seconds:
        copy.start()
    stage(5)
    for copy in returns.values():
        copy.wait_recv()
    routed = combine.run(out_block)
    output_ref[...] = (residual_ref[...] + routed).astype(bf16)
    if inside:
        for copy in alongs:
            copy.wait_recv()
        wgrad_ref[...] = along_out[up].astype(f32) + (
            along_in[1].astype(f32) + along_in[2].astype(f32) + along_in[3].astype(f32)
        )
    for copy in seconds:
        copy.wait_recv()
    total = first_out[1]
    for k in range(1, NFFN):
        total = total + first_dp[k]
    first_ref[...] = total

    for copy in moved:
        copy.wait_recv()
    for copy in mine:
        copy.wait()
    if inside:
        for copy in [over] + alongs:
            copy.wait_send()
    for copy in moved + p_core + p_chip + list(returns.values()) + stages + firsts + seconds:
        copy.wait_send()
    combine.drain()
    trip.drain()


def attention_back(
    agrad, hgrad, x, params, rows1, w, q, k, v, mixed, lse, pick, gate, residual, outp, small, dw,
    groups,
):
    rows, width = x.shape
    everyone = MP * rows
    cos, sin = rope_constants()
    inside = groups == 1
    cols = w.shape[-1]
    heads = q.shape[0]
    depth = width // NFFN
    hidden_cols = dw.shape[-1]
    sd = jax.ShapeDtypeStruct
    vm = pltpu.VMEM
    dma = pltpu.SemaphoreType.DMA
    outs = [
        sd((rows, width), bf16),
        sd((rows, width), f32),
        sd((depth if inside else width, cols), f32),
        sd((40, width), f32),
        sd((1, width), f32),
        sd((NFFN, 3, depth, hidden_cols), bf16),
    ]
    return pl.pallas_call(
        functools.partial(back_kernel, inside),
        out_shape=outs,
        in_specs=[VM] * 19,
        out_specs=[VM] * 5 + [HB],
        scratch_shapes=[
            vm((MP, rows, width), bf16),
            vm((everyone, heads * HD), bf16),
            vm((everyone, 3 * heads * HD), bf16),
            vm((everyone, HD), f32),
            vm((everyone, HD), f32),
            vm((width, cols), f32),
            vm((NFFN // 2, depth, cols), bf16),
            vm((NFFN // 2, depth, cols), bf16),
            vm((NFFN // 2, depth, cols), bf16),
            vm((NFFN // 2, depth, cols), bf16),
            vm((NFFN, QUARTER, width), bf16),
            vm((2, rows, width), bf16),
            vm((2, rows, width), bf16),
            vm((rows, width), bf16),
            vm((rows, width), bf16),
            vm((2, rows, width), bf16),
            vm((2, rows, width), bf16),
            vm((rows, width), bf16),
            vm((rows, width), bf16),
            vm((5, 40, width), f32),
            vm((5, 40, width), f32),
            vm((MP, 1, width), f32),
            vm((NFFN, 1, width), f32),
            vm((2, 1, width), f32),
            vm((2, NFFN, QUARTER, width), bf16),
            vm((NFFN, QUARTER, width), bf16),
            vm((NFFN, QUARTER, width), bf16),
            vm((NFFN, QUARTER, width), bf16),
            dma((3,)), dma((3,)),
            dma((8,)), dma((8,)),
            dma((8,)), dma((8,)),
            dma((4,)), dma((4,)), dma((8,)),
            dma((3,)), dma((3,)),
            dma((3,)), dma((3,)),
            dma((8,)), dma((8,)),
            dma((5,)), dma((5,)),
            dma((MP + NFFN,)), dma((MP + NFFN,)),
        ],
        compiler_params=pltpu.CompilerParams(
            collective_id=1, has_side_effects=True, vmem_limit_bytes=60 * 2**20
        ),
        name="attention_backward",
    )(
        agrad, hgrad, x, params, jnp.asarray(cos), jnp.asarray(sin), rows1, w, q, k, v, mixed, lse,
        pick, gate, residual, outp, small, dw,
    )


def clusters():
    groups = lax.axis_size("dp") // NFFN
    near = [[group * NFFN + expert for expert in range(NFFN)] for group in range(groups)]
    far = [[group * NFFN + expert for group in range(groups)] for expert in range(NFFN)]
    return groups, near, far


def exchange(shard, dim):
    _, near, far = clusters()
    own = lax.all_to_all(shard, "dp", 0, dim, axis_index_groups=near, tiled=True)
    return lax.all_gather(own, "dp", axis=dim, axis_index_groups=far, tiled=True)


def exchange_back(grads, dim):
    _, near, far = clusters()
    grads = lax.psum_scatter(
        grads.astype(f32), "dp", scatter_dimension=dim, axis_index_groups=far, tiled=True
    )
    return lax.all_to_all(grads.astype(bf16), "dp", dim, 0, axis_index_groups=near, tiled=True)


def per_device(
    inputs,
    query_key_value,
    output_weight,
    expert_input,
    expert_output,
    first_gain,
    second_gain,
    router_weight,
    logit_carry,
    constant_mix,
    constant_values,
    previous_logits,
    routes,
    cotangent,
):
    rows, width = inputs.shape
    groups, _, far = clusters()

    def padded(array, high, wide, value=0.0):
        return jnp.pad(
            array.astype(f32), ((0, high - array.shape[0]), (0, wide - array.shape[1])),
            constant_values=value,
        )

    params = jnp.concatenate(
        [
            padded(router_weight.T, 16, width),
            constant_mix.T.astype(f32),
            constant_values.astype(f32),
            second_gain.astype(f32)[None],
            first_gain.astype(f32)[None],
            padded(logit_carry, 16, width),
        ],
        axis=0,
    )
    everyone = rows * MP
    routing = jnp.concatenate(
        [padded(previous_logits.T, 16, everyone), padded(routes.T, 8, everyone, -1.0)], axis=0
    )
    shard_depth = query_key_value.shape[0]
    shard = jnp.concatenate(
        [query_key_value.reshape(shard_depth, -1), output_weight.T], axis=1
    )
    cols = output_weight.shape[0]
    expert_output_t = expert_output.transpose(0, 2, 1)
    if groups > 1:
        shard = lax.all_gather(shard, "dp", axis=0, tiled=True)
        win = exchange(expert_input, 2)[0]
        wout = exchange(expert_output_t, 1)[0]
    if groups == 1:
        win, wout = expert_input, expert_output_t
    (rows1, w, q, k, v, mixed, lse, residual, hidden_grad, attended_grad, logits_grad, small, pick,
     gate, outp, dw) = forward(
        inputs, cotangent, params, routing, shard, win, wout, groups
    )
    output, input_grad, weight_grad, sums, first_grad, expert_grad = attention_back(
        attended_grad, hidden_grad, inputs, params, rows1, w, q, k, v, mixed, lse, pick, gate,
        residual, outp, small, dw, groups,
    )
    if groups > 1:
        weight_grad = lax.psum_scatter(weight_grad, "dp", scatter_dimension=0, tiled=True)
        whole = expert_grad.transpose(1, 0, 2, 3).reshape(1, 3, width, -1)
        expert_grad = exchange_back(whole, 2)
        sums, first_grad = lax.psum((sums, first_grad), "dp", axis_index_groups=far)
    expert_in_grad = expert_grad[:, :2].astype(f32)
    expert_out_grad = expert_grad[:, 2].transpose(0, 2, 1).astype(f32)
    return (
        output,
        input_grad,
        logits_grad[:NEXP].T,
        weight_grad[:, : 3 * cols].reshape(shard_depth, 3, cols),
        weight_grad[:, 3 * cols :].T,
        expert_in_grad,
        expert_out_grad,
        first_grad[0],
        sums[22],
        sums[:NEXP].T,
        sums[24 : 24 + NEXP, :NEXP],
        sums[16:20].T,
        sums[20:22],
    )


def solution(mesh):
    in_specs = (
        P(("dp", "mp"), None),
        P("dp", None, "mp"),
        P("mp", "dp"),
        P(None, None, "dp", "mp"),
        P(None, "mp", "dp"),
        P(),
        P(),
        P(),
        P(),
        P(),
        P(),
        P("dp", None),
        P("dp", None),
        P(("dp", "mp"), None),
    )
    out_specs = (
        P(("dp", "mp"), None),
        P(("dp", "mp"), None),
        P(("dp", "mp"), None),
        P("dp", None, "mp"),
        P("mp", "dp"),
        P(None, None, "dp", "mp"),
        P(None, "mp", "dp"),
        P(),
        P(),
        P(),
        P(),
        P(),
        P(),
    )
    return jax.shard_map(
        per_device, mesh=mesh, in_specs=in_specs, out_specs=out_specs, check_vma=False
    )
```

time: 361 us -> 327 us (0.906)
  Pallas kernels: 326 us -> 296 us
  local copies, waits for them, and re-layouts: 26.8 us -> 19.4 us
  other arithmetic: 5.55 us -> 10.4 us
    pallas_call x2 -> x1, Pallas kernels: 214 us -> 190 us  [forward(): pl.pallas_call(functools.partial(forward_kernel, inside), out_shape=outs,...]
    pad x8 -> x1, local copies, waits for them, and re-layouts: 7.86 us -> 0.7 us  [padded(): jnp.pad(array.astype(f32), ((0, high - array.shape[0]), (0, wide - array....]
    pallas_call x1, Pallas kernels: 112 us -> 106 us  [attention_back(): pl.pallas_call(functools.partial(back_kernel, inside), out_shape=outs, in...]
where the time goes in v4:
time: 327 us; the launch traced here: 326 us
  Pallas kernels  296 us (91%)
  local copies, waits for them, and re-layouts  19.4 us (6%)
  other arithmetic  10.4 us (3%)
    pallas_call x1, Pallas kernels, forward(): pl.pallas_call(functools.partial(forward_kernel, inside), out_shape=outs,...  190 us
    pallas_call x1, Pallas kernels, attention_back(): pl.pallas_call(functools.partial(back_kernel, inside), out_shape=outs, in...  106 us

profile of v4, /device:TPU:0, one launch (start us, length us, event | category | flops | bytes accessed | tf_op | source)
XLA Modules:
  0.0 326.5 jit_solution(18089068759212463414)
XLA Ops:
  0.6 0.7 reshape.37
  1.3 0.7 reshape.36
  2.0 0.7 convert_bitcast_fusion.2
  2.7 0.7 convert_bitcast_fusion.1
  3.4 0.9 copy.36
  4.3 0.7 pad_convert_fusion
  5.1 0.7 pad.21
  5.8 2.6 concatenate.9.params_ref
  8.3 1.5 select_maximum_fusion.routing_ref
  9.8 1.1 copy.35
  10.9 0.2 copy.37
  11.0 0.8 pad_maximum_fusion.wshard_ref
  11.8 189.5 %forward.1 = (bf16[4,256,768]{2,1,0:T(8,128)(2,1)}, bf16[8,96,768]{2,1,0:T(8,128)(2,1)}, bf16[3,1024,64]{2,1,0:T(8,128)(2,1)}, bf16[3,1024,64]{2,1,0:T(8,128)(2,...) custom-call(bf16[256,768]{1,0:T(8,128)(2,1)} %x_ref.3, ...), custom_call_target="tpu_custom_call" | custom-call | tf_op jit(solution)/shard_map/forward/pallas_call | solution.py:708
  201.3 0.0 copy-start.3
  201.3 106.4 %attention_backward.1 = (bf16[256,768]{1,0:T(8,128)(2,1)}, f32[256,768]{1,0:T(8,128)}, f32[96,768]{1,0:T(8,128)}, f32[40,768]{1,0:T(8,128)}, f32[1,768]{1,0:T(1,128)}, /*index=5*/bf16[8,3,96,512]{3,2,1,0:T(8,128)(2,1)}) custom-call(bf16[256,768]{1,0:T(8,128)(2,1)} %get-tuple-element.35.agrad_ref, f32[256,768]{1,0:T(8,128)} %get-tuple-element.36.hgrad_ref, ...), custom_call_target="tpu_custom_call" | custom-call | tf_op jit(solution)/shard_map/attention_backward/pallas_call | solution.py:1046
  307.8 0.0 copy-start
  307.8 1.4 reduce
  309.2 1.3 slice_reduce_fusion
  310.6 1.3 slice.39
  311.9 1.3 slice.37
  313.2 1.3 slice_bitcast_fusion.3
  314.5 1.4 slice_bitcast_fusion.1
  315.9 0.6 slice_bitcast_fusion.2
  316.6 1.0 slice_bitcast_fusion
  317.5 1.0 slice.31
  318.5 0.7 copy.40
  319.2 0.1 copy.38
  319.4 0.9 copy.39
  320.3 2.5 convert_bitcast_fusion
  322.8 2.1 slice_convert_fusion
  324.9 0.7 copy.43
  325.6 0.9 copy.44
  (6 shorter events, 0.0 us)
Async XLA Ops:
  201.3 114.6 %copy-start.3 = (f32[16,256]{1,0:T(8,128)S(1)}, f32[16,256]{1,0:T(8,128)}, u32[]{:S(2)}) copy-start(f32[16,256]{1,0:T(8,128)} %get-tuple-element.52) | copy-start | bytes 49156
  307.8 15.0 %copy-start = (bf16[8,3,96,512]{3,2,1,0:T(8,128)(2,1)S(1)}, bf16[8,3,96,512]{3,2,1,0:T(8,128)(2,1)}, u32[]{:S(2)}) copy-start(bf16[8,3,96,512]{3,2,1,0:T(8,128)(2,1)} %get-tuple-element.54) | copy-start | bytes 7077892
  322.8 2.1 copy-start.2
  322.8 2.8 copy-start.1

commit v5 on v4

--- a/solution.py
+++ b/solution.py
@@ -14,6 +14,8 @@
 CAP = 256
 MP = 4
 QUARTER = CAP // MP
+WIDE = 640
+VMEM_LIMIT = 62 * 2**20
 
 epsilon = 1e-06
 rope_base = 10000.0
@@ -155,19 +157,27 @@
             copy.wait_send()
 
 
-def forward_kernel(
+def layer_kernel(
     inside,
     x_ref, cot_ref, params_ref, routing_ref, cos_ref, sin_ref, wshard_ref, win_shard, wout_shard,
-    rows1_ref, w_ref, q_ref, k_ref, v_ref, mixed_ref, lse_ref,
-    residual_ref, hgrad_ref, agrad_ref, lgrad_ref, small_ref, pick_ref, gate_ref, outp_ref, dw_ref,
+    output_ref, xgrad_ref, lgrad_ref, wgrad_ref, sums_ref, first_ref, dw_own,
+    rows1_ref, w_ref, q_ref, k_ref, v_ref, mixed_ref, lse_ref, pick_ref, gate_ref, outp_ref, dw_ref,
     rows2_ref, hidden_ref, sum_ref, core_in, chip_out, chip_in, core_out,
-    cot_all, place_ref, gates_ref, prior_ref, msgx, msgc, xs, cs, units_ref, pgrad_ref,
+    place_ref, gates_ref, prior_ref, msgx, msgc, xs, cs, units_ref, pgrad_ref,
     part_ref, keep_ref, gcore_out, gcore_in, gchip_out, gchip_in, gret, score_out, score_in,
     ncore_in, nchip_in,
+    key_acc, value_acc, grads_ref, across_out, across_in, along_in, ret_ref,
+    sum_out, sum_in, first_mp, first_dp, first_out,
     sends, recvs, wsend, wrecv, esend, erecv, local,
     csend, crecv, xsend, xrecv, dsend, drecv, xgs, xgr, cgs, cgr, gsend, grecv,
     rsend, rrecv, ssend, srecv, nsend, nrecv,
+    asend, arecv, osend, orecv, msend, mrecv, psend, precv, mlocal, bsend, brecv, tsend, trecv,
+    vsend, vrecv, zsend, zrecv, fsend, frecv,
 ):
+    cot_all = rows2_ref
+    residual_ref = sum_ref
+    hgrad_ref = xgrad_ref
+    small_ref = sum_out.at[0]
     mp_me = lax.axis_index("mp")
     dp_me = lax.axis_index("dp")
     near = lax.rem(dp_me, NFFN)
@@ -556,6 +566,27 @@
 
     lax.fori_loop(0, width // 128, weights_step, 0)
 
+    din = dw_own.shape[2]
+
+    def rows_of(index):
+        return pl.ds(pl.multiple_of(index * din, din), din)
+
+    if inside:
+        moved = [
+            remote(dw_ref.at[:, rows_of(flip(near, k))], dw_own.at[near], msend.at[k],
+                   mrecv.at[k], dp=base + flip(near, k))
+            for k in (4, 6, 5, 7, 2, 3, 1)
+        ]
+        kept = [pltpu.make_async_copy(dw_ref.at[:, rows_of(near)], dw_own.at[near], mlocal.at[0])]
+    else:
+        moved = []
+        kept = [
+            pltpu.make_async_copy(dw_ref.at[:, rows_of(p)], dw_own.at[p], mlocal.at[p])
+            for p in range(NFFN)
+        ]
+    for copy in moved + kept:
+        copy.start()
+
     n_bf = rows2_ref[mp_me]
     n = n_bf.astype(f32)
     cot = cot_ref[...].astype(f32)
@@ -639,12 +670,12 @@
         routing_ref[0:16, own_at], logit_grad, NT, preferred_element_type=f32, precision=highest
     )
     stacked = jnp.concatenate([logit_grad, mix_grads.T[:16]], axis=0)
-    heads = params_ref[0:32]
+    stack = params_ref[0:32]
     sublane = lax.broadcasted_iota(jnp.int32, (32, width), 0)
-    heads = jnp.where(sublane < 20, heads, 0.0).astype(bf16)
+    stack = jnp.where(sublane < 20, stack, 0.0).astype(bf16)
     feature_grads = exact(stacked, n_bf)
     small_ref[0:20] = feature_grads[0:20]
-    normed_grad = normed_grad + exact(stacked, heads, TN)
+    normed_grad = normed_grad + exact(stacked, stack, TN)
     scale = lax.rsqrt(jnp.mean(hidden * hidden, axis=-1, keepdims=True) + epsilon)
     scaled = hidden * scale
     small_ref[22:23] = jnp.sum(normed_grad * scaled, axis=0, keepdims=True)
@@ -654,7 +685,9 @@
         weighted - scaled * jnp.mean(weighted * scaled, axis=-1, keepdims=True)
     )
     hgrad_ref[...] = hidden_grad
-    agrad_ref[...] = hidden_grad.astype(bf16)
+    rows2_ref[mp_me] = hidden_grad.astype(bf16)
+    agather = Gather(rows2_ref, mp_me, asend, arecv)
+    agather.start()
 
     trip.drain()
     for copy in score_copies:
@@ -670,8 +703,228 @@
         for copy in weights:
             copy.wait_send()
 
-
-def forward(x, cot, params, routing, wshard, win, wout, groups):
+    p_core = [
+        remote(outp_ref.at[:, far], cs.at[:, 0], psend.at[0], precv.at[0], mp=core),
+        remote(outp_ref.at[:, core], cs.at[:, 1], psend.at[1], precv.at[1], mp=core),
+    ]
+    for copy in p_core:
+        copy.start()
+    parts = (slice(4, 8), slice(0, 4))
+    p_chip = [
+        remote(cs.at[part, 3], cs.at[part, 2], psend.at[2 + j], precv.at[2 + j], mp=chip)
+        for j, part in enumerate(parts)
+    ]
+    returns = {
+        k: remote(msgc.at[k], ret_ref.at[k], osend.at[k], orecv.at[k],
+                  dp=base + lax.rem(near - k + NFFN, NFFN))
+        for k in range(1, NFFN)
+    }
+
+    def results_across():
+        p_core[0].wait_recv()
+        for j, part in enumerate(parts):
+            cs[part, 3] = (
+                outp_ref[part, chip].astype(f32) + cs[part, 0].astype(f32)
+            ).astype(bf16)
+            p_chip[j].start()
+
+    def results_away(j):
+        part = parts[j]
+        if j == 0:
+            p_core[1].wait_recv()
+        p_chip[j].wait_recv()
+        msgc[part] = (
+            outp_ref[part, mp_me].astype(f32)
+            + (cs[part, 1].astype(f32) + cs[part, 2].astype(f32))
+        ).astype(bf16)
+        for k in range(part.start, part.stop):
+            if k > 0:
+                returns[k].start()
+            else:
+                ret_ref[0] = msgc[0]
+
+    places = [{"mp": flip(mp_me, 1)}, {"mp": flip(mp_me, 2)}] + [
+        {"dp": base + flip(near, k)} for k in (1, 2, 4)
+    ]
+    stages = [
+        remote(sum_out.at[j], sum_in.at[j], zsend.at[j], zrecv.at[j], **where)
+        for j, where in enumerate(places)
+    ]
+
+    def stage(j):
+        if j > 0:
+            stages[j - 1].wait_recv()
+            total = sum_out[j - 1] + sum_in[j - 1]
+            if j == len(stages):
+                sums_ref[...] = total
+                return
+            sum_out[j] = total
+        stages[j].start()
+
+    stage(0)
+    agather.forward()
+    stage(1)
+    agather.finish()
+
+    w_all = w_ref[...].reshape(width, w_ref.shape[2])
+    out_weight = w_all[:, 3 * cols :]
+    for i in range(MP):
+        xs[i, :, :, WIDE : WIDE + cols] = (
+            dotf(rows2_ref[i], out_weight).astype(bf16).reshape(MP, QUARTER, cols)
+        )
+    grads_ref[:, 3 * cols :] = dotf(rows2_ref[...].reshape(everyone, width), mixed_ref[...], TN)
+
+    combine = Scatter(mp_me, core_out, ncore_in, chip_out, nchip_in, bsend, brecv)
+
+    def out_block(q):
+        at = pl.ds(pl.multiple_of(q * rows, rows), rows)
+        weighted = (ret_ref[...].astype(f32) * gate_ref[:, :, 0:1]).astype(bf16)
+        return dotf(
+            pick_ref[:, :, at].reshape(NFFN * QUARTER, rows),
+            weighted.reshape(NFFN * QUARTER, width), TN,
+        )
+
+    def head_back(h):
+        lanes = slice(h * HD, (h + 1) * HD)
+        for b in range(MP):
+            at = slice(b * rows, (b + 1) * rows)
+            seen = (b + 1) * rows
+            query = q_ref[h, at]
+            keys = k_ref[h, :seen]
+            out_grad = xs[b, :, :, WIDE + h * HD : WIDE + (h + 1) * HD].reshape(rows, HD)
+            scores = dotf(query, keys, NT) * HD**-0.5
+            allowed = b * rows + lax.broadcasted_iota(
+                jnp.int32, (rows, seen), 0
+            ) >= lax.broadcasted_iota(jnp.int32, (rows, seen), 1)
+            probs = jnp.where(allowed, jnp.exp(scores - lse_ref[at, h : h + 1]), 0.0)
+            probs_grad = dotf(out_grad, v_ref[h, :seen], NT)
+            inner = jnp.sum(probs * probs_grad, axis=1, keepdims=True)
+            score_grad = (probs * (probs_grad - inner)).astype(bf16)
+            query_grad = dotf(score_grad, keys) * HD**-0.5
+            xs[b, :, :, lanes] = (
+                (query_grad * cos_ref[at] - swap_halves(query_grad) * sin_ref[at])
+                .astype(bf16)
+                .reshape(MP, QUARTER, HD)
+            )
+            key_grad = dotf(score_grad, query, TN) * HD**-0.5
+            value_grad = dotf(probs.astype(bf16), out_grad, TN)
+            if b == 0:
+                key_acc[...] = jnp.zeros_like(key_acc)
+                value_acc[...] = jnp.zeros_like(value_acc)
+            key_acc[:seen] += key_grad
+            value_acc[:seen] += value_grad
+        key_grad = key_acc[...]
+        key_grad = key_grad * cos_ref[...] - swap_halves(key_grad) * sin_ref[...]
+        xs[0:MP, :, :, cols + h * HD : cols + (h + 1) * HD] = key_grad.astype(bf16).reshape(
+            MP, MP, QUARTER, HD
+        )
+        xs[0:MP, :, :, 2 * cols + h * HD : 2 * cols + (h + 1) * HD] = (
+            value_acc[...].astype(bf16).reshape(MP, MP, QUARTER, HD)
+        )
+
+    last = heads - 1
+    for h in range(heads):
+        head_back(h)
+        if h == 0:
+            stage(2)
+            results_across()
+        if h == min(1, last):
+            results_away(0)
+        if h == last:
+            stage(3)
+            results_away(1)
+
+    depth = width // NFFN
+    grads_ref[:, : 3 * cols] = dotf(
+        rows1_ref[...].reshape(everyone, width),
+        xs[0:MP, :, :, 0 : 3 * cols].reshape(everyone, 3 * cols), TN,
+    )
+    if inside:
+        lean = lax.rem(near, 2)
+        tall = grads_ref[...].reshape(NFFN // 2, 2, depth, grads_ref.shape[1])
+        keep = jnp.where(lean == 0, tall[:, 0], tall[:, 1])
+        across_out[...] = jnp.where(lean == 0, tall[:, 1], tall[:, 0]).astype(bf16)
+        over = remote(across_out, across_in, vsend.at[0], vrecv.at[0], dp=base + flip(near, 1))
+        over.start()
+    else:
+        wgrad_ref[...] = grads_ref[...]
+    stage(4)
+
+    home = Scatter(mp_me, core_out, core_in, chip_out, chip_in, tsend, trecv)
+
+    def x_block(q):
+        joint = xs[q, :, :, 0 : 3 * cols].reshape(rows, 3 * cols)
+        return dotf(joint, w_all[:, : 3 * cols], NT)
+
+    normed_grad = home.run(x_block)
+    home.drain()
+    if inside:
+        over.wait_recv()
+        over.wait_send()
+        across_out[...] = (keep + across_in[...].astype(f32)).astype(bf16)
+        up = near // 2
+        alongs = [
+            remote(across_out.at[flip(near, k) // 2], along_in.at[k // 2], vsend.at[k], vrecv.at[k],
+                   dp=base + flip(near, k))
+            for k in (4, 6, 2)
+        ]
+        for copy in alongs:
+            copy.start()
+    tokens = x_ref[...].astype(f32)
+    scale = lax.rsqrt(jnp.mean(tokens * tokens, axis=-1, keepdims=True) + epsilon)
+    scaled = tokens * scale
+    first_out[0] = jnp.sum(normed_grad * scaled, axis=0, keepdims=True)
+    firsts = [
+        remote(first_out.at[0], first_mp.at[k], fsend.at[k], frecv.at[k], mp=flip(mp_me, k))
+        for k in range(1, MP)
+    ]
+    for copy in firsts:
+        copy.start()
+    weighted = normed_grad * params_ref[23:24]
+    xgrad_ref[...] = hgrad_ref[...] + scale * (
+        weighted - scaled * jnp.mean(weighted * scaled, axis=-1, keepdims=True)
+    )
+    for copy in firsts:
+        copy.wait_recv()
+    first_out[1] = first_out[0] + first_mp[1] + first_mp[2] + first_mp[3]
+    seconds = [
+        remote(first_out.at[1], first_dp.at[k], fsend.at[MP + k], frecv.at[MP + k],
+               dp=base + flip(near, k))
+        for k in range(1, NFFN)
+    ]
+    for copy in seconds:
+        copy.start()
+    stage(5)
+    for copy in returns.values():
+        copy.wait_recv()
+    routed = combine.run(out_block)
+    output_ref[...] = (residual_ref[...] + routed).astype(bf16)
+    if inside:
+        for copy in alongs:
+            copy.wait_recv()
+        wgrad_ref[...] = across_out[up].astype(f32) + (
+            along_in[1].astype(f32) + along_in[2].astype(f32) + along_in[3].astype(f32)
+        )
+    for copy in seconds:
+        copy.wait_recv()
+    total = first_out[1]
+    for k in range(1, NFFN):
+        total = total + first_dp[k]
+    first_ref[...] = total
+
+    for copy in moved:
+        copy.wait_recv()
+    for copy in kept:
+        copy.wait()
+    if inside:
+        for copy in alongs:
+            copy.wait_send()
+    for copy in moved + p_core + p_chip + list(returns.values()) + stages + firsts + seconds:
+        copy.wait_send()
+    combine.drain()
+
+
+def layer(x, cot, params, routing, wshard, win, wout, groups):
     rows, width = x.shape
     cos, sin = rope_constants()
     inside = groups == 1
@@ -686,31 +939,33 @@
     vm = pltpu.VMEM
     dma = pltpu.SemaphoreType.DMA
     outs = [
-        sd((MP, rows, width), bf16),
-        sd((NFFN, depth, cols), bf16),
-        sd((heads, SEQ, HD), bf16),
-        sd((heads, SEQ, HD), bf16),
-        sd((heads, SEQ, HD), bf16),
-        sd((SEQ, heads * HD), bf16),
-        sd((SEQ, 128), f32),
+        sd((rows, width), bf16),
         sd((rows, width), f32),
-        sd((rows, width), f32),
-        sd((rows, width), bf16),
         sd((16, rows), f32),
+        sd((depth if inside else width, cols), f32),
         sd((40, width), f32),
-        sd((NFFN, QUARTER, everyone), bf16),
-        sd((NFFN, QUARTER, 128), f32),
-        sd((NFFN, MP, QUARTER, width), bf16),
-        sd((3, width, hidden_cols), bf16),
+        sd((1, width), f32),
+        sd((NFFN, 3, depth, hidden_cols), bf16),
     ]
     if not inside:
         wshard = wshard.reshape(NFFN, depth, cols)
     return pl.pallas_call(
-        functools.partial(forward_kernel, inside),
+        functools.partial(layer_kernel, inside),
         out_shape=outs,
         in_specs=[VM] * 7 + [HB, HB],
-        out_specs=[VM] * len(outs),
+        out_specs=[VM] * 6 + [HB],
         scratch_shapes=[
+            vm((MP, rows, width), bf16),
+            vm((NFFN, depth, cols), bf16),
+            vm((heads, SEQ, HD), bf16),
+            vm((heads, SEQ, HD), bf16),
+            vm((heads, SEQ, HD), bf16),
+            vm((SEQ, heads * HD), bf16),
+            vm((SEQ, 128), f32),
+            vm((NFFN, QUARTER, everyone), bf16),
+            vm((NFFN, QUARTER, 128), f32),
+            vm((NFFN, MP, QUARTER, width), bf16),
+            vm((3, width, hidden_cols), bf16),
             vm((MP, rows, width), bf16),
             vm((rows, width), f32),
             vm((rows, width), f32),
@@ -718,7 +973,6 @@
             vm((rows, width), bf16),
             vm((rows, width), bf16),
             vm((2, rows, width), bf16),
-            vm((MP, rows, width), bf16),
             vm((16, everyone), f32),
             vm((16, everyone), f32),
             vm((16, everyone), f32),
@@ -739,6 +993,18 @@
             vm((MP, 8, rows), f32),
             vm((2, rows, width), bf16),
             vm((rows, width), bf16),
+            vm((everyone, HD), f32),
+            vm((everyone, HD), f32),
+            vm((width, cols), f32),
+            vm((NFFN // 2, depth, cols), bf16),
+            vm((NFFN // 2, depth, cols), bf16),
+            vm((NFFN // 2, depth, cols), bf16),
+            vm((NFFN, QUARTER, width), bf16),
+            vm((5, 40, width), f32),
+            vm((5, 40, width), f32),
+            vm((MP, 1, width), f32),
+            vm((NFFN, 1, width), f32),
+            vm((2, 1, width), f32),
             dma((9,)), dma((9,)),
             dma((8,)), dma((8,)),
             dma((2, 8)), dma((2, 8)),
@@ -752,331 +1018,6 @@
             dma((8,)), dma((8,)),
             dma((4,)), dma((4,)),
             dma((3,)), dma((3,)),
-        ],
-        compiler_params=pltpu.CompilerParams(
-            collective_id=0, has_side_effects=True, vmem_limit_bytes=60 * 2**20
-        ),
-        name="forward",
-    )(x, cot, params, routing, jnp.asarray(cos), jnp.asarray(sin), wshard, win, wout)
-
-
-def back_kernel(
-    inside,
-    agrad_ref, hgrad_ref, x_ref, params_ref, cos_ref, sin_ref, rows1_ref, w_ref, q_ref, k_ref, v_ref,
-    mixed_ref, lse_ref, pick_ref, gate_ref, residual_ref, outp_ref, small_ref, dw_ref,
-    output_ref, xgrad_ref, wgrad_ref, sums_ref, first_ref, dw_own,
-    agrad_all, mgrad_ref, joint_ref, key_acc, value_acc, grads_ref, across_out, across_in,
-    along_out, along_in, ret_ref, ocore_out, ocore_in, ochip_out, ochip_in,
-    xcore_out, xcore_in, xchip_out, xchip_in, sum_out, sum_in, first_mp, first_dp, first_out,
-    pcore_in, pchip_out, pchip_in, outq_ref,
-    asend, arecv, osend, orecv, esend, erecv, psend, precv, local, rsend, rrecv, xsend, xrecv,
-    wsend, wrecv, ssend, srecv, fsend, frecv,
-):
-    mp_me = lax.axis_index("mp")
-    dp_me = lax.axis_index("dp")
-    near = lax.rem(dp_me, NFFN)
-    base = dp_me - near
-    rows, width = agrad_ref.shape
-    everyone = MP * rows
-    heads = q_ref.shape[0]
-    cols = heads * HD
-    greet(mp_me, near, base)
-
-    agrad_all[mp_me] = agrad_ref[...]
-    gather = Gather(agrad_all, mp_me, asend, arecv)
-    gather.start()
-    core, chip, far = flip(mp_me, 1), flip(mp_me, 2), flip(mp_me, 3)
-    din = dw_own.shape[2]
-
-    def rows_of(index):
-        return pl.ds(pl.multiple_of(index * din, din), din)
-
-    if inside:
-        moved = [
-            remote(dw_ref.at[:, rows_of(flip(near, k))], dw_own.at[near], esend.at[k],
-                   erecv.at[k], dp=base + flip(near, k))
-            for k in (4, 6, 5, 7, 2, 3, 1)
-        ]
-        mine = [pltpu.make_async_copy(dw_ref.at[:, rows_of(near)], dw_own.at[near], local.at[0])]
-    else:
-        moved = []
-        mine = [
-            pltpu.make_async_copy(dw_ref.at[:, rows_of(p)], dw_own.at[p], local.at[p])
-            for p in range(NFFN)
-        ]
-    for copy in moved + mine:
-        copy.start()
-
-    p_core = [
-        remote(outp_ref.at[:, far], pcore_in.at[0], psend.at[0], precv.at[0], mp=core),
-        remote(outp_ref.at[:, core], pcore_in.at[1], psend.at[1], precv.at[1], mp=core),
-    ]
-    for copy in p_core:
-        copy.start()
-    parts = (slice(4, 8), slice(0, 4))
-    p_chip = [
-        remote(pchip_out.at[part], pchip_in.at[part], psend.at[2 + j], precv.at[2 + j], mp=chip)
-        for j, part in enumerate(parts)
-    ]
-    returns = {
-        k: remote(outq_ref.at[k], ret_ref.at[k], osend.at[k], orecv.at[k],
-                  dp=base + lax.rem(near - k + NFFN, NFFN))
-        for k in range(1, NFFN)
-    }
-
-    def results_across():
-        p_core[0].wait_recv()
-        for j, part in enumerate(parts):
-            pchip_out[part] = (
-                outp_ref[part, chip].astype(f32) + pcore_in[0, part].astype(f32)
-            ).astype(bf16)
-            p_chip[j].start()
-
-    def results_away(j):
-        part = parts[j]
-        if j == 0:
-            p_core[1].wait_recv()
-        p_chip[j].wait_recv()
-        outq_ref[part] = (
-            outp_ref[part, mp_me].astype(f32)
-            + (pcore_in[1, part].astype(f32) + pchip_in[part].astype(f32))
-        ).astype(bf16)
-        for k in range(part.start, part.stop):
-            if k > 0:
-                returns[k].start()
-            else:
-                ret_ref[0] = outq_ref[0]
-
-    sum_out[0] = small_ref[...]
-    places = [{"mp": flip(mp_me, 1)}, {"mp": flip(mp_me, 2)}] + [
-        {"dp": base + flip(near, k)} for k in (1, 2, 4)
-    ]
-    stages = [
-        remote(sum_out.at[j], sum_in.at[j], ssend.at[j], srecv.at[j], **where)
-        for j, where in enumerate(places)
-    ]
-
-    def stage(j):
-        if j > 0:
-            stages[j - 1].wait_recv()
-            total = sum_out[j - 1] + sum_in[j - 1]
-            if j == len(stages):
-                sums_ref[...] = total
-                return
-            sum_out[j] = total
-        stages[j].start()
-
-    stage(0)
-    gather.forward()
-    stage(1)
-    gather.finish()
-
-    w_all = w_ref[...].reshape(width, w_ref.shape[2])
-    out_weight = w_all[:, 3 * cols :]
-    for i in range(MP):
-        mgrad_ref[i * rows : (i + 1) * rows] = dotf(agrad_all[i], out_weight).astype(bf16)
-    grads_ref[:, 3 * cols :] = dotf(agrad_all[...].reshape(everyone, width), mixed_ref[...], TN)
-
-    combine = Scatter(mp_me, ocore_out, ocore_in, ochip_out, ochip_in, rsend, rrecv)
-
-    def out_block(q):
-        at = pl.ds(pl.multiple_of(q * rows, rows), rows)
-        weighted = (ret_ref[...].astype(f32) * gate_ref[:, :, 0:1]).astype(bf16)
-        return dotf(
-            pick_ref[:, :, at].reshape(NFFN * QUARTER, rows),
-            weighted.reshape(NFFN * QUARTER, width), TN,
-        )
-
-    def head_back(h):
-        lanes = slice(h * HD, (h + 1) * HD)
-        for b in range(MP):
-            at = slice(b * rows, (b + 1) * rows)
-            seen = (b + 1) * rows
-            query = q_ref[h, at]
-            keys = k_ref[h, :seen]
-            out_grad = mgrad_ref[at, lanes]
-            scores = dotf(query, keys, NT) * HD**-0.5
-            allowed = b * rows + lax.broadcasted_iota(
-                jnp.int32, (rows, seen), 0
-            ) >= lax.broadcasted_iota(jnp.int32, (rows, seen), 1)
-            probs = jnp.where(allowed, jnp.exp(scores - lse_ref[at, h : h + 1]), 0.0)
-            probs_grad = dotf(out_grad, v_ref[h, :seen], NT)
-            inner = jnp.sum(probs * probs_grad, axis=1, keepdims=True)
-            score_grad = (probs * (probs_grad - inner)).astype(bf16)
-            query_grad = dotf(score_grad, keys) * HD**-0.5
-            joint_ref[at, lanes] = (
-                query_grad * cos_ref[at] - swap_halves(query_grad) * sin_ref[at]
-            ).astype(bf16)
-            key_grad = dotf(score_grad, query, TN) * HD**-0.5
-            value_grad = dotf(probs.astype(bf16), out_grad, TN)
-            if b == 0:
-                key_acc[...] = jnp.zeros_like(key_acc)
-                value_acc[...] = jnp.zeros_like(value_acc)
-            key_acc[:seen] += key_grad
-            value_acc[:seen] += value_grad
-        key_grad = key_acc[...]
-        joint_ref[:, cols + h * HD : cols + (h + 1) * HD] = (
-            key_grad * cos_ref[...] - swap_halves(key_grad) * sin_ref[...]
-        ).astype(bf16)
-        joint_ref[:, 2 * cols + h * HD : 2 * cols + (h + 1) * HD] = value_acc[...].astype(bf16)
-
-    last = heads - 1
-    for h in range(heads):
-        head_back(h)
-        if h == 0:
-            stage(2)
-            results_across()
-        if h == min(1, last):
-            results_away(0)
-        if h == last:
-            stage(3)
-            results_away(1)
-
-    depth = width // NFFN
-    grads_ref[:, : 3 * cols] = dotf(
-        rows1_ref[...].reshape(everyone, width), joint_ref[...], TN
-    )
-    if inside:
-        lean = lax.rem(near, 2)
-        tall = grads_ref[...].reshape(NFFN // 2, 2, depth, grads_ref.shape[1])
-        keep = jnp.where(lean == 0, tall[:, 0], tall[:, 1])
-        across_out[...] = jnp.where(lean == 0, tall[:, 1], tall[:, 0]).astype(bf16)
-        over = remote(across_out, across_in, wsend.at[0], wrecv.at[0], dp=base + flip(near, 1))
-        over.start()
-    else:
-        wgrad_ref[...] = grads_ref[...]
-    stage(4)
-
-    trip = Scatter(mp_me, xcore_out, xcore_in, xchip_out, xchip_in, xsend, xrecv)
-
-    def x_block(q):
-        at = pl.ds(pl.multiple_of(q * rows, rows), rows)
-        return dotf(joint_ref[at], w_all[:, : 3 * cols], NT)
-
-    normed_grad = trip.run(x_block)
-    if inside:
-        over.wait_recv()
-        along_out[...] = (keep + across_in[...].astype(f32)).astype(bf16)
-        up = near // 2
-        alongs = [
-            remote(along_out.at[flip(near, k) // 2], along_in.at[k // 2], wsend.at[k], wrecv.at[k],
-                   dp=base + flip(near, k))
-            for k in (4, 6, 2)
-        ]
-        for copy in alongs:
-            copy.start()
-    tokens = x_ref[...].astype(f32)
-    scale = lax.rsqrt(jnp.mean(tokens * tokens, axis=-1, keepdims=True) + epsilon)
-    scaled = tokens * scale
-    first_out[0] = jnp.sum(normed_grad * scaled, axis=0, keepdims=True)
-    firsts = [
-        remote(first_out.at[0], first_mp.at[k], fsend.at[k], frecv.at[k], mp=flip(mp_me, k))
-        for k in range(1, MP)
-    ]
-    for copy in firsts:
-        copy.start()
-    weighted = normed_grad * params_ref[23:24]
-    xgrad_ref[...] = hgrad_ref[...] + scale * (
-        weighted - scaled * jnp.mean(weighted * scaled, axis=-1, keepdims=True)
-    )
-    for copy in firsts:
-        copy.wait_recv()
-    first_out[1] = first_out[0] + first_mp[1] + first_mp[2] + first_mp[3]
-    seconds = [
-        remote(first_out.at[1], first_dp.at[k], fsend.at[MP + k], frecv.at[MP + k],
-               dp=base + flip(near, k))
-        for k in range(1, NFFN)
-    ]
-    for copy in seconds:
-        copy.start()
-    stage(5)
-    for copy in returns.values():
-        copy.wait_recv()
-    routed = combine.run(out_block)
-    output_ref[...] = (residual_ref[...] + routed).astype(bf16)
-    if inside:
-        for copy in alongs:
-            copy.wait_recv()
-        wgrad_ref[...] = along_out[up].astype(f32) + (
-            along_in[1].astype(f32) + along_in[2].astype(f32) + along_in[3].astype(f32)
-        )
-    for copy in seconds:
-        copy.wait_recv()
-    total = first_out[1]
-    for k in range(1, NFFN):
-        total = total + first_dp[k]
-    first_ref[...] = total
-
-    for copy in moved:
-        copy.wait_recv()
-    for copy in mine:
-        copy.wait()
-    if inside:
-        for copy in [over] + alongs:
-            copy.wait_send()
-    for copy in moved + p_core + p_chip + list(returns.values()) + stages + firsts + seconds:
-        copy.wait_send()
-    combine.drain()
-    trip.drain()
-
-
-def attention_back(
-    agrad, hgrad, x, params, rows1, w, q, k, v, mixed, lse, pick, gate, residual, outp, small, dw,
-    groups,
-):
-    rows, width = x.shape
-    everyone = MP * rows
-    cos, sin = rope_constants()
-    inside = groups == 1
-    cols = w.shape[-1]
-    heads = q.shape[0]
-    depth = width // NFFN
-    hidden_cols = dw.shape[-1]
-    sd = jax.ShapeDtypeStruct
-    vm = pltpu.VMEM
-    dma = pltpu.SemaphoreType.DMA
-    outs = [
-        sd((rows, width), bf16),
-        sd((rows, width), f32),
-        sd((depth if inside else width, cols), f32),
-        sd((40, width), f32),
-        sd((1, width), f32),
-        sd((NFFN, 3, depth, hidden_cols), bf16),
-    ]
-    return pl.pallas_call(
-        functools.partial(back_kernel, inside),
-        out_shape=outs,
-        in_specs=[VM] * 19,
-        out_specs=[VM] * 5 + [HB],
-        scratch_shapes=[
-            vm((MP, rows, width), bf16),
-            vm((everyone, heads * HD), bf16),
-            vm((everyone, 3 * heads * HD), bf16),
-            vm((everyone, HD), f32),
-            vm((everyone, HD), f32),
-            vm((width, cols), f32),
-            vm((NFFN // 2, depth, cols), bf16),
-            vm((NFFN // 2, depth, cols), bf16),
-            vm((NFFN // 2, depth, cols), bf16),
-            vm((NFFN // 2, depth, cols), bf16),
-            vm((NFFN, QUARTER, width), bf16),
-            vm((2, rows, width), bf16),
-            vm((2, rows, width), bf16),
-            vm((rows, width), bf16),
-            vm((rows, width), bf16),
-            vm((2, rows, width), bf16),
-            vm((2, rows, width), bf16),
-            vm((rows, width), bf16),
-            vm((rows, width), bf16),
-            vm((5, 40, width), f32),
-            vm((5, 40, width), f32),
-            vm((MP, 1, width), f32),
-            vm((NFFN, 1, width), f32),
-            vm((2, 1, width), f32),
-            vm((2, NFFN, QUARTER, width), bf16),
-            vm((NFFN, QUARTER, width), bf16),
-            vm((NFFN, QUARTER, width), bf16),
-            vm((NFFN, QUARTER, width), bf16),
             dma((3,)), dma((3,)),
             dma((8,)), dma((8,)),
             dma((8,)), dma((8,)),
@@ -1088,13 +1029,10 @@
             dma((MP + NFFN,)), dma((MP + NFFN,)),
         ],
         compiler_params=pltpu.CompilerParams(
-            collective_id=1, has_side_effects=True, vmem_limit_bytes=60 * 2**20
+            collective_id=0, has_side_effects=True, vmem_limit_bytes=VMEM_LIMIT
         ),
-        name="attention_backward",
-    )(
-        agrad, hgrad, x, params, jnp.asarray(cos), jnp.asarray(sin), rows1, w, q, k, v, mixed, lse,
-        pick, gate, residual, outp, small, dw,
-    )
+        name="layer",
+    )(x, cot, params, routing, jnp.asarray(cos), jnp.asarray(sin), wshard, win, wout)
 
 
 def clusters():
@@ -1170,13 +1108,8 @@
         wout = exchange(expert_output_t, 1)[0]
     if groups == 1:
         win, wout = expert_input, expert_output_t
-    (rows1, w, q, k, v, mixed, lse, residual, hidden_grad, attended_grad, logits_grad, small, pick,
-     gate, outp, dw) = forward(
+    output, input_grad, logits_grad, weight_grad, sums, first_grad, expert_grad = layer(
         inputs, cotangent, params, routing, shard, win, wout, groups
-    )
-    output, input_grad, weight_grad, sums, first_grad, expert_grad = attention_back(
-        attended_grad, hidden_grad, inputs, params, rows1, w, q, k, v, mixed, lse, pick, gate,
-        residual, outp, small, dw, groups,
     )
     if groups > 1:
         weight_grad = lax.psum_scatter(weight_grad, "dp", scatter_dimension=0, tiled=True)

time: 327 us -> 308 us (0.942)
  Pallas kernels: 296 us -> 278 us
    pallas_call x2 -> x1, Pallas kernels: 296 us -> 278 us  [layer(): pl.pallas_call(functools.partial(layer_kernel, inside), out_shape=outs, i...]
where the time goes in v5:
time: 308 us; the launch traced here: 307 us
  Pallas kernels  278 us (90%)
  local copies, waits for them, and re-layouts  17.6 us (6%)
  other arithmetic  11.1 us (4%)
    pallas_call x1, Pallas kernels, layer(): pl.pallas_call(functools.partial(layer_kernel, inside), out_shape=outs, i...  278 us

profile of v5, /device:TPU:0, one launch (start us, length us, event | category | flops | bytes accessed | tf_op | source)
XLA Modules:
  0.0 307.1 jit_solution(6915262600517624615)
XLA Ops:
  0.6 1.1 copy.33
  1.7 0.2 copy.35
  1.9 0.9 copy.34
  2.8 0.7 pad_maximum_fusion.wshard_ref
  3.5 0.7 pad.21
  4.2 0.7 pad_convert_fusion
  5.0 0.7 convert_bitcast_fusion.1
  5.7 0.7 reshape.36
  6.3 0.7 reshape.37
  7.0 2.6 concatenate.9.params_ref
  9.6 0.7 convert_bitcast_fusion.2
  10.3 1.5 select_maximum_fusion.routing_ref
  11.8 277.8 %layer.1 = (bf16[256,768]{1,0:T(8,128)(2,1)}, f32[256,768]{1,0:T(8,128)}, f32[16,256]{1,0:T(8,128)}, f32[96,768]{1,0:T(8,128)}, f32[40,768]{1,0:T(8,128)}, /*ind...) custom-call(bf16[256,768]{1,0:T(8,128)(2,1)} %x_ref.1, bf16[256,768]{1,0:T(8,128)(2,1)} %cot_ref.1, ...), custom_call_target="tpu_custom_call" | custom-call | tf_op jit(solution)/shard_map/layer/pallas_call | solution.py:952
  289.5 1.4 slice_bitcast_fusion.1
  291.0 1.3 slice_bitcast_fusion.3
  292.3 1.3 slice.37
  293.6 1.3 slice.39
  294.9 1.3 slice_reduce_fusion
  296.3 3.5 %slice_convert_fusion = f32[8,2,96,512]{3,2,1,0:T(8,128)} fusion(bf16[8,3,96,512]{3,2,1,0:T(8,128)(2,1)} %get-tuple-element.24), kind=kLoop, calls=%fused_computation.1 | loop fusion | flops 786432 | bytes 4718592 | tf_op jit(solution)/shard_map/convert_element_type | solution.py:1119
  299.8 0.0 copy-start
  299.8 2.6 convert_bitcast_fusion
  302.4 0.0 copy-done.1
  302.4 0.1 copy.36
  302.6 0.9 copy.37
  303.5 0.1 slice_bitcast_fusion
  303.5 0.7 copy.38
  304.3 0.0 copy-done.3
  304.3 0.6 slice_bitcast_fusion.2
  304.9 0.0 copy-done.4
  304.9 0.6 reduce
  305.5 0.7 copy.41
  306.3 0.9 copy.42
  (7 shorter events, 0.0 us)
Async XLA Ops:
  299.8 2.6 copy-start.1
  299.8 4.5 %copy-start.3 = (f32[16,256]{1,0:T(8,128)S(1)}, f32[16,256]{1,0:T(8,128)}, u32[]{:S(2)}) copy-start(f32[16,256]{1,0:T(8,128)} %get-tuple-element.22) | copy-start | bytes 49156
  299.8 5.1 %copy-start.4 = (f32[1,768]{1,0:T(1,128)S(1)}, f32[1,768]{1,0:T(1,128)}, u32[]{:S(2)}) copy-start(f32[1,768]{1,0:T(1,128)} %get-tuple-element.25) | copy-start | bytes 9220
  299.8 5.7 %copy-start.2 = (bf16[256,768]{1,0:T(8,128)(2,1)S(1)}, bf16[256,768]{1,0:T(8,128)(2,1)}, u32[]{:S(2)}) copy-start(bf16[256,768]{1,0:T(8,128)(2,1)} %get-tuple-element.66) | copy-start | bytes 1179652
  299.8 6.5 %copy-start = (f32[256,768]{1,0:T(8,128)S(1)}, f32[256,768]{1,0:T(8,128)}, u32[]{:S(2)}) copy-start(f32[256,768]{1,0:T(8,128)} %get-tuple-element.67) | copy-start | bytes 2359300

commit v6 on v5

--- a/solution.py
+++ b/solution.py
@@ -15,7 +15,7 @@
 MP = 4
 QUARTER = CAP // MP
 WIDE = 640
-VMEM_LIMIT = 62 * 2**20
+VMEM_LIMIT = 63 * 2**20
 
 epsilon = 1e-06
 rope_base = 10000.0
@@ -167,6 +167,7 @@
     part_ref, keep_ref, gcore_out, gcore_in, gchip_out, gchip_in, gret, score_out, score_in,
     ncore_in, nchip_in,
     key_acc, value_acc, grads_ref, across_out, across_in, along_in, ret_ref,
+    pcore_in, pchip_in,
     sum_out, sum_in, first_mp, first_dp, first_out,
     sends, recvs, wsend, wrecv, esend, erecv, local,
     csend, crecv, xsend, xrecv, dsend, drecv, xgs, xgr, cgs, cgr, gsend, grecv,
@@ -555,6 +556,46 @@
 
     lax.fori_loop(0, NFFN + 4, expert_step, 0)
 
+    p_core = [
+        remote(outp_ref.at[:, far], pcore_in.at[0], psend.at[0], precv.at[0], mp=core),
+        remote(outp_ref.at[:, core], pcore_in.at[1], psend.at[1], precv.at[1], mp=core),
+    ]
+    for copy in p_core:
+        copy.start()
+    parts = (slice(4, 8), slice(0, 4))
+    p_chip = [
+        remote(cs.at[part, 3], pchip_in.at[part], psend.at[2 + j], precv.at[2 + j], mp=chip)
+        for j, part in enumerate(parts)
+    ]
+    returns = {
+        k: remote(msgc.at[k], ret_ref.at[k], osend.at[k], orecv.at[k],
+                  dp=base + lax.rem(near - k + NFFN, NFFN))
+        for k in range(1, NFFN)
+    }
+
+    def results_across():
+        p_core[0].wait_recv()
+        for j, part in enumerate(parts):
+            cs[part, 3] = (
+                outp_ref[part, chip].astype(f32) + pcore_in[0, part].astype(f32)
+            ).astype(bf16)
+            p_chip[j].start()
+
+    def results_away(j):
+        part = parts[j]
+        if j == 0:
+            p_core[1].wait_recv()
+        p_chip[j].wait_recv()
+        msgc[part] = (
+            outp_ref[part, mp_me].astype(f32)
+            + (pcore_in[1, part].astype(f32) + pchip_in[part].astype(f32))
+        ).astype(bf16)
+        for k in range(part.start, part.stop):
+            if k > 0:
+                returns[k].start()
+            else:
+                ret_ref[0] = msgc[0]
+
     def weights_step(j, carried):
         at = pl.ds(pl.multiple_of(j * 128, 128), 128)
         x = xs[:, :, :, at].reshape(NFFN * CAP, 128)
@@ -584,8 +625,10 @@
             pltpu.make_async_copy(dw_ref.at[:, rows_of(p)], dw_own.at[p], mlocal.at[p])
             for p in range(NFFN)
         ]
-    for copy in moved + kept:
+    early = 7
+    for copy in moved[:early] + kept:
         copy.start()
+    results_across()
 
     n_bf = rows2_ref[mp_me]
     n = n_bf.astype(f32)
@@ -655,6 +698,11 @@
 
     trip = Scatter(mp_me, core_out, ncore_in, chip_out, nchip_in, nsend, nrecv)
     normed_grad = trip.run(grad_block) + local_grad
+    lax.fori_loop(1, NFFN, lambda k, carried: (c_copy(k).wait_send(), carried)[1], 0)
+    results_away(0)
+    results_away(1)
+    for copy in moved[early:]:
+        copy.start()
 
     for copy in score_copies:
         copy.wait_recv()
@@ -694,7 +742,6 @@
         copy.wait_send()
 
     def drain(k, carried):
-        c_copy(k).wait_send()
         g_copy(k).wait_send()
         return carried
 
@@ -702,46 +749,6 @@
     if inside:
         for copy in weights:
             copy.wait_send()
-
-    p_core = [
-        remote(outp_ref.at[:, far], cs.at[:, 0], psend.at[0], precv.at[0], mp=core),
-        remote(outp_ref.at[:, core], cs.at[:, 1], psend.at[1], precv.at[1], mp=core),
-    ]
-    for copy in p_core:
-        copy.start()
-    parts = (slice(4, 8), slice(0, 4))
-    p_chip = [
-        remote(cs.at[part, 3], cs.at[part, 2], psend.at[2 + j], precv.at[2 + j], mp=chip)
-        for j, part in enumerate(parts)
-    ]
-    returns = {
-        k: remote(msgc.at[k], ret_ref.at[k], osend.at[k], orecv.at[k],
-                  dp=base + lax.rem(near - k + NFFN, NFFN))
-        for k in range(1, NFFN)
-    }
-
-    def results_across():
-        p_core[0].wait_recv()
-        for j, part in enumerate(parts):
-            cs[part, 3] = (
-                outp_ref[part, chip].astype(f32) + cs[part, 0].astype(f32)
-            ).astype(bf16)
-            p_chip[j].start()
-
-    def results_away(j):
-        part = parts[j]
-        if j == 0:
-            p_core[1].wait_recv()
-        p_chip[j].wait_recv()
-        msgc[part] = (
-            outp_ref[part, mp_me].astype(f32)
-            + (cs[part, 1].astype(f32) + cs[part, 2].astype(f32))
-        ).astype(bf16)
-        for k in range(part.start, part.stop):
-            if k > 0:
-                returns[k].start()
-            else:
-                ret_ref[0] = msgc[0]
 
     places = [{"mp": flip(mp_me, 1)}, {"mp": flip(mp_me, 2)}] + [
         {"dp": base + flip(near, k)} for k in (1, 2, 4)
@@ -772,7 +779,7 @@
         xs[i, :, :, WIDE : WIDE + cols] = (
             dotf(rows2_ref[i], out_weight).astype(bf16).reshape(MP, QUARTER, cols)
         )
-    grads_ref[:, 3 * cols :] = dotf(rows2_ref[...].reshape(everyone, width), mixed_ref[...], TN)
+    grads_ref[:, 3 * cols :] = dotf(rows2_ref[...].reshape(everyone, width), mixed_ref[...], TN).astype(bf16)
 
     combine = Scatter(mp_me, core_out, ncore_in, chip_out, nchip_in, bsend, brecv)
 
@@ -827,27 +834,23 @@
         head_back(h)
         if h == 0:
             stage(2)
-            results_across()
-        if h == min(1, last):
-            results_away(0)
         if h == last:
             stage(3)
-            results_away(1)
 
     depth = width // NFFN
     grads_ref[:, : 3 * cols] = dotf(
         rows1_ref[...].reshape(everyone, width),
         xs[0:MP, :, :, 0 : 3 * cols].reshape(everyone, 3 * cols), TN,
-    )
+    ).astype(bf16)
     if inside:
         lean = lax.rem(near, 2)
         tall = grads_ref[...].reshape(NFFN // 2, 2, depth, grads_ref.shape[1])
-        keep = jnp.where(lean == 0, tall[:, 0], tall[:, 1])
-        across_out[...] = jnp.where(lean == 0, tall[:, 1], tall[:, 0]).astype(bf16)
+        across_out[...] = jnp.where(lean == 0, tall[:, 1], tall[:, 0])
+        kept_half = jnp.where(lean == 0, tall[:, 0], tall[:, 1])
         over = remote(across_out, across_in, vsend.at[0], vrecv.at[0], dp=base + flip(near, 1))
         over.start()
     else:
-        wgrad_ref[...] = grads_ref[...]
+        wgrad_ref[...] = grads_ref[...].astype(f32)
     stage(4)
 
     home = Scatter(mp_me, core_out, core_in, chip_out, chip_in, tsend, trecv)
@@ -861,7 +864,7 @@
     if inside:
         over.wait_recv()
         over.wait_send()
-        across_out[...] = (keep + across_in[...].astype(f32)).astype(bf16)
+        across_out[...] = (kept_half.astype(f32) + across_in[...].astype(f32)).astype(bf16)
         up = near // 2
         alongs = [
             remote(across_out.at[flip(near, k) // 2], along_in.at[k // 2], vsend.at[k], vrecv.at[k],
@@ -995,10 +998,12 @@
             vm((rows, width), bf16),
             vm((everyone, HD), f32),
             vm((everyone, HD), f32),
-            vm((width, cols), f32),
+            vm((width, cols), bf16),
             vm((NFFN // 2, depth, cols), bf16),
             vm((NFFN // 2, depth, cols), bf16),
             vm((NFFN // 2, depth, cols), bf16),
+            vm((NFFN, QUARTER, width), bf16),
+            vm((2, NFFN, QUARTER, width), bf16),
             vm((NFFN, QUARTER, width), bf16),
             vm((5, 40, width), f32),
             vm((5, 40, width), f32),

time: 308 us -> 295 us (0.958)
  Pallas kernels: 278 us -> 264 us
    pallas_call x1, Pallas kernels: 278 us -> 264 us  [layer(): pl.pallas_call(functools.partial(layer_kernel, inside), out_shape=outs, i...]
where the time goes in v6:
time: 295 us; the launch traced here: 294 us
  Pallas kernels  264 us (89%)
  local copies, waits for them, and re-layouts  17.6 us (6%)
  other arithmetic  11.1 us (4%)
    pallas_call x1, Pallas kernels, layer(): pl.pallas_call(functools.partial(layer_kernel, inside), out_shape=outs, i...  264 us

profile of v6, /device:TPU:0, one launch (start us, length us, event | category | flops | bytes accessed | tf_op | source)
XLA Modules:
  0.0 293.8 jit_solution(11149223819870366043)
XLA Ops:
  0.6 1.1 copy.33
  1.7 0.2 copy.35
  1.9 0.9 copy.34
  2.8 0.7 pad_maximum_fusion.wshard_ref
  3.5 0.7 pad.21
  4.2 0.7 pad_convert_fusion
  5.0 0.7 convert_bitcast_fusion.1
  5.7 0.7 reshape.36
  6.3 0.7 reshape.37
  7.0 2.6 concatenate.9.params_ref
  9.6 0.7 convert_bitcast_fusion.2
  10.3 1.5 select_maximum_fusion.routing_ref
  11.8 264.4 %layer.1 = (bf16[256,768]{1,0:T(8,128)(2,1)}, f32[256,768]{1,0:T(8,128)}, f32[16,256]{1,0:T(8,128)}, f32[96,768]{1,0:T(8,128)}, f32[40,768]{1,0:T(8,128)}, /*ind...) custom-call(bf16[256,768]{1,0:T(8,128)(2,1)} %x_ref.1, bf16[256,768]{1,0:T(8,128)(2,1)} %cot_ref.1, ...), custom_call_target="tpu_custom_call" | custom-call | tf_op jit(solution)/shard_map/layer/pallas_call | solution.py:955
  276.2 1.4 slice_bitcast_fusion.1
  277.6 1.3 slice_bitcast_fusion.3
  278.9 1.3 slice.37
  280.2 1.3 slice.39
  281.6 1.3 slice_reduce_fusion
  282.9 3.5 %slice_convert_fusion = f32[8,2,96,512]{3,2,1,0:T(8,128)} fusion(bf16[8,3,96,512]{3,2,1,0:T(8,128)(2,1)} %get-tuple-element.24), kind=kLoop, calls=%fused_computation.1 | loop fusion | flops 786432 | bytes 4718592 | tf_op jit(solution)/shard_map/convert_element_type | solution.py:1124
  286.4 0.0 copy-start
  286.4 2.6 convert_bitcast_fusion
  289.0 0.0 copy-done.1
  289.1 0.1 copy.36
  289.2 0.9 copy.37
  290.1 0.1 slice_bitcast_fusion
  290.2 0.7 copy.38
  290.9 0.0 copy-done.3
  290.9 0.6 slice_bitcast_fusion.2
  291.5 0.6 reduce
  292.1 0.7 copy.41
  292.9 0.0 copy-done
  292.9 0.9 copy.42
  (7 shorter events, 0.0 us)
Async XLA Ops:
  286.4 2.6 copy-start.1
  286.4 4.5 %copy-start.3 = (f32[16,256]{1,0:T(8,128)S(1)}, f32[16,256]{1,0:T(8,128)}, u32[]{:S(2)}) copy-start(f32[16,256]{1,0:T(8,128)} %get-tuple-element.22) | copy-start | bytes 49156
  286.4 5.1 %copy-start.4 = (f32[1,768]{1,0:T(1,128)S(1)}, f32[1,768]{1,0:T(1,128)}, u32[]{:S(2)}) copy-start(f32[1,768]{1,0:T(1,128)} %get-tuple-element.25) | copy-start | bytes 9220
  286.4 5.7 %copy-start.2 = (bf16[256,768]{1,0:T(8,128)(2,1)S(1)}, bf16[256,768]{1,0:T(8,128)(2,1)}, u32[]{:S(2)}) copy-start(bf16[256,768]{1,0:T(8,128)(2,1)} %get-tuple-element.66) | copy-start | bytes 1179652
  286.4 6.5 %copy-start = (f32[256,768]{1,0:T(8,128)S(1)}, f32[256,768]{1,0:T(8,128)}, u32[]{:S(2)}) copy-start(f32[256,768]{1,0:T(8,128)} %get-tuple-element.67) | copy-start | bytes 2359300

commit v7 on v6

--- a/solution.py
+++ b/solution.py
@@ -159,7 +159,8 @@
 
 def layer_kernel(
     inside,
-    x_ref, cot_ref, params_ref, routing_ref, cos_ref, sin_ref, wshard_ref, win_shard, wout_shard,
+    x_ref, cot_ref, router_ref, mix_ref, values_ref, gain2_ref, gain1_ref, carry_ref, previous_ref,
+    routes_ref, cos_ref, sin_ref, wshard_ref, win_shard, wout_shard,
     output_ref, xgrad_ref, lgrad_ref, wgrad_ref, sums_ref, first_ref, dw_own,
     rows1_ref, w_ref, q_ref, k_ref, v_ref, mixed_ref, lse_ref, pick_ref, gate_ref, outp_ref, dw_ref,
     rows2_ref, hidden_ref, sum_ref, core_in, chip_out, chip_in, core_out,
@@ -167,7 +168,7 @@
     part_ref, keep_ref, gcore_out, gcore_in, gchip_out, gchip_in, gret, score_out, score_in,
     ncore_in, nchip_in,
     key_acc, value_acc, grads_ref, across_out, across_in, along_in, ret_ref,
-    pcore_in, pchip_in,
+    pcore_in, pchip_in, params_ref, routing_ref,
     sum_out, sum_in, first_mp, first_dp, first_out,
     sends, recvs, wsend, wrecv, esend, erecv, local,
     csend, crecv, xsend, xrecv, dsend, drecv, xgs, xgr, cgs, cgr, gsend, grecv,
@@ -187,6 +188,17 @@
     rows, width = x_ref.shape
     everyone = MP * rows
     greet(mp_me, near, base)
+
+    params_ref[...] = jnp.zeros_like(params_ref)
+    params_ref[0:NEXP] = router_ref[...].astype(f32)
+    params_ref[16:20] = mix_ref[...].astype(f32)
+    params_ref[20:22] = values_ref[...].astype(f32)
+    params_ref[22:23] = gain2_ref[...].astype(f32)
+    params_ref[23:24] = gain1_ref[...].astype(f32)
+    params_ref[24 : 24 + NEXP, 0:NEXP] = carry_ref[...]
+    routing_ref[...] = jnp.zeros_like(routing_ref)
+    routing_ref[0:NEXP] = previous_ref[...]
+    routing_ref[16:18] = routes_ref[...].astype(f32)
 
     tokens = x_ref[...].astype(f32)
     scale = lax.rsqrt(jnp.mean(tokens * tokens, axis=-1, keepdims=True) + epsilon)
@@ -927,7 +939,7 @@
     combine.drain()
 
 
-def layer(x, cot, params, routing, wshard, win, wout, groups):
+def layer(x, cot, small, wshard, win, wout, groups):
     rows, width = x.shape
     cos, sin = rope_constants()
     inside = groups == 1
@@ -955,7 +967,7 @@
     return pl.pallas_call(
         functools.partial(layer_kernel, inside),
         out_shape=outs,
-        in_specs=[VM] * 7 + [HB, HB],
+        in_specs=[VM] * 13 + [HB, HB],
         out_specs=[VM] * 6 + [HB],
         scratch_shapes=[
             vm((MP, rows, width), bf16),
@@ -1005,6 +1017,8 @@
             vm((NFFN, QUARTER, width), bf16),
             vm((2, NFFN, QUARTER, width), bf16),
             vm((NFFN, QUARTER, width), bf16),
+            vm((40, width), f32),
+            vm((24, everyone), f32),
             vm((5, 40, width), f32),
             vm((5, 40, width), f32),
             vm((MP, 1, width), f32),
@@ -1037,7 +1051,7 @@
             collective_id=0, has_side_effects=True, vmem_limit_bytes=VMEM_LIMIT
         ),
         name="layer",
-    )(x, cot, params, routing, jnp.asarray(cos), jnp.asarray(sin), wshard, win, wout)
+    )(x, cot, *small, jnp.asarray(cos), jnp.asarray(sin), wshard, win, wout)
 
 
 def clusters():
@@ -1080,26 +1094,15 @@
     rows, width = inputs.shape
     groups, _, far = clusters()
 
-    def padded(array, high, wide, value=0.0):
-        return jnp.pad(
-            array.astype(f32), ((0, high - array.shape[0]), (0, wide - array.shape[1])),
-            constant_values=value,
-        )
-
-    params = jnp.concatenate(
-        [
-            padded(router_weight.T, 16, width),
-            constant_mix.T.astype(f32),
-            constant_values.astype(f32),
-            second_gain.astype(f32)[None],
-            first_gain.astype(f32)[None],
-            padded(logit_carry, 16, width),
-        ],
-        axis=0,
-    )
-    everyone = rows * MP
-    routing = jnp.concatenate(
-        [padded(previous_logits.T, 16, everyone), padded(routes.T, 8, everyone, -1.0)], axis=0
+    small = (
+        router_weight.T,
+        constant_mix.T,
+        constant_values,
+        second_gain[None],
+        first_gain[None],
+        logit_carry,
+        previous_logits.T,
+        routes.T,
     )
     shard_depth = query_key_value.shape[0]
     shard = jnp.concatenate(
@@ -1114,7 +1117,7 @@
     if groups == 1:
         win, wout = expert_input, expert_output_t
     output, input_grad, logits_grad, weight_grad, sums, first_grad, expert_grad = layer(
-        inputs, cotangent, params, routing, shard, win, wout, groups
+        inputs, cotangent, small, shard, win, wout, groups
     )
     if groups > 1:
         weight_grad = lax.psum_scatter(weight_grad, "dp", scatter_dimension=0, tiled=True)

time: 295 us -> 289 us (0.980)
  other arithmetic: 11.1 us -> 7.45 us
where the time goes in v7:
time: 289 us; the launch traced here: 288 us
  Pallas kernels  265 us (92%)
  local copies, waits for them, and re-layouts  15.5 us (5%)
  other arithmetic  7.45 us (3%)
    pallas_call x1, Pallas kernels, layer(): pl.pallas_call(functools.partial(layer_kernel, inside), out_shape=outs, i...  265 us

profile of v7, /device:TPU:0, one launch (start us, length us, event | category | flops | bytes accessed | tf_op | source)
XLA Modules:
  0.0 288.4 jit_solution(16570600867908532673)
XLA Ops:
  0.6 1.1 copy.33
  1.7 0.2 copy.35
  1.9 0.9 copy.34
  2.8 0.7 pad_maximum_fusion.wshard_ref
  3.5 1.3 broadcast_in_dim.6.gain2_ref
  4.8 1.3 broadcast_in_dim.7.gain1_ref
  6.0 264.7 %layer.1 = (bf16[256,768]{1,0:T(8,128)(2,1)}, f32[256,768]{1,0:T(8,128)}, f32[16,256]{1,0:T(8,128)}, f32[96,768]{1,0:T(8,128)}, f32[40,768]{1,0:T(8,128)}, /*ind...) custom-call(bf16[256,768]{1,0:T(8,128)(2,1)} %x_ref.1, bf16[256,768]{1,0:T(8,128)(2,1)} %cot_ref.1, ...), custom_call_target="tpu_custom_call" | custom-call | tf_op jit(solution)/shard_map/layer/pallas_call | solution.py:967
  270.8 1.4 slice_bitcast_fusion.1
  272.2 1.3 slice_bitcast_fusion.3
  273.5 1.3 slice.37
  274.8 1.3 slice.39
  276.2 1.3 slice_reduce_fusion
  277.5 3.5 %slice_convert_fusion = f32[8,2,96,512]{3,2,1,0:T(8,128)} fusion(bf16[8,3,96,512]{3,2,1,0:T(8,128)(2,1)} %get-tuple-element.24), kind=kLoop, calls=%fused_computation.1 | loop fusion | flops 786432 | bytes 4718592 | tf_op jit(solution)/shard_map/convert_element_type | solution.py:1127
  281.0 0.0 copy-start.1
  281.0 0.0 copy-start.3
  281.0 0.0 copy-start.4
  281.0 0.0 copy-start.2
  281.0 0.0 copy-start
  281.0 2.6 convert_bitcast_fusion
  283.6 0.0 copy-done.1
  283.7 0.1 copy.36
  283.8 0.9 copy.37
  284.7 0.1 slice_bitcast_fusion
  284.8 0.7 copy.38
  285.5 0.0 copy-done.3
  285.5 0.6 slice_bitcast_fusion.2
  286.1 0.0 copy-done.4
  286.1 0.6 reduce
  286.7 0.0 copy-done.2
  286.7 0.7 copy.41
  287.5 0.0 copy-done
  287.5 0.9 copy.42
  (1 shorter events, 0.0 us)
Async XLA Ops:
  281.0 2.6 copy-start.1
  281.0 4.5 %copy-start.3 = (f32[16,256]{1,0:T(8,128)S(1)}, f32[16,256]{1,0:T(8,128)}, u32[]{:S(2)}) copy-start(f32[16,256]{1,0:T(8,128)} %get-tuple-element.22) | copy-start | bytes 49156
  281.0 5.1 %copy-start.4 = (f32[1,768]{1,0:T(1,128)S(1)}, f32[1,768]{1,0:T(1,128)}, u32[]{:S(2)}) copy-start(f32[1,768]{1,0:T(1,128)} %get-tuple-element.25) | copy-start | bytes 9220
  281.0 5.7 %copy-start.2 = (bf16[256,768]{1,0:T(8,128)(2,1)S(1)}, bf16[256,768]{1,0:T(8,128)(2,1)}, u32[]{:S(2)}) copy-start(bf16[256,768]{1,0:T(8,128)(2,1)} %get-tuple-element.66) | copy-start | bytes 1179652
  281.0 6.5 %copy-start = (f32[256,768]{1,0:T(8,128)S(1)}, f32[256,768]{1,0:T(8,128)}, u32[]{:S(2)}) copy-start(f32[256,768]{1,0:T(8,128)} %get-tuple-element.67) | copy-start | bytes 2359300

commit v8 on v7

--- a/solution.py
+++ b/solution.py
@@ -159,7 +159,7 @@
 
 def layer_kernel(
     inside,
-    x_ref, cot_ref, router_ref, mix_ref, values_ref, gain2_ref, gain1_ref, carry_ref, previous_ref,
+    x_ref, cot_ref, router_ref, mix_ref, values_ref, gains_ref, carry_ref, previous_ref,
     routes_ref, cos_ref, sin_ref, wshard_ref, win_shard, wout_shard,
     output_ref, xgrad_ref, lgrad_ref, wgrad_ref, sums_ref, first_ref, dw_own,
     rows1_ref, w_ref, q_ref, k_ref, v_ref, mixed_ref, lse_ref, pick_ref, gate_ref, outp_ref, dw_ref,
@@ -193,8 +193,7 @@
     params_ref[0:NEXP] = router_ref[...].astype(f32)
     params_ref[16:20] = mix_ref[...].astype(f32)
     params_ref[20:22] = values_ref[...].astype(f32)
-    params_ref[22:23] = gain2_ref[...].astype(f32)
-    params_ref[23:24] = gain1_ref[...].astype(f32)
+    params_ref[22:24] = gains_ref[...].astype(f32)
     params_ref[24 : 24 + NEXP, 0:NEXP] = carry_ref[...]
     routing_ref[...] = jnp.zeros_like(routing_ref)
     routing_ref[0:NEXP] = previous_ref[...]
@@ -967,7 +966,7 @@
     return pl.pallas_call(
         functools.partial(layer_kernel, inside),
         out_shape=outs,
-        in_specs=[VM] * 13 + [HB, HB],
+        in_specs=[VM] * 12 + [HB, HB],
         out_specs=[VM] * 6 + [HB],
         scratch_shapes=[
             vm((MP, rows, width), bf16),
@@ -1098,8 +1097,7 @@
         router_weight.T,
         constant_mix.T,
         constant_values,
-        second_gain[None],
-        first_gain[None],
+        jnp.stack([second_gain, first_gain]),
         logit_carry,
         previous_logits.T,
         routes.T,

time: 289 us -> 288 us (level)
  no operation moved by 1% of the time
where the time goes in v8:
time: 288 us; the launch traced here: 287 us
  Pallas kernels  264 us (92%)
  local copies, waits for them, and re-layouts  14.3 us (5%)
  other arithmetic  8.05 us (3%)
    pallas_call x1, Pallas kernels, layer(): pl.pallas_call(functools.partial(layer_kernel, inside), out_shape=outs, i...  264 us

profile of v8, /device:TPU:0, one launch (start us, length us, event | category | flops | bytes accessed | tf_op | source)
XLA Modules:
  0.0 287.3 jit_solution(8909308367974736287)
XLA Ops:
  0.6 1.1 copy.33
  1.7 0.2 copy.35
  1.9 0.9 copy.34
  2.8 0.7 pad_maximum_fusion.wshard_ref
  3.5 0.7 stack.10
  4.2 0.7 stack.9
  4.9 0.6 pad_maximum_fusion.1.gains_ref
  5.5 264.2 %layer.1 = (bf16[256,768]{1,0:T(8,128)(2,1)}, f32[256,768]{1,0:T(8,128)}, f32[16,256]{1,0:T(8,128)}, f32[96,768]{1,0:T(8,128)}, f32[40,768]{1,0:T(8,128)}, /*ind...) custom-call(bf16[256,768]{1,0:T(8,128)(2,1)} %x_ref.1, bf16[256,768]{1,0:T(8,128)(2,1)} %cot_ref.1, ...), custom_call_target="tpu_custom_call" | custom-call | tf_op jit(solution)/shard_map/layer/pallas_call | solution.py:966
  269.7 1.4 slice_bitcast_fusion.1
  271.1 1.3 slice_bitcast_fusion.3
  272.5 1.3 slice.37
  273.8 1.3 slice.39
  275.1 1.3 slice_reduce_fusion
  276.4 3.5 %slice_convert_fusion = f32[8,2,96,512]{3,2,1,0:T(8,128)} fusion(bf16[8,3,96,512]{3,2,1,0:T(8,128)(2,1)} %get-tuple-element.24), kind=kLoop, calls=%fused_computation.1 | loop fusion | flops 786432 | bytes 4718592 | tf_op jit(solution)/shard_map/convert_element_type | solution.py:1125
  280.0 0.0 copy-start.3
  280.0 0.0 copy-start.4
  280.0 0.0 copy-start.2
  280.0 0.0 copy-start
  280.0 2.6 convert_bitcast_fusion
  282.6 0.0 copy-done.1
  282.6 0.1 copy.36
  282.7 0.9 copy.37
  283.6 0.1 slice_bitcast_fusion
  283.7 0.7 copy.38
  284.5 0.0 copy-done.3
  284.5 0.6 slice_bitcast_fusion.2
  285.1 0.0 copy-done.4
  285.1 0.6 reduce
  285.7 0.0 copy-done.2
  285.7 0.7 copy.41
  286.4 0.0 copy-done
  286.4 0.9 copy.42
  (2 shorter events, 0.0 us)
Async XLA Ops:
  279.9 2.6 copy-start.1
  280.0 4.5 %copy-start.3 = (f32[16,256]{1,0:T(8,128)S(1)}, f32[16,256]{1,0:T(8,128)}, u32[]{:S(2)}) copy-start(f32[16,256]{1,0:T(8,128)} %get-tuple-element.22) | copy-start | bytes 49156
  280.0 5.1 %copy-start.4 = (f32[1,768]{1,0:T(1,128)S(1)}, f32[1,768]{1,0:T(1,128)}, u32[]{:S(2)}) copy-start(f32[1,768]{1,0:T(1,128)} %get-tuple-element.25) | copy-start | bytes 9220
  280.0 5.7 %copy-start.2 = (bf16[256,768]{1,0:T(8,128)(2,1)S(1)}, bf16[256,768]{1,0:T(8,128)(2,1)}, u32[]{:S(2)}) copy-start(bf16[256,768]{1,0:T(8,128)(2,1)} %get-tuple-element.66) | copy-start | bytes 1179652
  280.0 6.5 %copy-start = (f32[256,768]{1,0:T(8,128)S(1)}, f32[256,768]{1,0:T(8,128)}, u32[]{:S(2)}) copy-start(f32[256,768]{1,0:T(8,128)} %get-tuple-element.67) | copy-start | bytes 2359300
